TPU v7x, 128 devices: a whole 4x4x4 slice. The times are simulated.
128 devices in a mesh: blk: 32 (over y, x, core), tok: 4 (over z).
Axes of the slice: x: 4, y: 4, z: 4, core: 2. Of those that a mesh axis runs over, the one named last changes fastest.
Arguments:
- tokens: bfloat16 [4096, 8192], P('tok', 'blk'), may hold values from -6 to 6
- w_first: bfloat16 [64, 128, 128], P('blk'), may hold values from -0.5 to 0.5
- w_second: bfloat16 [64, 8, 128, 128], P('blk'), may hold values from -0.1875 to 0.1875
- tile_src: int32 [64, 8], replicated, may hold values from 0 to 63, as said below
- tile_live: int32 [64, 8], replicated, may hold values 0 or 1
- grad_out: bfloat16 [4096, 8192], P('tok', 'blk'), may hold values from -6 to 6
Outputs:
- layer_out: bfloat16 [4096, 8192], P('tok', 'blk')
- grad_tokens: bfloat16 [4096, 8192], P('tok', 'blk')
- grad_first: float32 [64, 128, 128], P('blk', 'tok')
- grad_second: float32 [64, 8, 128, 128], P('blk', None, 'tok')
Inputs may be any that keep to these rules, and one draw needn't show every extreme that they name: `tile_src`: for each d, the 16 entries of rows 2 * d to 2 * d + 1 name distinct blocks, and at most 1 of them lie in any one range of blocks 2 * s to 2 * s + 1; some range holds exactly 1 of them.
All inputs are finite; a program needn't handle non-finite values.
Results may differ from a plain program's by a relative error of at most 0.0049.
Values may be sent and summed in bfloat16 or wider, within the bound.
No kernel may reach another device: no remote copies, remote signals or barrier semaphores. Data moves between devices by JAX's collectives and lax.ppermute only.
A program may use at most 192 MiB of HBM per device.

v0:
```python
import jax
import jax.numpy as jnp
from jax import lax
from jax.sharding import PartitionSpec as P


def shards(tokens, w_first, w_second, tile_src, tile_live, grad_out):
    tok_rows = tokens.shape[0]
    per_dev = w_first.shape[0]
    tile_width = w_first.shape[1]
    slot_count = w_second.shape[1]
    my_index = lax.axis_index("blk")
    need_count = per_dev * slot_count
    tok_blocks = tokens.reshape(tok_rows, per_dev, tile_width)
    pre_act = jnp.einsum("tnc,ncd->tnd", tok_blocks, w_first, preferred_element_type=jnp.float32)
    activated = jax.nn.gelu(pre_act).astype(jnp.bfloat16)
    my_src = lax.dynamic_slice_in_dim(tile_src, my_index * per_dev, per_dev, 0).reshape(need_count)
    my_live = lax.dynamic_slice_in_dim(tile_live, my_index * per_dev, per_dev, 0)
    w_live = w_second * my_live[:, :, None, None].astype(jnp.bfloat16)
    grad_blocks = grad_out.reshape(tok_rows, per_dev, tile_width)
    contribution = jnp.einsum(
        "tid,ikbd->tikb", grad_blocks, w_live, preferred_element_type=jnp.float32
    )
    contribution = contribution.reshape(tok_rows, need_count, tile_width)
    piece_rows = lax.all_gather(
        activated.reshape(tok_rows, per_dev * tile_width), "blk", axis=1, tiled=True
    )
    block_count = piece_rows.shape[1] // tile_width
    piece_blocks = piece_rows.reshape(tok_rows, block_count, tile_width)
    one_hot = (my_src[:, None] == jnp.arange(block_count, dtype=jnp.int32)[None, :]).astype(
        jnp.bfloat16
    )
    picked = jnp.einsum("qn,tnb->tqb", one_hot, piece_blocks, preferred_element_type=jnp.float32)
    gathered = picked.astype(jnp.bfloat16)
    one_hot = (
        my_src[:, None] == jnp.arange(lax.axis_size("blk") * per_dev, dtype=jnp.int32)[None, :]
    ).astype(jnp.float32)
    summed = lax.psum_scatter(
        jnp.einsum("qj,tqb->jtb", one_hot, contribution, precision=lax.Precision.HIGHEST),
        "blk",
        scatter_dimension=0,
        tiled=True,
    )
    grad_act = summed.transpose(1, 0, 2)
    gathered_tiles = gathered.reshape(tok_rows, per_dev, slot_count, tile_width)
    layer_out = jnp.einsum(
        "tikb,ikbd->tid", gathered_tiles, w_live, preferred_element_type=jnp.float32
    )
    layer_out = layer_out.astype(jnp.bfloat16).reshape(tok_rows, per_dev * tile_width)
    _, gelu_pull = jax.vjp(jax.nn.gelu, pre_act)
    grad_pre = gelu_pull(grad_act)[0].astype(jnp.bfloat16)
    grad_tokens = jnp.einsum("tnd,ncd->tnc", grad_pre, w_first, preferred_element_type=jnp.float32)
    grad_tokens = grad_tokens.astype(jnp.bfloat16).reshape(tok_rows, per_dev * tile_width)
    first_part = jnp.einsum(
        "tnc,tnd->ncd", tok_blocks, grad_pre, preferred_element_type=jnp.float32
    )
    second_part = jnp.einsum(
        "tikb,tid->ikbd", gathered_tiles, grad_blocks, preferred_element_type=jnp.float32
    )
    second_part = second_part * my_live[:, :, None, None].astype(jnp.float32)
    grad_first, grad_second = (
        lax.psum_scatter(first_part, "tok", scatter_dimension=1, tiled=True),
        lax.psum_scatter(second_part, "tok", scatter_dimension=2, tiled=True),
    )
    return (layer_out, grad_tokens, grad_first, grad_second)


def solution(mesh):
    in_specs = (
        P("tok", "blk"),
        P("blk", None, None),
        P("blk", None, None, None),
        P(),
        P(),
        P("tok", "blk"),
    )
    out_specs = (
        P("tok", "blk"),
        P("tok", "blk"),
        P("blk", "tok", None),
        P("blk", None, "tok", None),
    )
    return jax.shard_map(shards, mesh=mesh, in_specs=in_specs, out_specs=out_specs, check_vma=False)
```

profile of v0, /device:TPU:0, one launch (start us, length us, event | category | flops | bytes accessed | tf_op | source)
XLA Modules:
  0.0 397.9 jit_solution(9182644835780785748)
XLA Ops:
  7.2 0.8 dynamic-slice_convert_fusion
  8.3 1.2 reshape.42
  9.5 5.6 %fusion.16 = f32[2,8,128,1024]{3,2,1,0:T(8,128)} fusion(bf16[1024,2,128,1]{2,1,0,3:T(2,128)(2,1)S(1)} %bitcast.68, bf16[2,8,128,128]{3,2,1,0:T(8,128)(2,1)} %param.8, bf16[2,8]{1,0:T(2,128)(2,1)S(1)} %copy.28), kind=kOutput, calls=%fused_computation.27 | convolution fusion | flops 537133056 | bytes 9437216 | tf_op jit(solution)/shard_map/tid,ikbd->tikb/dot_general | solution.py:21
  15.1 9.2 %copy.36 = f32[1024,16,128]{2,1,0:T(8,128)} copy(f32[1024,16,128]{0,2,1:T(8,128)} %bitcast.66) | data formatting | bytes 16777216 | tf_op jit(solution)/shard_map/reshape | solution.py:24
  24.2 21.5 %fusion.23 = f32[64,1024,128]{2,0,1:T(8,128)} fusion(f32[1024,16,128]{2,1,0:T(8,128)} %copy.36, s32[16]{0:T(128)S(1)} %eq.8), kind=kOutput, calls=%fused_computation.35 | convolution fusion | flops 1610613760 | bytes 41943104 | tf_op jit(solution)/shard_map/qj,tqb->jtb/dot_general | solution.py:39
  45.7 32.2 %copy.37 = f32[64,1024,128]{1,2,0:T(8,128)} copy(f32[64,1024,128]{2,0,1:T(8,128)} %fusion.23) | data formatting | bytes 67108864 | tf_op jit(solution)/shard_map/qj,tqb->jtb/dot_general | solution.py:39
  78.0 167.3 %reduce-scatter.3.cloned.1.call-done = f32[2,1024,128]{1,2,0:T(8,128)} async-done(((f32[64,1024,128]{1,2,0:T(8,128)}), f32[2,1024,128]{1,2,0:T(8,128)}) %reduce-scatter.3.cloned.1.call-update) | async-done | bytes 1048592 | tf_op jit(solution)/shard_map/reduce_scatter | solution.py:38
  245.4 3.0 fusion.7
  248.5 0.3 convolution_bitcast_fusion.2
  248.8 0.8 copy.40
  249.6 0.2 reduce-scatter.5.cloned.1.call-start
  249.8 70.7 %all-gather.2.cloned.1.call-done = bf16[1024,8192]{0,1:T(8,128)(2,1)} async-done(((bf16[1024,256]{0,1:T(8,128)(2,1)}), bf16[1024,8192]{0,1:T(8,128)(2,1)}) %all-gather.2.cloned.1.call-update) | async-done | bytes 16777232 | tf_op jit(solution)/shard_map/all_gather | solution.py:25
  320.5 22.7 %copy.53 = bf16[1024,64,128]{2,1,0:T(8,128)(2,1)} copy(bf16[1024,64,128]{0,2,1:T(8,128)(2,1)} %bitcast.67) | data formatting | bytes 33554432 | tf_op jit(solution)/shard_map/reshape | solution.py:29
  343.2 10.1 %convert_bitcast_fusion = bf16[1024,2,8,128]{3,2,1,0:T(8,128)(2,1)} fusion(bf16[1024,64,128]{2,1,0:T(8,128)(2,1)} %copy.53, s32[16]{0:T(128)S(1)} %eq.8), kind=kOutput, calls=%fused_computation | convolution fusion | flops 270533632 | bytes 20971584 | tf_op jit(solution)/shard_map/qn,tnb->tqb/dot_general | solution.py:33
  353.3 6.8 %copy.41 = bf16[1024,2,8,128]{0,3,2,1:T(8,128)(2,1)} copy(bf16[1024,2,8,128]{3,2,1,0:T(8,128)(2,1)} %convert_bitcast_fusion) | data formatting | bytes 8388608 | tf_op jit(solution)/shard_map/reshape | solution.py:45
  360.1 4.4 %convolution_multiply_fusion = f32[2,8,128,128]{3,2,1,0:T(8,128)} fusion(bf16[1024,2,8,128]{0,3,2,1:T(8,128)(2,1)} %copy.41, f32[2,8]{1,0:T(2,128)S(1)} %copy.43, bf16[1024,2,128,1]{2,1,0,3:T(2,128)(2,1)S(1)} %bitcast.69), kind=kOutput, calls=%fused_computation.4 | convolution fusion | flops 537133056 | bytes 5767232 | tf_op jit(solution)/shard_map/tikb,tid->ikbd/dot_general | solution.py:57
  364.6 0.6 dynamic-slice
  365.8 0.3 convolution_convert_fusion
  366.1 1.0 copy.45
  367.1 0.8 constant_dynamic-slice_fusion
  367.8 0.6 copy.46
  368.5 3.0 fusion
  371.5 1.0 copy.44
  372.5 18.9 %reduce-scatter.5.cloned.1.call-done = f32[2,8,32,128]{3,2,1,0:T(8,128)} async-done(((f32[2,8,128,128]{3,2,1,0:T(8,128)}), f32[2,8,32,128]{3,2,1,0:T(8,128)}) %reduce-scatter.5.cloned.1.call-update) | async-done | bytes 262160 | tf_op jit(solution)/shard_map/reduce_scatter | solution.py:63
  (20 shorter events, 0.6 us)
Async XLA Ops:
  7.2 238.2 %copy-start = (bf16[1024,256]{1,0:T(8,128)(2,1)S(1)}, bf16[1024,256]{1,0:T(8,128)(2,1)}, u32[]{:S(2)}) copy-start(bf16[1024,256]{1,0:T(8,128)(2,1)} %param.6) | copy-start | bytes 1572868
  7.2 238.2 %reduce-scatter.3.cloned.1.call-start = ((), (), s32[]{:S(2)}) async-start(), calls=%async_computation.3 | async-start | bytes 34603008 | tf_op jit(solution)/shard_map/reduce_scatter | solution.py:38
  77.9 167.4 %copy-start.2 = (bf16[2,128,128]{2,1,0:T(8,128)(2,1)S(1)}, bf16[2,128,128]{2,1,0:T(8,128)(2,1)}, u32[]{:S(2)}) copy-start(bf16[2,128,128]{2,1,0:T(8,128)(2,1)} %param.7) | copy-start | bytes 196612
  78.0 242.5 %all-gather.2.cloned.1.call-start = ((), (), s32[]{:S(2)}) async-start(), calls=%async_computation.2 | async-start | bytes 17301504 | tf_op jit(solution)/shard_map/all_gather | solution.py:25
  248.4 118.7 %all-reduce.3.cloned.1.call-start = ((), (), s32[]{:S(2)}) async-start(), calls=%async_computation.5 | async-start | bytes 262144
  249.6 141.8 %reduce-scatter.5.cloned.1.call-start = ((), (), s32[]{:S(2)}) async-start(), calls=%async_computation.4 | async-start | bytes 1310720 | tf_op jit(solution)/shard_map/reduce_scatter | solution.py:63
  353.3 11.2 %copy-start.3 = (u32[128]{0:T(128)S(1)}, u32[128]{0:T(128)}, u32[]{:S(2)}) copy-start(u32[128]{0:T(128)} %constant.28) | copy-start | bytes 1540
  353.3 15.1 %copy-start.1 = (bf16[2,8,128,128]{3,2,1,0:T(8,128)(2,1)S(1)}, bf16[2,8,128,128]{3,2,1,0:T(8,128)(2,1)}, u32[]{:S(2)}) copy-start(bf16[2,8,128,128]{3,2,1,0:T(8,128)(2,1)} %param.8) | copy-start | bytes 1572868
Sparse Core Ops, SparseCore 0:
  78.1 167.2 reduce-scatter.2
  248.5 71.9 all-gather.1
  323.5 40.9 all-reduce.2
  367.4 23.9 reduce-scatter.4
where the time goes:
time: 400 us; the launch traced here: 398 us
  waiting for transfers between devices  257 us (64%)
  local copies, waits for them, and re-layouts  77.1 us (19%)
  matrix products  48.2 us (12%)
  between operations  14.5 us (4%)
    reduce_scatter x1, waiting for transfers between devices, shards(): lax.psum_scatter(jnp.einsum('qj,tqb->jtb', one_hot, contribution, precisi...  167 us
    all_gather x1, waiting for transfers between devices, shards(): lax.all_gather(activated.reshape(tok_rows, per_dev * tile_width), 'blk',...  70.7 us
    dot_general x1, local copies, waits for them, and re-layouts, shards(): jnp.einsum('qj,tqb->jtb', one_hot, contribution, precision=lax.Precision....  32.2 us
    reshape x1, local copies, waits for them, and re-layouts, shards(): piece_blocks = piece_rows.reshape(tok_rows, block_count, tile_width)  22.7 us
    dot_general x1, matrix products, shards(): jnp.einsum('qj,tqb->jtb', one_hot, contribution, precision=lax.Precision....  21.5 us
    reduce_scatter x1, waiting for transfers between devices, shards(): lax.psum_scatter(second_part, 'tok', scatter_dimension=2, tiled=True)  18.9 us
    dot_general x1, matrix products, shards(): jnp.einsum('qn,tnb->tqb', one_hot, piece_blocks, preferred_element_type=j...  10.1 us
    reshape x1, local copies, waits for them, and re-layouts, shards(): contribution = contribution.reshape(tok_rows, need_count, tile_width)  9.18 us
  transfers between devices with their start and end apart: 4, of which 3 were waited for; matrix products, arithmetic and copies ran while one was open for 13% of the time, Pallas kernels for 0%

commit v1 on v0

v1 whole, which is shorter than its diff:
```python
import functools

import jax
import jax.numpy as jnp
from jax import lax
from jax.experimental import pallas as pl
from jax.experimental.pallas import tpu as pltpu
from jax.sharding import PartitionSpec as P

NY, NX, NC, NZ = 4, 4, 2, 4
BF, F32 = jnp.bfloat16, jnp.float32
ROOT = 0.7978845608028654
CUBE = 0.044715
VMEM = pl.BlockSpec(memory_space=pltpu.VMEM)
SMEM = pl.BlockSpec(memory_space=pltpu.SMEM)
ANY = pl.BlockSpec(memory_space=pl.ANY)


def along(dy, dx, dc):
    pairs = []
    for y in range(NY):
        for x in range(NX):
            for c in range(NC):
                to = (((y + dy) % NY) * NX + (x + dx) % NX) * NC + (c + dc) % NC
                pairs.append(((y * NX + x) * NC + c, to))
    return pairs


def shift_y(value, step):
    return lax.ppermute(value, "blk", along(step, 0, 0))


def shift_x(value, step):
    return lax.ppermute(value, "blk", along(0, step, 0))


def swap_core(value):
    return lax.ppermute(value, "blk", along(0, 0, 1))


def shift_z(value, step):
    return lax.ppermute(value, "tok", [(z, (z + step) % NZ) for z in range(NZ)])


def dot(a, b, ca, cb):
    return lax.dot_general(a, b, (((ca,), (cb,)), ((), ())), preferred_element_type=F32)


def call(body, outs, in_specs, out_specs, flops, nbytes, scratch=()):
    return pl.pallas_call(
        body,
        out_shape=outs,
        in_specs=in_specs,
        out_specs=out_specs,
        scratch_shapes=list(scratch),
        compiler_params=pltpu.CompilerParams(vmem_limit_bytes=48 * 1024 * 1024),
        cost_estimate=pl.CostEstimate(flops=flops, bytes_accessed=nbytes, transcendentals=0),
    )


def sds(shape, dtype):
    return jax.ShapeDtypeStruct(shape, dtype)


def first_body(pos, tok, go, wf, a0, a1, a2, a3, g0, g1, g2, g3, slope):
    x = pos[1]
    for s, (a, g) in enumerate(((a0, g0), (a1, g1), (a2, g2), (a3, g3))):
        rows = pl.ds(pl.multiple_of(((x + s) & 3) * 256, 256), 256)
        g[...] = go[rows, :]
        for p in range(2):
            pre = dot(tok[rows, p * 128 : (p + 1) * 128], wf[p], 1, 0)
            sq = pre * pre
            th = jnp.tanh(ROOT * pre * (1.0 + CUBE * sq))
            a[p] = (0.5 * pre * (1.0 + th)).astype(BF)
            slope[s, p] = 0.5 * (1.0 + th) + 0.5 * pre * (1.0 - th * th) * (
                ROOT * (1.0 + 3.0 * CUBE * sq)
            )


def load_weights(pos, w_own, wq, buf, sems, base):
    z = pos[3]
    copies = [pltpu.make_async_copy(w_own, buf.at[0], sems.at[base])]
    for t, part in enumerate(wq):
        k0 = ((z - t) & 3) * 2
        for s in range(1, 4):
            copies.append(
                pltpu.make_async_copy(
                    part.at[s - 1], buf.at[s, :, pl.ds(k0, 2)], sems.at[base + 3 * t + s]
                )
            )
    return copies


def back_body(pos, src, live, w_own, q0, q1, q2, q3, g0, g1, g2, g3, s0, s1, s2, s3, own, wbuf, acc, sems):
    y, x, c = pos[0], pos[1], pos[2]
    copies = load_weights(pos, w_own, (q0, q1, q2, q3), wbuf, sems, 0)
    for copy in copies:
        copy.start()
    acc[...] = jnp.zeros_like(acc)
    for copy in copies:
        copy.wait()
    for s, g in enumerate((g0, g1, g2, g3)):
        for p in range(2):
            block = ((y * 4 + ((x - s) & 3)) * 2 + c) * 2 + p
            grad = g[:, p * 128 : (p + 1) * 128]
            for k in range(8):
                j = src[block, k]
                scale = live[block, k].astype(F32)
                r = j >> 1
                flat = (((r & 1) ^ c) * 16 + (((r >> 3) - y) & 3) * 4 + (((r >> 1) - x) & 3)) * 2 + (j & 1)
                acc[flat] += dot(grad, wbuf[s, p, k], 1, 1) * scale
    for s, out in enumerate((s0, s1, s2, s3)):
        out[...] = acc[32 + 8 * s : 40 + 8 * s].astype(BF)
    own[...] = acc[0:32]


def fore_body(pos, src, live, w_own, q0, q1, q2, q3, a0, a1, a2, a3, b0, b1, b2, b3, g0, g1, g2, g3,
              l0, l1, l2, l3, z0, z1, z2, z3, wbuf, abuf, cat, grads, sems):
    y, x, c, z = pos[0], pos[1], pos[2], pos[3]
    copies = load_weights(pos, w_own, (q0, q1, q2, q3), wbuf, sems, 0)
    for n, part in enumerate((a0, a1, a2, a3, b0, b1, b2, b3)):
        copies.append(pltpu.make_async_copy(part, abuf.at[n], sems.at[13 + n]))
    for copy in copies:
        copy.start()
    for copy in copies:
        copy.wait()
    for s, (g, out) in enumerate(((g0, l0), (g1, l1), (g2, l2), (g3, l3))):
        for p in range(2):
            n = s * 2 + p
            block = ((y * 4 + ((x - s) & 3)) * 2 + c) * 2 + p
            grad = g[:, p * 128 : (p + 1) * 128]
            for k in range(8):
                j = src[block, k]
                scale = live[block, k].astype(F32).astype(BF)
                r = j >> 1
                which = ((r & 1) ^ c) * 4 + ((y - (r >> 3)) & 3)
                cat[p, :, k * 128 : (k + 1) * 128] = abuf[which, (x - (r >> 1)) & 3, j & 1] * scale
            weights = wbuf[s, p].reshape(1024, 128)
            out[:, p * 128 : (p + 1) * 128] = dot(cat[p], weights, 1, 0).astype(BF)
            grads[...] = dot(cat[p], grad, 0, 0).reshape(8, 128, 128)
            z0[n] = grads[:, pl.ds(pl.multiple_of(z * 32, 32), 32), :]
            for t, to in ((1, z1), (2, z2), (3, z3)):
                rows = pl.ds(pl.multiple_of(((z + t) & 3) * 32, 32), 32)
                to[n] = grads[:, rows, :].astype(BF)


def last_body(pos, tok, wf, slope, h0, h1, h2, h3, gt, f0, f1, f2, f3, total):
    x, z = pos[1], pos[3]
    for s, h in enumerate((h0, h1, h2, h3)):
        rows = pl.ds(pl.multiple_of(((x - s) & 3) * 256, 256), 256)
        for p in range(2):
            cols = slice(p * 128, (p + 1) * 128)
            grad_pre = (h[p].astype(F32) * slope[(4 - s) % 4, p]).astype(BF)
            gt[rows, cols] = dot(grad_pre, wf[p], 1, 1).astype(BF)
            part = dot(tok[rows, cols], grad_pre, 0, 0)
            if s == 0:
                total[p] = part
            else:
                total[p] += part
    for t, out in enumerate((f0, f1, f2, f3)):
        out[...] = total[:, pl.ds(pl.multiple_of(((z + t) & 3) * 32, 32), 32), :]


def join_body(pos, p0, p1, p2, p3, out):
    x = pos[1]
    for s, part in enumerate((p0, p1, p2, p3)):
        out[pl.ds(pl.multiple_of(((x + s) & 3) * 256, 256), 256), :] = part[...]


def shards(tokens, w_first, w_second, tile_src, tile_live, grad_out):
    me, z = lax.axis_index("blk"), lax.axis_index("tok")
    pos = jnp.stack([me // 8, (me // 2) % 4, me % 2, z]).astype(jnp.int32)

    quarter = lax.dynamic_slice_in_dim(w_second, z * 2, 2, 1)
    q0 = jnp.stack([shift_x(quarter, s) for s in (1, 2, 3)])
    quarters = [q0] + [shift_z(q0, t) for t in (1, 2, 3)]

    chunk = sds((256, 256), BF)
    outs = call(
        first_body,
        [sds((2, 256, 128), BF)] * 4 + [chunk] * 4 + [sds((4, 2, 256, 128), F32)],
        [SMEM] + [VMEM] * 3,
        [VMEM] * 9,
        67_000_000 * 2,
        3_500_000,
    )(pos, tokens, grad_out, w_first)
    acts, grads, slope = outs[:4], outs[4:8], outs[8]
    act_row = jnp.stack([acts[0]] + [shift_x(acts[s], s) for s in (1, 2, 3)])
    grads = [grads[0]] + [shift_x(grads[s], s) for s in (1, 2, 3)]

    mine = [act_row] + [shift_y(act_row, s) for s in (1, 2, 3)]
    other = [swap_core(part) for part in mine]

    wscratch = pltpu.VMEM((4, 2, 8, 128, 128), BF)
    piece = sds((8, 256, 128), BF)
    outs = call(
        back_body,
        [piece] * 4 + [sds((32, 256, 128), F32)],
        [SMEM] * 3 + [ANY] * 5 + [VMEM] * 4,
        [VMEM] * 5,
        540_000_000 * 2,
        9_000_000,
        [wscratch, pltpu.VMEM((64, 256, 128), F32), pltpu.SemaphoreType.DMA((13,))],
    )(pos, tile_src, tile_live, w_second, *quarters, *grads)
    swapped = [swap_core(outs[s]) for s in (1, 2, 3, 0)]
    own = outs[4]
    sums = [own[8 * s : 8 * s + 8] + swapped[(s - 1) % 4].astype(F32) for s in range(4)]
    total = sums[0]
    for part in [shift_y(sums[s].astype(BF), s) for s in (1, 2, 3)]:
        total = total + part.astype(F32)
    pieces = [total[0:2]] + [
        shift_x(total[2 * s : 2 * s + 2].astype(BF), s) for s in (1, 2, 3)
    ]

    slab = (8, 8, 32, 128)
    outs = call(
        fore_body,
        [chunk] * 4 + [sds(slab, F32)] + [sds(slab, BF)] * 3,
        [SMEM] * 3 + [ANY] * 13 + [VMEM] * 4,
        [VMEM] * 8,
        2 * 540_000_000 * 2,
        12_000_000,
        [
            wscratch,
            pltpu.VMEM((8, 4, 2, 256, 128), BF),
            pltpu.VMEM((2, 256, 1024), BF),
            pltpu.VMEM((8, 128, 128), F32),
            pltpu.SemaphoreType.DMA((21,)),
        ],
    )(pos, tile_src, tile_live, w_second, *quarters, *mine, *other, *grads)
    rows = [outs[0]] + [shift_x(outs[s], -s) for s in (1, 2, 3)]
    layer_out = call(
        join_body, sds((1024, 256), BF), [SMEM] + [VMEM] * 4, VMEM, 0, 1_000_000
    )(pos, *rows)
    summed = outs[4]
    for part in [shift_z(outs[4 + t], t) for t in (1, 2, 3)]:
        summed = summed + part.astype(F32)
    grad_second = summed[0:2]
    for part in [shift_x(summed[2 * s : 2 * s + 2].astype(BF), -s) for s in (1, 2, 3)]:
        grad_second = grad_second + part.astype(F32)

    strip = sds((2, 32, 128), F32)
    outs = call(
        last_body,
        [sds((1024, 256), BF)] + [strip] * 4,
        [SMEM] + [VMEM] * 7,
        [VMEM] * 5,
        2 * 67_000_000 * 2,
        3_500_000,
        [pltpu.VMEM((2, 128, 128), F32)],
    )(pos, tokens, w_first, slope, *pieces)
    grad_tokens = outs[0]
    grad_first = outs[1]
    for part in [shift_z(outs[1 + t], t) for t in (1, 2, 3)]:
        grad_first = grad_first + part
    return (layer_out, grad_tokens, grad_first, grad_second)


def solution(mesh):
    in_specs = (
        P("tok", "blk"),
        P("blk", None, None),
        P("blk", None, None, None),
        P(),
        P(),
        P("tok", "blk"),
    )
    out_specs = (
        P("tok", "blk"),
        P("tok", "blk"),
        P("blk", "tok", None),
        P("blk", None, "tok", None),
    )
    return jax.shard_map(shards, mesh=mesh, in_specs=in_specs, out_specs=out_specs, check_vma=False)
```

time: 400 us -> 128 us (0.32)
  waiting for transfers between devices: 257 us -> 44.2 us
  local copies, waits for them, and re-layouts: 77.1 us -> 9.65 us
  matrix products: 48.2 us -> 0 us
  starting transfers between devices: 0.34 us -> 45.9 us
  Pallas kernels: 0 us -> 21.1 us
  between operations: 14.5 us -> 0.88 us
  other arithmetic: 0.83 us -> 5.8 us
    reduce_scatter x2 -> x0, waiting for transfers between devices: 186 us -> none  [the longest x1 167 us: shards(): lax.psum_scatter(jnp.einsum('qj,tqb->jtb', one_hot, contribution, precisi...]
    all_gather x1 -> x0, waiting for transfers between devices: 70.7 us -> none  [shards(): lax.all_gather(activated.reshape(tok_rows, per_dev * tile_width), 'blk',...]
    dot_general x8 -> x0, matrix products: 48.2 us -> none  [the longest x1 21.5 us: shards(): jnp.einsum('qj,tqb->jtb', one_hot, contribution, precision=lax.Precision....]
    ppermute x0 -> x41, starting transfers between devices: none -> 45.9 us  [the longest x18 20.7 us: shift_x(): return lax.ppermute(value, 'blk', along(0, step, 0))]
    ppermute x0 -> x41, waiting for transfers between devices: none -> 44.2 us  [the longest x6 22.2 us: shift_y(): return lax.ppermute(value, 'blk', along(step, 0, 0))]
    reshape x4 -> x0, local copies, waits for them, and re-layouts: 39.8 us -> none  [the longest x1 22.7 us: shards(): piece_blocks = piece_rows.reshape(tok_rows, block_count, tile_width)]
    dot_general x2 -> x0, local copies, waits for them, and re-layouts: 33 us -> none  [the longest x1 32.2 us: shards(): jnp.einsum('qj,tqb->jtb', one_hot, contribution, precision=lax.Precision....]
    pallas_call x0 -> x5, Pallas kernels: none -> 21.1 us  [the longest x1 8.84 us: shards(): call(fore_body, [chunk] * 4 + [sds(slab, F32)] + [sds(slab, BF)] * 3, [SM...]
  transfers between devices with their start and end apart: 4 -> 41, of which waited for: 3 -> 13; matrix products, arithmetic and copies ran while one was open for 13% -> 5% of each run, Pallas kernels for 0% -> 17%
where the time goes in v1:
time: 128 us
  starting transfers between devices  45.9 us (36%)
  waiting for transfers between devices  44.2 us (35%)
  Pallas kernels  21.1 us (16%)
  local copies, waits for them, and re-layouts  9.65 us (8%)
  other arithmetic  5.8 us (5%)
    ppermute x6, waiting for transfers between devices, shift_y(): return lax.ppermute(value, 'blk', along(step, 0, 0))  22.2 us
    ppermute x18, waiting for transfers between devices, shift_x(): return lax.ppermute(value, 'blk', along(0, step, 0))  21.2 us
    ppermute x18, starting transfers between devices, shift_x(): return lax.ppermute(value, 'blk', along(0, step, 0))  20.7 us
    ppermute x9, starting transfers between devices, shift_z(): return lax.ppermute(value, 'tok', [(z, (z + step) % NZ) for z in range(NZ)])  14.8 us
    pallas_call x1, Pallas kernels, shards(): call(fore_body, [chunk] * 4 + [sds(slab, F32)] + [sds(slab, BF)] * 3, [SM...  8.84 us
    ppermute x6, starting transfers between devices, shift_y(): return lax.ppermute(value, 'blk', along(step, 0, 0))  8.81 us
    unnamed x30, local copies, waits for them, and re-layouts  8.65 us
    pallas_call x1, Pallas kernels, shards(): call(back_body, [piece] * 4 + [sds((32, 256, 128), F32)], [SMEM] * 3 + [A...  7.16 us
  transfers between devices with their start and end apart: 41, of which 13 were waited for; matrix products, arithmetic and copies ran while one was open for 5% of the time, Pallas kernels for 17%

profile of v1, /device:TPU:0, one launch (start us, length us, event | category | flops | bytes accessed | tf_op | source)
XLA Modules:
  0.0 127.5 jit_solution(1723547829623377426)
XLA Ops:
  1.6 2.9 %collective-permute-start.2 = (bf16[2,2,128,128]{3,2,1,0:T(8,128)(2,1)S(1)}, bf16[2,2,128,128]{3,2,1,0:T(8,128)(2,1)S(1)}, u32[]{:S(2)}, u32[]{:S(2)}) collective-permute-start(bf16[2,2,128,128]{3,2,1,0:T(8,128)(2,1)S(1)} %constant_dynamic-slice_fusion), channel_id=1, source_target_pairs={{0,24},{4,28},{8,0},{12,4},{16,8},{20,12},{24,16},{28,20},{32,56},... | collective-permute-start | bytes 393224 | tf_op jit(solution)/shard_map/ppermute | solution.py:34
  9.2 1.9 %shard_map.93 = (bf16[2,256,128]{2,1,0:T(8,128)(2,1)S(1)}, bf16[2,256,128]{2,1,0:T(8,128)(2,1)S(1)}, bf16[2,256,128]{2,1,0:T(8,128)(2,1)S(1)}, bf16[2,256,128]{2...) custom-call(s32[4]{0:T(128)S(1)} %pad_add_fusion.pos, ...), custom_call_target="tpu_custom_call" | custom-call | flops 134000000 | bytes 3500000 | tf_op jit(solution)/shard_map/pallas_call | solution.py:179
  11.1 1.8 %collective-permute-start.6 = (bf16[2,256,128]{2,1,0:T(8,128)(2,1)S(1)}, bf16[2,256,128]{2,1,0:T(8,128)(2,1)S(1)}, u32[]{:S(2)}, u32[]{:S(2)}) collective-permute-start(bf16[2,256,128]{2,1,0:T(8,128)(2,1)S(1)} %get-tuple-element.32), channel_id=1, source_target_pairs={{0,8},{4,12},{8,16},{12,20},{16,24},{20,28},{24,0},{28,4},{32,40},... | collective-permute-start | bytes 393224 | tf_op jit(solution)/shard_map/ppermute | solution.py:34
  12.9 2.0 %collective-permute-start.7 = (bf16[2,256,128]{2,1,0:T(8,128)(2,1)S(1)}, bf16[2,256,128]{2,1,0:T(8,128)(2,1)S(1)}, u32[]{:S(2)}, u32[]{:S(2)}) collective-permute-start(bf16[2,256,128]{2,1,0:T(8,128)(2,1)S(1)} %get-tuple-element.33), channel_id=1, source_target_pairs={{0,16},{4,20},{8,24},{12,28},{16,0},{20,4},{24,8},{28,12},{32,48},... | collective-permute-start | bytes 393224 | tf_op jit(solution)/shard_map/ppermute | solution.py:34
  15.6 4.1 %collective-permute-start.5 = (bf16[3,2,2,128,128]{4,3,2,1,0:T(8,128)(2,1)S(1)}, bf16[3,2,2,128,128]{4,3,2,1,0:T(8,128)(2,1)S(1)}, u32[]{:S(2)}, u32[]{:S(2)}) collective-permute-start(bf16[3,2,2,128,128]{4,3,2,1,0:T(8,128)(2,1)S(1)} %pad_maximum_fusion.1.q0), channel_id=1, source_target_pairs={{0,3},{1,0},{2,1},{3,2},{4,7},{5,4},{6,5},{7,6},{8,11},{9,8},{10,9... | collective-permute-start | bytes 1179656 | tf_op jit(solution)/shard_map/ppermute | solution.py:42
  24.0 3.2 %collective-permute-done.16.g1 = bf16[256,256]{1,0:T(8,128)(2,1)S(1)} collective-permute-done((bf16[256,256]{1,0:T(8,128)(2,1)S(1)}, bf16[256,256]{1,0:T(8,128)(2,1)S(1)}, u32[]{:S(2)}, u32[]{:S(2)}) %collective-permute-start.16) | collective-permute-done | bytes 131104 | tf_op jit(solution)/shard_map/ppermute | solution.py:34
  27.2 3.0 %collective-permute-start.11 = (bf16[4,2,256,128]{3,2,1,0:T(8,128)(2,1)S(1)}, bf16[4,2,256,128]{3,2,1,0:T(8,128)(2,1)}, u32[]{:S(2)}, u32[]{:S(2)}) collective-permute-start(bf16[4,2,256,128]{3,2,1,0:T(8,128)(2,1)S(1)} %pad_maximum_fusion.a0), channel_id=1, source_target_pairs={{0,96},{4,100},{8,104},{12,108},{16,112},{20,116},{24,120},{28,124... | collective-permute-start | bytes 1572872 | tf_op jit(solution)/shard_map/ppermute | solution.py:30
  32.9 3.2 %collective-permute-done.18.g3 = bf16[256,256]{1,0:T(8,128)(2,1)} collective-permute-done((bf16[256,256]{1,0:T(8,128)(2,1)}, bf16[256,256]{1,0:T(8,128)(2,1)}, u32[]{:S(2)}, u32[]{:S(2)}) %collective-permute-start.18) | collective-permute-done | bytes 131104 | tf_op jit(solution)/shard_map/ppermute | solution.py:34
  36.1 1.8 %collective-permute-start.10 = (bf16[4,2,256,128]{3,2,1,0:T(8,128)(2,1)S(1)}, bf16[4,2,256,128]{3,2,1,0:T(8,128)(2,1)S(1)}, u32[]{:S(2)}, u32[]{:S(2)}) collective-permute-start(bf16[4,2,256,128]{3,2,1,0:T(8,128)(2,1)S(1)} %pad_maximum_fusion.a0), channel_id=1, source_target_pairs={{0,64},{4,68},{8,72},{12,76},{16,80},{20,84},{24,88},{28,92},{32,9... | collective-permute-start | bytes 1572872 | tf_op jit(solution)/shard_map/ppermute | solution.py:30
  40.6 7.2 %shard_map.96 = (bf16[8,256,128]{2,1,0:T(8,128)(2,1)S(1)}, bf16[8,256,128]{2,1,0:T(8,128)(2,1)S(1)}, bf16[8,256,128]{2,1,0:T(8,128)(2,1)S(1)}, bf16[8,256,128]{2,1,0:T(8,128)(2,1)S(1)}, f32[32,256,128]{2,1,0:T(8,128)}) custom-call(s32[4]{0:T(128)S(1)} %pad_add_fusion.pos, s32[64,8]{1,0:T(8,128)S(1)} %copy.10.src, s32[64,8]{1,0:T(8,128)S(1)} %copy.11.live, ...), custom_call_target="tpu_custom_call" | custom-call | flops 1080000000 | bytes 9000000 | tf_op jit(solution)/shard_map/pallas_call | solution.py:196
  48.4 2.6 %collective-permute-done.11.a3 = bf16[4,2,256,128]{3,2,1,0:T(8,128)(2,1)} collective-permute-done((bf16[4,2,256,128]{3,2,1,0:T(8,128)(2,1)S(1)}, bf16[4,2,256,128]{3,2,1,0:T(8,128)(2,1)}, u32[]{:S(2)}, u32[]{:S(2)}) %collective-permute-start.11) | collective-permute-done | bytes 524320 | tf_op jit(solution)/shard_map/ppermute | solution.py:30
  52.5 7.2 %collective-permute-done.9.a1 = bf16[4,2,256,128]{3,2,1,0:T(8,128)(2,1)S(1)} collective-permute-done((bf16[4,2,256,128]{3,2,1,0:T(8,128)(2,1)S(1)}, bf16[4,2,256,128]{3,2,1,0:T(8,128)(2,1)S(1)}, u32[]{:S(2)}, u32[]{:S(2)}) %collective-permute-start.9) | collective-permute-done | bytes 524320 | tf_op jit(solution)/shard_map/ppermute | solution.py:30
  60.7 2.3 %add_convert_fusion.2 = (bf16[8,256,128]{2,1,0:T(8,128)(2,1)S(1)}, bf16[8,256,128]{2,1,0:T(8,128)(2,1)S(1)}, bf16[8,256,128]{2,1,0:T(8,128)(2,1)S(1)}) fusion(bf16[8,256,128]{2,1,0:T(8,128)(2,1)S(1)} %collective-permute-done.23, f32[32,256,128]{2,1,0:T(8,128)} %get-tuple-element.44, bf16[8,256,128]{2,1,0:T(8,128)(2,1)S(1)} %collective-permute-done.27, ...), kind=kLoop, calls=%fused_computation.4 | loop fusion | flops 2359296 | bytes 6291456 | tf_op jit(solution)/shard_map/convert_element_type | solution.py:209
  63.2 3.2 %collective-permute-start.28 = (bf16[8,256,128]{2,1,0:T(8,128)(2,1)S(1)}, bf16[8,256,128]{2,1,0:T(8,128)(2,1)S(1)}, u32[]{:S(2)}, u32[]{:S(2)}) collective-permute-start(bf16[8,256,128]{2,1,0:T(8,128)(2,1)S(1)} %get-tuple-element.63), channel_id=1, source_target_pairs={{0,96},{4,100},{8,104},{12,108},{16,112},{20,116},{24,120},{28,124... | collective-permute-start | bytes 1572872 | tf_op jit(solution)/shard_map/ppermute | solution.py:30
  68.0 8.8 %shard_map.94 = (bf16[256,256]{1,0:T(8,128)(2,1)S(1)}, bf16[256,256]{1,0:T(8,128)(2,1)S(1)}, bf16[256,256]{1,0:T(8,128)(2,1)S(1)}, bf16[256,256]{1,0:T(8,128)(2,...) custom-call(s32[4]{0:T(128)S(1)} %pad_add_fusion.pos, ...), custom_call_target="tpu_custom_call" | custom-call | flops 2160000000 | bytes 12000000 | tf_op jit(solution)/shard_map/pallas_call | solution.py:216
  78.6 10.9 %collective-permute-done.24 = bf16[8,256,128]{2,1,0:T(8,128)(2,1)S(1)} collective-permute-done((bf16[8,256,128]{2,1,0:T(8,128)(2,1)S(1)}, bf16[8,256,128]{2,1,0:T(8,128)(2,1)S(1)}, u32[]{:S(2)}, u32[]{:S(2)}) %collective-permute-start.24) | collective-permute-done | bytes 524320 | tf_op jit(solution)/shard_map/ppermute | solution.py:30
  89.5 1.9 %collective-permute-start.35 = (bf16[8,8,32,128]{3,2,1,0:T(8,128)(2,1)S(1)}, bf16[8,8,32,128]{3,2,1,0:T(8,128)(2,1)S(1)}, u32[]{:S(2)}, u32[]{:S(2)}) collective-permute-start(bf16[8,8,32,128]{3,2,1,0:T(8,128)(2,1)S(1)} %get-tuple-element.55), channel_id=1, source_target_pairs={{0,1},{1,2},{2,3},{3,0},{4,5},{5,6},{6,7},{7,4},{8,9},{9,10},{10,1... | collective-permute-start | bytes 1572872 | tf_op jit(solution)/shard_map/ppermute | solution.py:42
  91.4 2.8 %collective-permute-start.36 = (bf16[8,8,32,128]{3,2,1,0:T(8,128)(2,1)S(1)}, bf16[8,8,32,128]{3,2,1,0:T(8,128)(2,1)S(1)}, u32[]{:S(2)}, u32[]{:S(2)}) collective-permute-start(bf16[8,8,32,128]{3,2,1,0:T(8,128)(2,1)S(1)} %get-tuple-element.56), channel_id=1, source_target_pairs={{0,2},{1,3},{2,0},{3,1},{4,6},{5,7},{6,4},{7,5},{8,10},{9,11},{10,... | collective-permute-start | bytes 1572872 | tf_op jit(solution)/shard_map/ppermute | solution.py:42
  96.8 3.2 %collective-permute-start.31 = (bf16[2,256,128]{2,1,0:T(8,128)(2,1)S(1)}, bf16[2,256,128]{2,1,0:T(8,128)(2,1)S(1)}, u32[]{:S(2)}, u32[]{:S(2)}) collective-permute-start(bf16[2,256,128]{2,1,0:T(8,128)(2,1)S(1)} %get-tuple-element.68), channel_id=1, source_target_pairs={{0,24},{4,28},{8,0},{12,4},{16,8},{20,12},{24,16},{28,20},{32,56},... | collective-permute-start | bytes 393224 | tf_op jit(solution)/shard_map/ppermute | solution.py:34
  100.1 2.9 %collective-permute-done.21.p3 = bf16[256,256]{1,0:T(8,128)(2,1)S(1)} collective-permute-done((bf16[256,256]{1,0:T(8,128)(2,1)S(1)}, bf16[256,256]{1,0:T(8,128)(2,1)S(1)}, u32[]{:S(2)}, u32[]{:S(2)}) %collective-permute-start.21) | collective-permute-done | bytes 131104 | tf_op jit(solution)/shard_map/ppermute | solution.py:34
  105.3 4.2 %collective-permute-done.30.h2 = bf16[2,256,128]{2,1,0:T(8,128)(2,1)S(1)} collective-permute-done((bf16[2,256,128]{2,1,0:T(8,128)(2,1)S(1)}, bf16[2,256,128]{2,1,0:T(8,128)(2,1)S(1)}, u32[]{:S(2)}, u32[]{:S(2)}) %collective-permute-start.30) | collective-permute-done | bytes 131104 | tf_op jit(solution)/shard_map/ppermute | solution.py:34
  114.6 2.0 %collective-permute-start.34 = (f32[2,32,128]{2,1,0:T(8,128)S(1)}, f32[2,32,128]{2,1,0:T(8,128)S(1)}, u32[]{:S(2)}, u32[]{:S(2)}) collective-permute-start(f32[2,32,128]{2,1,0:T(8,128)S(1)} %get-tuple-element.53), channel_id=1, source_target_pairs={{0,3},{1,0},{2,1},{3,2},{4,7},{5,4},{6,5},{7,6},{8,11},{9,8},{10,9... | collective-permute-start | bytes 98312 | tf_op jit(solution)/shard_map/ppermute | solution.py:42
  121.3 2.6 %collective-permute-done.38 = bf16[2,8,32,128]{3,2,1,0:T(8,128)(2,1)S(1)} collective-permute-done((bf16[2,8,32,128]{3,2,1,0:T(8,128)(2,1)S(1)}, bf16[2,8,32,128]{3,2,1,0:T(8,128)(2,1)S(1)}, u32[]{:S(2)}, u32[]{:S(2)}) %collective-permute-start.38) | collective-permute-done | bytes 131104 | tf_op jit(solution)/shard_map/ppermute | solution.py:34
  123.9 2.8 %collective-permute-done.40 = bf16[2,8,32,128]{3,2,1,0:T(8,128)(2,1)S(1)} collective-permute-done((bf16[2,8,32,128]{3,2,1,0:T(8,128)(2,1)S(1)}, bf16[2,8,32,128]{3,2,1,0:T(8,128)(2,1)S(1)}, u32[]{:S(2)}, u32[]{:S(2)}) %collective-permute-start.40) | collective-permute-done | bytes 131104 | tf_op jit(solution)/shard_map/ppermute | solution.py:34
  (105 shorter events, 37.9 us)
Async XLA Ops:
  1.6 13.3 %collective-permute-start.2 = (bf16[2,2,128,128]{3,2,1,0:T(8,128)(2,1)S(1)}, bf16[2,2,128,128]{3,2,1,0:T(8,128)(2,1)S(1)}, u32[]{:S(2)}, u32[]{:S(2)}) collective-permute-start(bf16[2,2,128,128]{3,2,1,0:T(8,128)(2,1)S(1)} %constant_dynamic-slice_fusion), channel_id=1, source_target_pairs={{0,24},{4,28},{8,0},{12,4},{16,8},{20,12},{24,16},{28,20},{32,56},... | collective-permute-start | bytes 393224 | tf_op jit(solution)/shard_map/ppermute | solution.py:34
  4.5 11.1 %collective-permute-start.1 = (bf16[2,2,128,128]{3,2,1,0:T(8,128)(2,1)S(1)}, bf16[2,2,128,128]{3,2,1,0:T(8,128)(2,1)S(1)}, u32[]{:S(2)}, u32[]{:S(2)}) collective-permute-start(bf16[2,2,128,128]{3,2,1,0:T(8,128)(2,1)S(1)} %constant_dynamic-slice_fusion), channel_id=1, source_target_pairs={{0,16},{4,20},{8,24},{12,28},{16,0},{20,4},{24,8},{28,12},{32,48},... | collective-permute-start | bytes 393224 | tf_op jit(solution)/shard_map/ppermute | solution.py:34
  5.3 10.3 %collective-permute-start = (bf16[2,2,128,128]{3,2,1,0:T(8,128)(2,1)S(1)}, bf16[2,2,128,128]{3,2,1,0:T(8,128)(2,1)S(1)}, u32[]{:S(2)}, u32[]{:S(2)}) collective-permute-start(bf16[2,2,128,128]{3,2,1,0:T(8,128)(2,1)S(1)} %constant_dynamic-slice_fusion), channel_id=1, source_target_pairs={{0,8},{4,12},{8,16},{12,20},{16,24},{20,28},{24,0},{28,4},{32,40},... | collective-permute-start | bytes 393224 | tf_op jit(solution)/shard_map/ppermute | solution.py:34
  11.1 8.7 %collective-permute-start.6 = (bf16[2,256,128]{2,1,0:T(8,128)(2,1)S(1)}, bf16[2,256,128]{2,1,0:T(8,128)(2,1)S(1)}, u32[]{:S(2)}, u32[]{:S(2)}) collective-permute-start(bf16[2,256,128]{2,1,0:T(8,128)(2,1)S(1)} %get-tuple-element.32), channel_id=1, source_target_pairs={{0,8},{4,12},{8,16},{12,20},{16,24},{20,28},{24,0},{28,4},{32,40},... | collective-permute-start | bytes 393224 | tf_op jit(solution)/shard_map/ppermute | solution.py:34
  12.9 8.1 %collective-permute-start.7 = (bf16[2,256,128]{2,1,0:T(8,128)(2,1)S(1)}, bf16[2,256,128]{2,1,0:T(8,128)(2,1)S(1)}, u32[]{:S(2)}, u32[]{:S(2)}) collective-permute-start(bf16[2,256,128]{2,1,0:T(8,128)(2,1)S(1)} %get-tuple-element.33), channel_id=1, source_target_pairs={{0,16},{4,20},{8,24},{12,28},{16,0},{20,4},{24,8},{28,12},{32,48},... | collective-permute-start | bytes 393224 | tf_op jit(solution)/shard_map/ppermute | solution.py:34
  15.6 22.4 %collective-permute-start.5 = (bf16[3,2,2,128,128]{4,3,2,1,0:T(8,128)(2,1)S(1)}, bf16[3,2,2,128,128]{4,3,2,1,0:T(8,128)(2,1)S(1)}, u32[]{:S(2)}, u32[]{:S(2)}) collective-permute-start(bf16[3,2,2,128,128]{4,3,2,1,0:T(8,128)(2,1)S(1)} %pad_maximum_fusion.1.q0), channel_id=1, source_target_pairs={{0,3},{1,0},{2,1},{3,2},{4,7},{5,4},{6,5},{7,6},{8,11},{9,8},{10,9... | collective-permute-start | bytes 1179656 | tf_op jit(solution)/shard_map/ppermute | solution.py:42
  19.7 18.9 %collective-permute-start.4 = (bf16[3,2,2,128,128]{4,3,2,1,0:T(8,128)(2,1)S(1)}, bf16[3,2,2,128,128]{4,3,2,1,0:T(8,128)(2,1)S(1)}, u32[]{:S(2)}, u32[]{:S(2)}) collective-permute-start(bf16[3,2,2,128,128]{4,3,2,1,0:T(8,128)(2,1)S(1)} %pad_maximum_fusion.1.q0), channel_id=1, source_target_pairs={{0,2},{1,3},{2,0},{3,1},{4,6},{5,7},{6,4},{7,5},{8,10},{9,11},{10,... | collective-permute-start | bytes 1179656 | tf_op jit(solution)/shard_map/ppermute | solution.py:42
  19.7 18.9 %collective-permute-start.3 = (bf16[3,2,2,128,128]{4,3,2,1,0:T(8,128)(2,1)S(1)}, bf16[3,2,2,128,128]{4,3,2,1,0:T(8,128)(2,1)S(1)}, u32[]{:S(2)}, u32[]{:S(2)}) collective-permute-start(bf16[3,2,2,128,128]{4,3,2,1,0:T(8,128)(2,1)S(1)} %pad_maximum_fusion.1.q0), channel_id=1, source_target_pairs={{0,1},{1,2},{2,3},{3,0},{4,5},{5,6},{6,7},{7,4},{8,9},{9,10},{10,1... | collective-permute-start | bytes 1179656 | tf_op jit(solution)/shard_map/ppermute | solution.py:42
  27.2 23.7 %collective-permute-start.11 = (bf16[4,2,256,128]{3,2,1,0:T(8,128)(2,1)S(1)}, bf16[4,2,256,128]{3,2,1,0:T(8,128)(2,1)}, u32[]{:S(2)}, u32[]{:S(2)}) collective-permute-start(bf16[4,2,256,128]{3,2,1,0:T(8,128)(2,1)S(1)} %pad_maximum_fusion.a0), channel_id=1, source_target_pairs={{0,96},{4,100},{8,104},{12,108},{16,112},{20,116},{24,120},{28,124... | collective-permute-start | bytes 1572872 | tf_op jit(solution)/shard_map/ppermute | solution.py:30
  36.1 16.4 %collective-permute-start.10 = (bf16[4,2,256,128]{3,2,1,0:T(8,128)(2,1)S(1)}, bf16[4,2,256,128]{3,2,1,0:T(8,128)(2,1)S(1)}, u32[]{:S(2)}, u32[]{:S(2)}) collective-permute-start(bf16[4,2,256,128]{3,2,1,0:T(8,128)(2,1)S(1)} %pad_maximum_fusion.a0), channel_id=1, source_target_pairs={{0,64},{4,68},{8,72},{12,76},{16,80},{20,84},{24,88},{28,92},{32,9... | collective-permute-start | bytes 1572872 | tf_op jit(solution)/shard_map/ppermute | solution.py:30
  38.0 21.7 %collective-permute-start.9 = (bf16[4,2,256,128]{3,2,1,0:T(8,128)(2,1)S(1)}, bf16[4,2,256,128]{3,2,1,0:T(8,128)(2,1)S(1)}, u32[]{:S(2)}, u32[]{:S(2)}) collective-permute-start(bf16[4,2,256,128]{3,2,1,0:T(8,128)(2,1)S(1)} %pad_maximum_fusion.a0), channel_id=1, source_target_pairs={{0,32},{4,36},{8,40},{12,44},{16,48},{20,52},{24,56},{28,60},{32,6... | collective-permute-start | bytes 1572872 | tf_op jit(solution)/shard_map/ppermute | solution.py:30
  47.8 11.9 %collective-permute-start.23 = (bf16[8,256,128]{2,1,0:T(8,128)(2,1)S(1)}, bf16[8,256,128]{2,1,0:T(8,128)(2,1)S(1)}, u32[]{:S(2)}, u32[]{:S(2)}) collective-permute-start(bf16[8,256,128]{2,1,0:T(8,128)(2,1)S(1)} %get-tuple-element.46), channel_id=1, source_target_pairs={{0,4},{4,0},{8,12},{12,8},{16,20},{20,16},{24,28},{28,24},{32,36},... | collective-permute-start | bytes 1572872 | tf_op jit(solution)/shard_map/ppermute | solution.py:38
  47.9 12.3 %collective-permute-start.25 = (bf16[8,256,128]{2,1,0:T(8,128)(2,1)S(1)}, bf16[8,256,128]{2,1,0:T(8,128)(2,1)S(1)}, u32[]{:S(2)}, u32[]{:S(2)}) collective-permute-start(bf16[8,256,128]{2,1,0:T(8,128)(2,1)S(1)} %get-tuple-element.47), channel_id=1, source_target_pairs={{0,4},{4,0},{8,12},{12,8},{16,20},{20,16},{24,28},{28,24},{32,36},... | collective-permute-start | bytes 1572872 | tf_op jit(solution)/shard_map/ppermute | solution.py:38
  50.9 9.4 %collective-permute-start.27 = (bf16[8,256,128]{2,1,0:T(8,128)(2,1)S(1)}, bf16[8,256,128]{2,1,0:T(8,128)(2,1)S(1)}, u32[]{:S(2)}, u32[]{:S(2)}) collective-permute-start(bf16[8,256,128]{2,1,0:T(8,128)(2,1)S(1)} %get-tuple-element.48), channel_id=1, source_target_pairs={{0,4},{4,0},{8,12},{12,8},{16,20},{20,16},{24,28},{28,24},{32,36},... | collective-permute-start | bytes 1572872 | tf_op jit(solution)/shard_map/ppermute | solution.py:38
  52.5 10.5 %collective-permute-start.12 = (bf16[4,2,256,128]{3,2,1,0:T(8,128)(2,1)S(1)}, bf16[4,2,256,128]{3,2,1,0:T(8,128)(2,1)S(1)}, u32[]{:S(2)}, u32[]{:S(2)}) collective-permute-start(bf16[4,2,256,128]{3,2,1,0:T(8,128)(2,1)S(1)} %pad_maximum_fusion.a0), channel_id=1, source_target_pairs={{0,4},{4,0},{8,12},{12,8},{16,20},{20,16},{24,28},{28,24},{32,36},... | collective-permute-start | bytes 1572872 | tf_op jit(solution)/shard_map/ppermute | solution.py:38
  60.2 18.2 %collective-permute-start.22 = (bf16[8,256,128]{2,1,0:T(8,128)(2,1)S(1)}, bf16[8,256,128]{2,1,0:T(8,128)(2,1)S(1)}, u32[]{:S(2)}, u32[]{:S(2)}) collective-permute-start(bf16[8,256,128]{2,1,0:T(8,128)(2,1)S(1)} %get-tuple-element.45), channel_id=1, source_target_pairs={{0,4},{4,0},{8,12},{12,8},{16,20},{20,16},{24,28},{28,24},{32,36},... | collective-permute-start | bytes 1572872 | tf_op jit(solution)/shard_map/ppermute | solution.py:38
  63.1 26.4 %collective-permute-start.24 = (bf16[8,256,128]{2,1,0:T(8,128)(2,1)S(1)}, bf16[8,256,128]{2,1,0:T(8,128)(2,1)S(1)}, u32[]{:S(2)}, u32[]{:S(2)}) collective-permute-start(bf16[8,256,128]{2,1,0:T(8,128)(2,1)S(1)} %get-tuple-element.62), channel_id=1, source_target_pairs={{0,32},{4,36},{8,40},{12,44},{16,48},{20,52},{24,56},{28,60},{32,6... | collective-permute-start | bytes 1572872 | tf_op jit(solution)/shard_map/ppermute | solution.py:30
  63.2 28.3 %collective-permute-start.28 = (bf16[8,256,128]{2,1,0:T(8,128)(2,1)S(1)}, bf16[8,256,128]{2,1,0:T(8,128)(2,1)S(1)}, u32[]{:S(2)}, u32[]{:S(2)}) collective-permute-start(bf16[8,256,128]{2,1,0:T(8,128)(2,1)S(1)} %get-tuple-element.63), channel_id=1, source_target_pairs={{0,96},{4,100},{8,104},{12,108},{16,112},{20,116},{24,120},{28,124... | collective-permute-start | bytes 1572872 | tf_op jit(solution)/shard_map/ppermute | solution.py:30
  66.4 27.9 %collective-permute-start.26 = (bf16[8,256,128]{2,1,0:T(8,128)(2,1)S(1)}, bf16[8,256,128]{2,1,0:T(8,128)(2,1)S(1)}, u32[]{:S(2)}, u32[]{:S(2)}) collective-permute-start(bf16[8,256,128]{2,1,0:T(8,128)(2,1)S(1)} %get-tuple-element.64), channel_id=1, source_target_pairs={{0,64},{4,68},{8,72},{12,76},{16,80},{20,84},{24,88},{28,92},{32,9... | collective-permute-start | bytes 1572872 | tf_op jit(solution)/shard_map/ppermute | solution.py:30
  76.9 19.9 %collective-permute-start.19 = (bf16[256,256]{1,0:T(8,128)(2,1)S(1)}, bf16[256,256]{1,0:T(8,128)(2,1)S(1)}, u32[]{:S(2)}, u32[]{:S(2)}) collective-permute-start(bf16[256,256]{1,0:T(8,128)(2,1)S(1)} %get-tuple-element.40), channel_id=1, source_target_pairs={{0,24},{4,28},{8,0},{12,4},{16,8},{20,12},{24,16},{28,20},{32,56},... | collective-permute-start | bytes 393224 | tf_op jit(solution)/shard_map/ppermute | solution.py:34
  78.4 18.5 %collective-permute-start.20 = (bf16[256,256]{1,0:T(8,128)(2,1)S(1)}, bf16[256,256]{1,0:T(8,128)(2,1)S(1)}, u32[]{:S(2)}, u32[]{:S(2)}) collective-permute-start(bf16[256,256]{1,0:T(8,128)(2,1)S(1)} %get-tuple-element.41), channel_id=1, source_target_pairs={{0,16},{4,20},{8,24},{12,28},{16,0},{20,4},{24,8},{28,12},{32,48},... | collective-permute-start | bytes 393224 | tf_op jit(solution)/shard_map/ppermute | solution.py:34
  89.5 25.1 %collective-permute-start.35 = (bf16[8,8,32,128]{3,2,1,0:T(8,128)(2,1)S(1)}, bf16[8,8,32,128]{3,2,1,0:T(8,128)(2,1)S(1)}, u32[]{:S(2)}, u32[]{:S(2)}) collective-permute-start(bf16[8,8,32,128]{3,2,1,0:T(8,128)(2,1)S(1)} %get-tuple-element.55), channel_id=1, source_target_pairs={{0,1},{1,2},{2,3},{3,0},{4,5},{5,6},{6,7},{7,4},{8,9},{9,10},{10,1... | collective-permute-start | bytes 1572872 | tf_op jit(solution)/shard_map/ppermute | solution.py:42
  91.4 25.8 %collective-permute-start.36 = (bf16[8,8,32,128]{3,2,1,0:T(8,128)(2,1)S(1)}, bf16[8,8,32,128]{3,2,1,0:T(8,128)(2,1)S(1)}, u32[]{:S(2)}, u32[]{:S(2)}) collective-permute-start(bf16[8,8,32,128]{3,2,1,0:T(8,128)(2,1)S(1)} %get-tuple-element.56), channel_id=1, source_target_pairs={{0,2},{1,3},{2,0},{3,1},{4,6},{5,7},{6,4},{7,5},{8,10},{9,11},{10,... | collective-permute-start | bytes 1572872 | tf_op jit(solution)/shard_map/ppermute | solution.py:42
  94.3 23.0 %collective-permute-start.37 = (bf16[8,8,32,128]{3,2,1,0:T(8,128)(2,1)S(1)}, bf16[8,8,32,128]{3,2,1,0:T(8,128)(2,1)S(1)}, u32[]{:S(2)}, u32[]{:S(2)}) collective-permute-start(bf16[8,8,32,128]{3,2,1,0:T(8,128)(2,1)S(1)} %get-tuple-element.57), channel_id=1, source_target_pairs={{0,3},{1,0},{2,1},{3,2},{4,7},{5,4},{6,5},{7,6},{8,11},{9,8},{10,9... | collective-permute-start | bytes 1572872 | tf_op jit(solution)/shard_map/ppermute | solution.py:42
  (31 other events, 229.5 us)

commit v2 on v1

v2 whole, which is shorter than its diff:
```python
import functools

import jax
import jax.numpy as jnp
from jax import lax
from jax.experimental import pallas as pl
from jax.experimental.pallas import tpu as pltpu
from jax.sharding import PartitionSpec as P

NY, NX, NC, NZ = 4, 4, 2, 4
BF, F32 = jnp.bfloat16, jnp.float32
ROOT = 0.7978845608028654
CUBE = 0.044715
VMEM = pl.BlockSpec(memory_space=pltpu.VMEM)
SMEM = pl.BlockSpec(memory_space=pltpu.SMEM)
ANY = pl.BlockSpec(memory_space=pl.ANY)


def along(dy, dx, dc):
    pairs = []
    for y in range(NY):
        for x in range(NX):
            for c in range(NC):
                to = (((y + dy) % NY) * NX + (x + dx) % NX) * NC + (c + dc) % NC
                pairs.append(((y * NX + x) * NC + c, to))
    return pairs


def shift_y(value, step):
    return lax.ppermute(value, "blk", along(step, 0, 0))


def shift_x(value, step):
    return lax.ppermute(value, "blk", along(0, step, 0))


def swap_core(value):
    return lax.ppermute(value, "blk", along(0, 0, 1))


def shift_z(value, step):
    return lax.ppermute(value, "tok", [(z, (z + step) % NZ) for z in range(NZ)])


def dot(a, b, ca, cb):
    return lax.dot_general(a, b, (((ca,), (cb,)), ((), ())), preferred_element_type=F32)


def call(body, outs, in_specs, out_specs, flops, nbytes, mib, scratch=()):
    return pl.pallas_call(
        body,
        out_shape=outs,
        in_specs=in_specs,
        out_specs=out_specs,
        scratch_shapes=list(scratch),
        compiler_params=pltpu.CompilerParams(vmem_limit_bytes=mib * 1024 * 1024),
        cost_estimate=pl.CostEstimate(flops=flops, bytes_accessed=nbytes, transcendentals=0),
    )


def sds(shape, dtype):
    return jax.ShapeDtypeStruct(shape, dtype)


def first_body(pos, tok, go, wf, a0, a1, a2, a3, g0, g1, g2, g3, slope, tbuf, sems):
    x = pos[1]
    acts, grads = (a0, a1, a2, a3), (g0, g1, g2, g3)
    order = (1, 3, 2, 0)
    rows = [pl.ds(pl.multiple_of(((x + s) & 3) * 256, 256), 256) for s in range(4)]
    loads = {s: pltpu.make_async_copy(tok.at[rows[s]], tbuf.at[s], sems.at[s]) for s in order}
    moves = {s: pltpu.make_async_copy(go.at[rows[s]], grads[s], sems.at[4 + s]) for s in order}
    for s in order:
        loads[s].start()
    for s in order:
        moves[s].start()
    for s in order:
        loads[s].wait()
        for p in range(2):
            pre = dot(tbuf[s, :, p * 128 : (p + 1) * 128], wf[p], 1, 0)
            sq = pre * pre
            th = jnp.tanh(ROOT * pre * (1.0 + CUBE * sq))
            acts[s][p] = (0.5 * pre * (1.0 + th)).astype(BF)
            slope[s, p] = 0.5 * (1.0 + th) + 0.5 * pre * (1.0 - th * th) * (
                ROOT * (1.0 + 3.0 * CUBE * sq)
            )
    for s in order:
        moves[s].wait()


def tiles(s, p, z, w_own, w0, w1, w2a, w2b, w3):
    found = []
    for k in range(8):
        if s == 0:
            found.append((k, w_own, (p, k)))
        else:
            t, kk = k // 2, k % 2
            slot = ((z - t) & 3) * 2 + kk
            if t == 2:
                found.append((slot, (w2a, w2b)[p], (s - 1, kk)))
            else:
                found.append((slot, (w0, w1, None, w3)[t], (p, s - 1, kk)))
    return found


def back_body(pos, src, live, w_own, w0, w1, w2a, w2b, w3, g0, g1, g2, g3, s0, s1, s2, s3, own, acc):
    y, x, c, z = pos[0], pos[1], pos[2], pos[3]
    acc[...] = jnp.zeros_like(acc)
    for s, g in enumerate((g0, g1, g2, g3)):
        for p in range(2):
            block = ((y * 4 + ((x - s) & 3)) * 2 + c) * 2 + p
            grad = g[:, p * 128 : (p + 1) * 128]
            for slot, ref, at in tiles(s, p, z, w_own, w0, w1, w2a, w2b, w3):
                j = src[block, slot]
                scale = live[block, slot].astype(F32)
                r = j >> 1
                flat = (((r & 1) ^ c) * 16 + (((r >> 3) - y) & 3) * 4 + (((r >> 1) - x) & 3)) * 2 + (j & 1)
                acc[flat] += dot(grad, ref[at], 1, 1) * scale
    for s, out in enumerate((s0, s1, s2, s3)):
        out[...] = acc[32 + 8 * s : 40 + 8 * s].astype(BF)
    own[...] = acc[0:32]


def pick(cat, n, at, abuf, src, live, block, slot, y, x, c):
    j = src[block, slot]
    scale = live[block, slot].astype(F32).astype(BF)
    r = j >> 1
    which = ((r & 1) ^ c) * 4 + ((y - (r >> 3)) & 3)
    cat[n, :, at * 128 : (at + 1) * 128] = abuf[which, (x - (r >> 1)) & 3, j & 1] * scale


def weight_body(pos, src, live, abuf, g0, g1, g2, g3, z0, z1, z2, z3, cat, grads):
    y, x, c, z = pos[0], pos[1], pos[2], pos[3]
    for s, g in enumerate((g0, g1, g2, g3)):
        for p in range(2):
            n = s * 2 + p
            block = ((y * 4 + ((x - s) & 3)) * 2 + c) * 2 + p
            for k in range(8):
                pick(cat, p, k, abuf, src, live, block, k, y, x, c)
            grads[p] = dot(cat[p], g[:, p * 128 : (p + 1) * 128], 0, 0).reshape(8, 128, 128)
            for t, to in enumerate((z0, z1, z2, z3)):
                rows = pl.ds(pl.multiple_of(((z + t) & 3) * 32, 32), 32)
                to[n] = grads[p, :, rows, :].astype(to.dtype)


def layer_body(pos, src, live, w_own, w0, w1, w2a, w2b, w3, abuf, l0, l1, l2, l3, cat):
    y, x, c, z = pos[0], pos[1], pos[2], pos[3]
    for s, out in enumerate((l0, l1, l2, l3)):
        for p in range(2):
            block = ((y * 4 + ((x - s) & 3)) * 2 + c) * 2 + p
            found = tiles(s, p, z, w_own, w0, w1, w2a, w2b, w3)
            for k, (slot, _, _) in enumerate(found):
                pick(cat, p, k, abuf, src, live, block, slot, y, x, c)
            total = None
            for k in range(0, 8, 2):
                _, ref, at = found[k]
                pair = ref[at[:-1] + (slice(at[-1], at[-1] + 2),)].reshape(256, 128)
                part = dot(cat[p, :, k * 128 : (k + 2) * 128], pair, 1, 0)
                total = part if total is None else total + part
            out[:, p * 128 : (p + 1) * 128] = total.astype(BF)


def last_body(pos, tok, wf, slope, h0, h1, h2, h3, gt, f0, f1, f2, f3, total):
    x, z = pos[1], pos[3]
    for s, h in enumerate((h0, h1, h2, h3)):
        rows = pl.ds(pl.multiple_of(((x - s) & 3) * 256, 256), 256)
        for p in range(2):
            cols = slice(p * 128, (p + 1) * 128)
            grad_pre = (h[p].astype(F32) * slope[(4 - s) % 4, p]).astype(BF)
            gt[rows, cols] = dot(grad_pre, wf[p], 1, 1).astype(BF)
            part = dot(tok[rows, cols], grad_pre, 0, 0)
            if s == 0:
                total[p] = part
            else:
                total[p] += part
    for t, out in enumerate((f0, f1, f2, f3)):
        out[...] = total[:, pl.ds(pl.multiple_of(((z + t) & 3) * 32, 32), 32), :]


def join_body(pos, p0, p1, p2, p3, out):
    x = pos[1]
    for s, part in enumerate((p0, p1, p2, p3)):
        out[pl.ds(pl.multiple_of(((x + s) & 3) * 256, 256), 256), :] = part[...]


def ring_gather(value, shift):
    half = value.shape[0] // 2
    behind, ahead = shift(value, 1), shift(value, -1)
    return behind, ahead, shift(behind[:half], 1), shift(ahead[half:], -1)


def ring_sum(parts, shift):
    half = parts[2].shape[0] // 2
    low, high = shift(parts[2][:half], 1), shift(parts[2][half:], -1)
    one = jnp.concatenate([parts[1][:half] + low.astype(F32), parts[1][half:]]).astype(BF)
    three = jnp.concatenate([parts[3][:half], parts[3][half:] + high.astype(F32)]).astype(BF)
    return parts[0] + shift(one, 1).astype(F32) + shift(three, -1).astype(F32)


def shards(tokens, w_first, w_second, tile_src, tile_live, grad_out):
    me, z = lax.axis_index("blk"), lax.axis_index("tok")
    pos = jnp.stack([me // 8, (me // 2) % 4, me % 2, z]).astype(jnp.int32)

    quarter = lax.dynamic_slice_in_dim(w_second, z * 2, 2, 1)
    q0 = jnp.stack([shift_x(quarter, s) for s in (1, 2, 3)], axis=1)
    q1, q3, q2a, q2b = ring_gather(q0, shift_z)
    weights = (w_second, q0, q1, q2a[0], q2b[0], q3)

    chunk = sds((256, 256), BF)
    outs = call(
        first_body,
        [sds((2, 256, 128), BF)] * 4 + [chunk] * 4 + [sds((4, 2, 256, 128), F32)],
        [SMEM, ANY, ANY, VMEM],
        [VMEM] * 9,
        67_000_000 * 2,
        3_500_000,
        8,
        [pltpu.VMEM((4, 256, 256), BF), pltpu.SemaphoreType.DMA((8,))],
    )(pos, tokens, grad_out, w_first)
    acts, grads, slope = outs[:4], outs[4:8], outs[8]
    act_row = jnp.stack([acts[0]] + [shift_x(acts[s], s) for s in (1, 2, 3)])
    grads = [grads[0]] + [shift_x(grads[s], s) for s in (1, 2, 3)]

    behind, ahead, low, high = ring_gather(act_row, shift_y)
    mine = [act_row, behind, low, high, ahead]
    other = [swap_core(part) for part in mine]
    abuf = jnp.concatenate(mine + other).reshape(8, 4, 2, 256, 128)

    piece = sds((8, 256, 128), BF)
    outs = call(
        back_body,
        [piece] * 4 + [sds((32, 256, 128), F32)],
        [SMEM] * 3 + [VMEM] * 10,
        [VMEM] * 5,
        540_000_000 * 2,
        9_000_000,
        20,
        [pltpu.VMEM((64, 256, 128), F32)],
    )(pos, tile_src, tile_live, *weights, *grads)
    own = outs[4]
    swapped = {s: swap_core(outs[s]) for s in (2, 1, 3, 0)}
    sums = [own[8 * s : 8 * s + 8] + swapped[s].astype(F32) for s in range(4)]
    sums[2] = sums[2].astype(BF)
    total = ring_sum(sums, shift_y)
    pieces = [total[0:2]] + [
        shift_x(total[2 * s : 2 * s + 2].astype(BF), s) for s in (1, 2, 3)
    ]

    slab = (8, 8, 32, 128)
    cat = pltpu.VMEM((2, 256, 1024), BF)
    parts = call(
        weight_body,
        [sds(slab, F32), sds(slab, F32), sds(slab, BF), sds(slab, F32)],
        [SMEM] * 3 + [VMEM] * 5,
        [VMEM] * 4,
        540_000_000 * 2,
        12_000_000,
        14,
        [cat, pltpu.VMEM((2, 8, 128, 128), F32)],
    )(pos, tile_src, tile_live, abuf, *grads)
    summed = ring_sum(parts, shift_z)
    grad_second = summed[0:2]
    for part in [shift_x(summed[2 * s : 2 * s + 2].astype(BF), -s) for s in (1, 2, 3)]:
        grad_second = grad_second + part.astype(F32)

    outs = call(
        layer_body,
        [chunk] * 4,
        [SMEM] * 3 + [VMEM] * 7,
        [VMEM] * 4,
        540_000_000 * 2,
        9_000_000,
        10,
        [cat],
    )(pos, tile_src, tile_live, *weights, abuf)
    rows = [outs[0]] + [shift_x(outs[s], -s) for s in (1, 2, 3)]
    layer_out = call(
        join_body, sds((1024, 256), BF), [SMEM] + [VMEM] * 4, VMEM, 0, 1_000_000, 4
    )(pos, *rows)

    strip = sds((2, 32, 128), F32)
    outs = call(
        last_body,
        [sds((1024, 256), BF)] + [strip] * 4,
        [SMEM] + [VMEM] * 7,
        [VMEM] * 5,
        2 * 67_000_000 * 2,
        3_500_000,
        8,
        [pltpu.VMEM((2, 128, 128), F32)],
    )(pos, tokens, w_first, slope, *pieces)
    grad_tokens = outs[0]
    grad_first = outs[1]
    for part in [shift_z(outs[1 + t], t) for t in (1, 2, 3)]:
        grad_first = grad_first + part
    return (layer_out, grad_tokens, grad_first, grad_second)


def solution(mesh):
    in_specs = (
        P("tok", "blk"),
        P("blk", None, None),
        P("blk", None, None, None),
        P(),
        P(),
        P("tok", "blk"),
    )
    out_specs = (
        P("tok", "blk"),
        P("tok", "blk"),
        P("blk", "tok", None),
        P("blk", None, "tok", None),
    )
    return jax.shard_map(shards, mesh=mesh, in_specs=in_specs, out_specs=out_specs, check_vma=False)
```

time: 128 us -> 124 us (0.969)
  waiting for transfers between devices: 44.2 us -> 30.1 us
  local copies, waits for them, and re-layouts: 9.65 us -> 17.7 us
  starting transfers between devices: 45.9 us -> 53.4 us
  other arithmetic: 5.8 us -> 2.91 us
  Pallas kernels: 21.1 us -> 18.3 us
    ppermute x6 -> x8, waiting for transfers between devices: 22.2 us -> 2.02 us  [shift_y(): return lax.ppermute(value, 'blk', along(step, 0, 0))]
    ppermute x9 -> x11, waiting for transfers between devices: 0.78 us -> 18.8 us  [shift_z(): return lax.ppermute(value, 'tok', [(z, (z + step) % NZ) for z in range(NZ)])]
    ppermute x18, waiting for transfers between devices: 21.2 us -> 9.27 us  [shift_x(): return lax.ppermute(value, 'blk', along(0, step, 0))]
    unnamed x30, local copies, waits for them, and re-layouts: 8.65 us -> 15.5 us
    ppermute x6 -> x8, starting transfers between devices: 8.81 us -> 13.8 us  [shift_y(): return lax.ppermute(value, 'blk', along(step, 0, 0))]
    pallas_call x3 -> x4, Pallas kernels: 17.4 us -> 13.3 us  [the longest x1 4.48 us: shards(): call(weight_body, [sds(slab, F32), sds(slab, F32), sds(slab, BF), sds(sla...]
    convert_element_type x1 -> x0, other arithmetic: 2.33 us -> none  [shards(): sums[s].astype(BF)]
    ppermute x18, starting transfers between devices: 20.7 us -> 22.5 us  [shift_x(): return lax.ppermute(value, 'blk', along(0, step, 0))]
  transfers between devices with their start and end apart: 41 -> 46, of which waited for: 13 -> 13; matrix products, arithmetic and copies ran while one was open for 5% -> 12% of each run, Pallas kernels for 17% -> 12%
where the time goes in v2:
time: 124 us; the launch traced here: 123 us
  starting transfers between devices  53.4 us (43%)
  waiting for transfers between devices  30.1 us (24%)
  Pallas kernels  18.3 us (15%)
  local copies, waits for them, and re-layouts  17.7 us (14%)
  other arithmetic  2.91 us (2%)
    ppermute x18, starting transfers between devices, shift_x(): return lax.ppermute(value, 'blk', along(0, step, 0))  22.5 us
    ppermute x11, waiting for transfers between devices, shift_z(): return lax.ppermute(value, 'tok', [(z, (z + step) % NZ) for z in range(NZ)])  18.8 us
    unnamed x30, local copies, waits for them, and re-layouts  15.5 us
    ppermute x11, starting transfers between devices, shift_z(): return lax.ppermute(value, 'tok', [(z, (z + step) % NZ) for z in range(NZ)])  14.9 us
    ppermute x8, starting transfers between devices, shift_y(): return lax.ppermute(value, 'blk', along(step, 0, 0))  13.8 us
    ppermute x18, waiting for transfers between devices, shift_x(): return lax.ppermute(value, 'blk', along(0, step, 0))  9.27 us
    pallas_call x1, Pallas kernels, shards(): call(weight_body, [sds(slab, F32), sds(slab, F32), sds(slab, BF), sds(sla...  4.48 us
    pallas_call x1, Pallas kernels, shards(): call(back_body, [piece] * 4 + [sds((32, 256, 128), F32)], [SMEM] * 3 + [V...  3.8 us
  transfers between devices with their start and end apart: 46, of which 13 were waited for; matrix products, arithmetic and copies ran while one was open for 12% of the time, Pallas kernels for 12%

profile of v2, /device:TPU:0, one launch (start us, length us, event | category | flops | bytes accessed | tf_op | source)
XLA Modules:
  0.0 123.4 jit_solution(11597877675285055512)
XLA Ops:
  3.7 3.2 %shard_map.93 = (bf16[2,256,128]{2,1,0:T(8,128)(2,1)S(1)}, bf16[2,256,128]{2,1,0:T(8,128)(2,1)S(1)}, bf16[2,256,128]{2,1,0:T(8,128)(2,1)S(1)}, bf16[2,256,128]{2...) custom-call(s32[4]{0:T(128)S(1)} %pad_add_fusion.pos, ...), custom_call_target="tpu_custom_call" | custom-call | flops 134000000 | bytes 3500000 | tf_op jit(solution)/shard_map/pallas_call | solution.py:209
  13.7 2.0 %collective-permute-start.8 = (bf16[2,256,128]{2,1,0:T(8,128)(2,1)S(1)}, bf16[2,256,128]{2,1,0:T(8,128)(2,1)S(1)}, u32[]{:S(2)}, u32[]{:S(2)}) collective-permute-start(bf16[2,256,128]{2,1,0:T(8,128)(2,1)S(1)} %get-tuple-element.33), channel_id=1, source_target_pairs={{0,16},{4,20},{8,24},{12,28},{16,0},{20,4},{24,8},{28,12},{32,48},... | collective-permute-start | bytes 393224 | tf_op jit(solution)/shard_map/ppermute | solution.py:34
  19.5 3.4 %collective-permute-done.8 = bf16[2,256,128]{2,1,0:T(8,128)(2,1)S(1)} collective-permute-done((bf16[2,256,128]{2,1,0:T(8,128)(2,1)S(1)}, bf16[2,256,128]{2,1,0:T(8,128)(2,1)S(1)}, u32[]{:S(2)}, u32[]{:S(2)}) %collective-permute-start.8) | collective-permute-done | bytes 131104 | tf_op jit(solution)/shard_map/ppermute | solution.py:34
  27.1 2.0 %collective-permute-start.3 = (bf16[2,3,2,128,128]{4,3,2,1,0:T(8,128)(2,1)S(1)}, bf16[2,3,2,128,128]{4,3,2,1,0:T(8,128)(2,1)S(1)}, u32[]{:S(2)}, u32[]{:S(2)}) collective-permute-start(bf16[2,3,2,128,128]{4,3,2,1,0:T(8,128)(2,1)S(1)} %pad_maximum_fusion.5.w0), channel_id=1, source_target_pairs={{0,1},{1,2},{2,3},{3,0},{4,5},{5,6},{6,7},{7,4},{8,9},{9,10},{10,1... | collective-permute-start | bytes 1179656 | tf_op jit(solution)/shard_map/ppermute | solution.py:42
  29.1 2.2 %collective-permute-start.5 = (bf16[2,3,2,128,128]{4,3,2,1,0:T(8,128)(2,1)S(1)}, bf16[2,3,2,128,128]{4,3,2,1,0:T(8,128)(2,1)S(1)}, u32[]{:S(2)}, u32[]{:S(2)}) collective-permute-start(bf16[2,3,2,128,128]{4,3,2,1,0:T(8,128)(2,1)S(1)} %pad_maximum_fusion.5.w0), channel_id=1, source_target_pairs={{0,3},{1,0},{2,1},{3,2},{4,7},{5,4},{6,5},{7,6},{8,11},{9,8},{10,9... | collective-permute-start | bytes 1179656 | tf_op jit(solution)/shard_map/ppermute | solution.py:42
  32.6 5.9 %collective-permute-done.3.w1 = bf16[2,3,2,128,128]{4,3,2,1,0:T(8,128)(2,1)S(1)} collective-permute-done((bf16[2,3,2,128,128]{4,3,2,1,0:T(8,128)(2,1)S(1)}, bf16[2,3,2,128,128]{4,3,2,1,0:T(8,128)(2,1)S(1)}, u32[]{:S(2)}, u32[]{:S(2)}) %collective-permute-start.3) | collective-permute-done | bytes 393248 | tf_op jit(solution)/shard_map/ppermute | solution.py:42
  38.5 2.6 %collective-permute-start.23 = (bf16[256,256]{1,0:T(8,128)(2,1)S(1)}, bf16[256,256]{1,0:T(8,128)(2,1)S(1)}, u32[]{:S(2)}, u32[]{:S(2)}) collective-permute-start(bf16[256,256]{1,0:T(8,128)(2,1)S(1)} %get-tuple-element.42), channel_id=1, source_target_pairs={{0,16},{4,20},{8,24},{12,28},{16,0},{20,4},{24,8},{28,12},{32,48},... | collective-permute-start | bytes 393224 | tf_op jit(solution)/shard_map/ppermute | solution.py:34
  41.1 3.2 %collective-permute-start.24 = (bf16[256,256]{1,0:T(8,128)(2,1)S(1)}, bf16[256,256]{1,0:T(8,128)(2,1)S(1)}, u32[]{:S(2)}, u32[]{:S(2)}) collective-permute-start(bf16[256,256]{1,0:T(8,128)(2,1)S(1)} %get-tuple-element.43), channel_id=1, source_target_pairs={{0,24},{4,28},{8,0},{12,4},{16,8},{20,12},{24,16},{28,20},{32,56},... | collective-permute-start | bytes 393224 | tf_op jit(solution)/shard_map/ppermute | solution.py:34
  44.4 3.3 %collective-permute-start.6 = (bf16[1,3,2,128,128]{4,3,2,1,0:T(8,128)(2,1)S(1)}, bf16[1,3,2,128,128]{4,3,2,1,0:T(8,128)(2,1)S(1)}, u32[]{:S(2)}, u32[]{:S(2)}) collective-permute-start(bf16[1,3,2,128,128]{4,3,2,1,0:T(8,128)(2,1)S(1)} %slice.123), channel_id=1, source_target_pairs={{0,3},{1,0},{2,1},{3,2},{4,7},{5,4},{6,5},{7,6},{8,11},{9,8},{10,9... | collective-permute-start | bytes 589832 | tf_op jit(solution)/shard_map/ppermute | solution.py:42
  48.7 3.1 %collective-permute-start.13 = (bf16[2,2,256,128]{3,2,1,0:T(8,128)(2,1)S(1)}, bf16[2,2,256,128]{3,2,1,0:T(8,128)(2,1)S(1)}, u32[]{:S(2)}, u32[]{:S(2)}) collective-permute-start(bf16[2,2,256,128]{3,2,1,0:T(8,128)(2,1)S(1)} %slice.125), channel_id=1, source_target_pairs={{0,96},{4,100},{8,104},{12,108},{16,112},{20,116},{24,120},{28,124... | collective-permute-start | bytes 786440 | tf_op jit(solution)/shard_map/ppermute | solution.py:30
  53.2 3.8 %shard_map.96 = (bf16[8,256,128]{2,1,0:T(8,128)(2,1)S(1)}, bf16[8,256,128]{2,1,0:T(8,128)(2,1)S(1)}, bf16[8,256,128]{2,1,0:T(8,128)(2,1)S(1)}, bf16[8,256,128]{2,1,0:T(8,128)(2,1)S(1)}, f32[32,256,128]{2,1,0:T(8,128)S(1)}) custom-call(s32[4]{0:T(128)S(1)} %pad_add_fusion.pos, s32[64,8]{1,0:T(8,128)S(1)} %copy.12.src, s32[64,8]{1,0:T(8,128)S(1)} %copy.13.live, ...), custom_call_target="tpu_custom_call" | custom-call | flops 1080000000 | bytes 9000000 | tf_op jit(solution)/shard_map/pallas_call | solution.py:229
  64.9 2.2 %copy-done = bf16[32,2,256,128]{3,2,1,0:T(8,128)(2,1)S(1)} copy-done((bf16[32,2,256,128]{3,2,1,0:T(8,128)(2,1)S(1)}, bf16[32,2,256,128]{3,2,1,0:T(8,128)(2,1)}, u32[]{:S(2)}) %copy-start) | copy-done | bytes 4194328
  67.0 4.5 %shard_map.98 = (f32[8,8,32,128]{3,2,1,0:T(8,128)S(1)}, f32[8,8,32,128]{3,2,1,0:T(8,128)S(1)}, bf16[8,8,32,128]{3,2,1,0:T(8,128)(2,1)S(1)}, f32[8,8,32,128]{3,2,1,0:T(8,128)S(1)}) custom-call(s32[4]{0:T(128)S(1)} %pad_add_fusion.pos, s32[64,8]{1,0:T(8,128)S(1)} %copy.12.src, s32[64,8]{1,0:T(8,128)S(1)} %copy.13.live, ...), custom_call_target="tpu_custom_call" | custom-call | flops 1080000000 | bytes 12000000 | tf_op jit(solution)/shard_map/pallas_call | solution.py:250
  74.3 3.4 %collective-permute-start.31 = (bf16[4,256,128]{2,1,0:T(8,128)(2,1)S(1)}, bf16[4,256,128]{2,1,0:T(8,128)(2,1)S(1)}, u32[]{:S(2)}, u32[]{:S(2)}) collective-permute-start(bf16[4,256,128]{2,1,0:T(8,128)(2,1)S(1)} %get-tuple-element.74), channel_id=1, source_target_pairs={{0,96},{4,100},{8,104},{12,108},{16,112},{20,116},{24,120},{28,124... | collective-permute-start | bytes 786440 | tf_op jit(solution)/shard_map/ppermute | solution.py:30
  77.9 2.2 %collective-permute-done.41 = bf16[4,8,32,128]{3,2,1,0:T(8,128)(2,1)S(1)} collective-permute-done((bf16[4,8,32,128]{3,2,1,0:T(8,128)(2,1)S(1)}, bf16[4,8,32,128]{3,2,1,0:T(8,128)(2,1)S(1)}, u32[]{:S(2)}, u32[]{:S(2)}) %collective-permute-start.41) | collective-permute-done | bytes 262176 | tf_op jit(solution)/shard_map/ppermute | solution.py:42
  80.2 3.1 %collective-permute-start.42 = (bf16[8,8,32,128]{3,2,1,0:T(8,128)(2,1)S(1)}, bf16[8,8,32,128]{3,2,1,0:T(8,128)(2,1)S(1)}, u32[]{:S(2)}, u32[]{:S(2)}) collective-permute-start(bf16[8,8,32,128]{3,2,1,0:T(8,128)(2,1)S(1)} %pad_maximum_fusion.4), channel_id=1, source_target_pairs={{0,3},{1,0},{2,1},{3,2},{4,7},{5,4},{6,5},{7,6},{8,11},{9,8},{10,9... | collective-permute-start | bytes 1572872 | tf_op jit(solution)/shard_map/ppermute | solution.py:42
  83.6 3.7 %collective-permute-start.32 = (bf16[8,256,128]{2,1,0:T(8,128)(2,1)S(1)}, bf16[8,256,128]{2,1,0:T(8,128)(2,1)S(1)}, u32[]{:S(2)}, u32[]{:S(2)}) collective-permute-start(bf16[8,256,128]{2,1,0:T(8,128)(2,1)S(1)} %pad_maximum_fusion.2), channel_id=1, source_target_pairs={{0,96},{4,100},{8,104},{12,108},{16,112},{20,116},{24,120},{28,124... | collective-permute-start | bytes 1572872 | tf_op jit(solution)/shard_map/ppermute | solution.py:30
  87.4 3.6 %shard_map.94 = (bf16[256,256]{1,0:T(8,128)(2,1)S(1)}, bf16[256,256]{1,0:T(8,128)(2,1)S(1)}, bf16[256,256]{1,0:T(8,128)(2,1)S(1)}, bf16[256,256]{1,0:T(8,128)(2,1)S(1)}) custom-call(s32[4]{0:T(128)S(1)} %pad_add_fusion.pos, s32[64,8]{1,0:T(8,128)S(1)} %copy.12.src, s32[64,8]{1,0:T(8,128)S(1)} %copy.13.live, bf16[2,8,128,128]{3,2,1,0:T(8,128)(2,1)S(1)} %copy-done.4, ...), custom_call_target="tpu_custom_call" | custom-call | flops 1080000000 | bytes 9000000 | tf_op jit(solution)/shard_map/pallas_call | solution.py:265
  91.0 3.2 %collective-permute-done.42 = bf16[8,8,32,128]{3,2,1,0:T(8,128)(2,1)S(1)} collective-permute-done((bf16[8,8,32,128]{3,2,1,0:T(8,128)(2,1)S(1)}, bf16[8,8,32,128]{3,2,1,0:T(8,128)(2,1)S(1)}, u32[]{:S(2)}, u32[]{:S(2)}) %collective-permute-start.42) | collective-permute-done | bytes 524320 | tf_op jit(solution)/shard_map/ppermute | solution.py:42
  94.3 3.6 %collective-permute-done.40 = bf16[8,8,32,128]{3,2,1,0:T(8,128)(2,1)S(1)} collective-permute-done((bf16[8,8,32,128]{3,2,1,0:T(8,128)(2,1)S(1)}, bf16[8,8,32,128]{3,2,1,0:T(8,128)(2,1)S(1)}, u32[]{:S(2)}, u32[]{:S(2)}) %collective-permute-start.40) | collective-permute-done | bytes 524320 | tf_op jit(solution)/shard_map/ppermute | solution.py:42
  99.3 2.0 %collective-permute-done.29 = bf16[8,256,128]{2,1,0:T(8,128)(2,1)S(1)} collective-permute-done((bf16[8,256,128]{2,1,0:T(8,128)(2,1)S(1)}, bf16[8,256,128]{2,1,0:T(8,128)(2,1)S(1)}, u32[]{:S(2)}, u32[]{:S(2)}) %collective-permute-start.29) | collective-permute-done | bytes 524320 | tf_op jit(solution)/shard_map/ppermute | solution.py:30
  102.1 2.2 %collective-permute-start.34 = (bf16[2,256,128]{2,1,0:T(8,128)(2,1)S(1)}, bf16[2,256,128]{2,1,0:T(8,128)(2,1)S(1)}, u32[]{:S(2)}, u32[]{:S(2)}) collective-permute-start(bf16[2,256,128]{2,1,0:T(8,128)(2,1)S(1)} %get-tuple-element.71), channel_id=1, source_target_pairs={{0,16},{4,20},{8,24},{12,28},{16,0},{20,4},{24,8},{28,12},{32,48},... | collective-permute-start | bytes 393224 | tf_op jit(solution)/shard_map/ppermute | solution.py:34
  106.5 2.7 %collective-permute-done.21.p3 = bf16[256,256]{1,0:T(8,128)(2,1)S(1)} collective-permute-done((bf16[256,256]{1,0:T(8,128)(2,1)S(1)}, bf16[256,256]{1,0:T(8,128)(2,1)S(1)}, u32[]{:S(2)}, u32[]{:S(2)}) %collective-permute-start.21) | collective-permute-done | bytes 131104 | tf_op jit(solution)/shard_map/ppermute | solution.py:34
  120.1 2.2 %collective-permute-done.37 = f32[2,32,128]{2,1,0:T(8,128)S(1)} collective-permute-done((f32[2,32,128]{2,1,0:T(8,128)S(1)}, f32[2,32,128]{2,1,0:T(8,128)S(1)}, u32[]{:S(2)}, u32[]{:S(2)}) %collective-permute-start.37) | collective-permute-done | bytes 32800 | tf_op jit(solution)/shard_map/ppermute | solution.py:42
  (135 shorter events, 49.3 us)
Async XLA Ops:
  9.4 15.9 %collective-permute-start.2 = (bf16[2,2,128,128]{3,2,1,0:T(8,128)(2,1)S(1)}, bf16[2,2,128,128]{3,2,1,0:T(8,128)(2,1)S(1)}, u32[]{:S(2)}, u32[]{:S(2)}) collective-permute-start(bf16[2,2,128,128]{3,2,1,0:T(8,128)(2,1)S(1)} %constant_dynamic-slice_fusion), channel_id=1, source_target_pairs={{0,24},{4,28},{8,0},{12,4},{16,8},{20,12},{24,16},{28,20},{32,56},... | collective-permute-start | bytes 393224 | tf_op jit(solution)/shard_map/ppermute | solution.py:34
  11.2 15.8 %collective-permute-start.1 = (bf16[2,2,128,128]{3,2,1,0:T(8,128)(2,1)S(1)}, bf16[2,2,128,128]{3,2,1,0:T(8,128)(2,1)S(1)}, u32[]{:S(2)}, u32[]{:S(2)}) collective-permute-start(bf16[2,2,128,128]{3,2,1,0:T(8,128)(2,1)S(1)} %constant_dynamic-slice_fusion), channel_id=1, source_target_pairs={{0,16},{4,20},{8,24},{12,28},{16,0},{20,4},{24,8},{28,12},{32,48},... | collective-permute-start | bytes 393224 | tf_op jit(solution)/shard_map/ppermute | solution.py:34
  13.1 13.9 %collective-permute-start = (bf16[2,2,128,128]{3,2,1,0:T(8,128)(2,1)S(1)}, bf16[2,2,128,128]{3,2,1,0:T(8,128)(2,1)S(1)}, u32[]{:S(2)}, u32[]{:S(2)}) collective-permute-start(bf16[2,2,128,128]{3,2,1,0:T(8,128)(2,1)S(1)} %constant_dynamic-slice_fusion), channel_id=1, source_target_pairs={{0,8},{4,12},{8,16},{12,20},{16,24},{20,28},{24,0},{28,4},{32,40},... | collective-permute-start | bytes 393224 | tf_op jit(solution)/shard_map/ppermute | solution.py:34
  22.9 21.5 %collective-permute-start.22 = (bf16[256,256]{1,0:T(8,128)(2,1)S(1)}, bf16[256,256]{1,0:T(8,128)(2,1)S(1)}, u32[]{:S(2)}, u32[]{:S(2)}) collective-permute-start(bf16[256,256]{1,0:T(8,128)(2,1)S(1)} %get-tuple-element.41), channel_id=1, source_target_pairs={{0,8},{4,12},{8,16},{12,20},{16,24},{20,28},{24,0},{28,4},{32,40},... | collective-permute-start | bytes 393224 | tf_op jit(solution)/shard_map/ppermute | solution.py:34
  23.7 20.6 %collective-permute-start.10 = (bf16[4,2,256,128]{3,2,1,0:T(8,128)(2,1)S(1)}, bf16[4,2,256,128]{3,2,1,0:T(8,128)(2,1)S(1)}, u32[]{:S(2)}, u32[]{:S(2)}) collective-permute-start(bf16[4,2,256,128]{3,2,1,0:T(8,128)(2,1)S(1)} %pad_maximum_fusion), channel_id=1, source_target_pairs={{0,32},{4,36},{8,40},{12,44},{16,48},{20,52},{24,56},{28,60},{32,6... | collective-permute-start | bytes 1572872 | tf_op jit(solution)/shard_map/ppermute | solution.py:30
  25.3 22.3 %collective-permute-start.12 = (bf16[4,2,256,128]{3,2,1,0:T(8,128)(2,1)S(1)}, bf16[4,2,256,128]{3,2,1,0:T(8,128)(2,1)S(1)}, u32[]{:S(2)}, u32[]{:S(2)}) collective-permute-start(bf16[4,2,256,128]{3,2,1,0:T(8,128)(2,1)S(1)} %pad_maximum_fusion), channel_id=1, source_target_pairs={{0,96},{4,100},{8,104},{12,108},{16,112},{20,116},{24,120},{28,124... | collective-permute-start | bytes 1572872 | tf_op jit(solution)/shard_map/ppermute | solution.py:30
  27.1 11.5 %collective-permute-start.3 = (bf16[2,3,2,128,128]{4,3,2,1,0:T(8,128)(2,1)S(1)}, bf16[2,3,2,128,128]{4,3,2,1,0:T(8,128)(2,1)S(1)}, u32[]{:S(2)}, u32[]{:S(2)}) collective-permute-start(bf16[2,3,2,128,128]{4,3,2,1,0:T(8,128)(2,1)S(1)} %pad_maximum_fusion.5.w0), channel_id=1, source_target_pairs={{0,1},{1,2},{2,3},{3,0},{4,5},{5,6},{6,7},{7,4},{8,9},{9,10},{10,1... | collective-permute-start | bytes 1179656 | tf_op jit(solution)/shard_map/ppermute | solution.py:42
  29.1 12.0 %collective-permute-start.5 = (bf16[2,3,2,128,128]{4,3,2,1,0:T(8,128)(2,1)S(1)}, bf16[2,3,2,128,128]{4,3,2,1,0:T(8,128)(2,1)S(1)}, u32[]{:S(2)}, u32[]{:S(2)}) collective-permute-start(bf16[2,3,2,128,128]{4,3,2,1,0:T(8,128)(2,1)S(1)} %pad_maximum_fusion.5.w0), channel_id=1, source_target_pairs={{0,3},{1,0},{2,1},{3,2},{4,7},{5,4},{6,5},{7,6},{8,11},{9,8},{10,9... | collective-permute-start | bytes 1179656 | tf_op jit(solution)/shard_map/ppermute | solution.py:42
  38.5 10.1 %collective-permute-start.23 = (bf16[256,256]{1,0:T(8,128)(2,1)S(1)}, bf16[256,256]{1,0:T(8,128)(2,1)S(1)}, u32[]{:S(2)}, u32[]{:S(2)}) collective-permute-start(bf16[256,256]{1,0:T(8,128)(2,1)S(1)} %get-tuple-element.42), channel_id=1, source_target_pairs={{0,16},{4,20},{8,24},{12,28},{16,0},{20,4},{24,8},{28,12},{32,48},... | collective-permute-start | bytes 393224 | tf_op jit(solution)/shard_map/ppermute | solution.py:34
  48.6 11.3 %collective-permute-start.14 = (bf16[4,2,256,128]{3,2,1,0:T(8,128)(2,1)S(1)}, bf16[4,2,256,128]{3,2,1,0:T(8,128)(2,1)S(1)}, u32[]{:S(2)}, u32[]{:S(2)}) collective-permute-start(bf16[4,2,256,128]{3,2,1,0:T(8,128)(2,1)S(1)} %pad_maximum_fusion), channel_id=1, source_target_pairs={{0,4},{4,0},{8,12},{12,8},{16,20},{20,16},{24,28},{28,24},{32,36},... | collective-permute-start | bytes 1572872 | tf_op jit(solution)/shard_map/ppermute | solution.py:38
  52.8 11.2 %collective-permute-start.18 = (bf16[4,2,256,128]{3,2,1,0:T(8,128)(2,1)S(1)}, bf16[4,2,256,128]{3,2,1,0:T(8,128)(2,1)S(1)}, u32[]{:S(2)}, u32[]{:S(2)}) collective-permute-start(bf16[4,2,256,128]{3,2,1,0:T(8,128)(2,1)S(1)} %collective-permute-done.12), channel_id=1, source_target_pairs={{0,4},{4,0},{8,12},{12,8},{16,20},{20,16},{24,28},{28,24},{32,36},... | collective-permute-start | bytes 1572872 | tf_op jit(solution)/shard_map/ppermute | solution.py:38
  57.0 16.2 %collective-permute-start.26 = (bf16[8,256,128]{2,1,0:T(8,128)(2,1)S(1)}, bf16[8,256,128]{2,1,0:T(8,128)(2,1)S(1)}, u32[]{:S(2)}, u32[]{:S(2)}) collective-permute-start(bf16[8,256,128]{2,1,0:T(8,128)(2,1)S(1)} %get-tuple-element.46), channel_id=1, source_target_pairs={{0,4},{4,0},{8,12},{12,8},{16,20},{20,16},{24,28},{28,24},{32,36},... | collective-permute-start | bytes 1572872 | tf_op jit(solution)/shard_map/ppermute | solution.py:38
  60.9 13.0 %collective-permute-start.30 = (bf16[8,256,128]{2,1,0:T(8,128)(2,1)S(1)}, bf16[8,256,128]{2,1,0:T(8,128)(2,1)S(1)}, u32[]{:S(2)}, u32[]{:S(2)}) collective-permute-start(bf16[8,256,128]{2,1,0:T(8,128)(2,1)S(1)} %get-tuple-element.48), channel_id=1, source_target_pairs={{0,4},{4,0},{8,12},{12,8},{16,20},{20,16},{24,28},{28,24},{32,36},... | collective-permute-start | bytes 1572872 | tf_op jit(solution)/shard_map/ppermute | solution.py:38
  62.1 11.8 %collective-permute-start.27 = (bf16[8,256,128]{2,1,0:T(8,128)(2,1)S(1)}, bf16[8,256,128]{2,1,0:T(8,128)(2,1)S(1)}, u32[]{:S(2)}, u32[]{:S(2)}) collective-permute-start(bf16[8,256,128]{2,1,0:T(8,128)(2,1)S(1)} %get-tuple-element.47), channel_id=1, source_target_pairs={{0,4},{4,0},{8,12},{12,8},{16,20},{20,16},{24,28},{28,24},{32,36},... | collective-permute-start | bytes 1572872 | tf_op jit(solution)/shard_map/ppermute | solution.py:38
  62.9 36.2 %collective-permute-start.25 = (bf16[8,256,128]{2,1,0:T(8,128)(2,1)S(1)}, bf16[8,256,128]{2,1,0:T(8,128)(2,1)S(1)}, u32[]{:S(2)}, u32[]{:S(2)}) collective-permute-start(bf16[8,256,128]{2,1,0:T(8,128)(2,1)S(1)} %get-tuple-element.45), channel_id=1, source_target_pairs={{0,4},{4,0},{8,12},{12,8},{16,20},{20,16},{24,28},{28,24},{32,36},... | collective-permute-start | bytes 1572872 | tf_op jit(solution)/shard_map/ppermute | solution.py:38
  80.2 14.1 %collective-permute-start.42 = (bf16[8,8,32,128]{3,2,1,0:T(8,128)(2,1)S(1)}, bf16[8,8,32,128]{3,2,1,0:T(8,128)(2,1)S(1)}, u32[]{:S(2)}, u32[]{:S(2)}) collective-permute-start(bf16[8,8,32,128]{3,2,1,0:T(8,128)(2,1)S(1)} %pad_maximum_fusion.4), channel_id=1, source_target_pairs={{0,3},{1,0},{2,1},{3,2},{4,7},{5,4},{6,5},{7,6},{8,11},{9,8},{10,9... | collective-permute-start | bytes 1572872 | tf_op jit(solution)/shard_map/ppermute | solution.py:42
  83.4 14.5 %collective-permute-start.40 = (bf16[8,8,32,128]{3,2,1,0:T(8,128)(2,1)S(1)}, bf16[8,8,32,128]{3,2,1,0:T(8,128)(2,1)S(1)}, u32[]{:S(2)}, u32[]{:S(2)}) collective-permute-start(bf16[8,8,32,128]{3,2,1,0:T(8,128)(2,1)S(1)} %pad_maximum_fusion.3), channel_id=1, source_target_pairs={{0,1},{1,2},{2,3},{3,0},{4,5},{5,6},{6,7},{7,4},{8,9},{9,10},{10,1... | collective-permute-start | bytes 1572872 | tf_op jit(solution)/shard_map/ppermute | solution.py:42
  83.6 15.7 %collective-permute-start.32 = (bf16[8,256,128]{2,1,0:T(8,128)(2,1)S(1)}, bf16[8,256,128]{2,1,0:T(8,128)(2,1)S(1)}, u32[]{:S(2)}, u32[]{:S(2)}) collective-permute-start(bf16[8,256,128]{2,1,0:T(8,128)(2,1)S(1)} %pad_maximum_fusion.2), channel_id=1, source_target_pairs={{0,96},{4,100},{8,104},{12,108},{16,112},{20,116},{24,120},{28,124... | collective-permute-start | bytes 1572872 | tf_op jit(solution)/shard_map/ppermute | solution.py:30
  87.3 13.9 %collective-permute-start.29 = (bf16[8,256,128]{2,1,0:T(8,128)(2,1)S(1)}, bf16[8,256,128]{2,1,0:T(8,128)(2,1)S(1)}, u32[]{:S(2)}, u32[]{:S(2)}) collective-permute-start(bf16[8,256,128]{2,1,0:T(8,128)(2,1)S(1)} %pad_maximum_fusion.1), channel_id=1, source_target_pairs={{0,32},{4,36},{8,40},{12,44},{16,48},{20,52},{24,56},{28,60},{32,6... | collective-permute-start | bytes 1572872 | tf_op jit(solution)/shard_map/ppermute | solution.py:30
  94.3 10.0 %collective-permute-start.19 = (bf16[256,256]{1,0:T(8,128)(2,1)S(1)}, bf16[256,256]{1,0:T(8,128)(2,1)S(1)}, u32[]{:S(2)}, u32[]{:S(2)}) collective-permute-start(bf16[256,256]{1,0:T(8,128)(2,1)S(1)} %get-tuple-element.36), channel_id=1, source_target_pairs={{0,24},{4,28},{8,0},{12,4},{16,8},{20,12},{24,16},{28,20},{32,56},... | collective-permute-start | bytes 393224 | tf_op jit(solution)/shard_map/ppermute | solution.py:34
  101.6 10.5 %collective-permute-start.33 = (bf16[2,256,128]{2,1,0:T(8,128)(2,1)S(1)}, bf16[2,256,128]{2,1,0:T(8,128)(2,1)S(1)}, u32[]{:S(2)}, u32[]{:S(2)}) collective-permute-start(bf16[2,256,128]{2,1,0:T(8,128)(2,1)S(1)} %get-tuple-element.72), channel_id=1, source_target_pairs={{0,8},{4,12},{8,16},{12,20},{16,24},{20,28},{24,0},{28,4},{32,40},... | collective-permute-start | bytes 393224 | tf_op jit(solution)/shard_map/ppermute | solution.py:34
  102.1 12.2 %collective-permute-start.34 = (bf16[2,256,128]{2,1,0:T(8,128)(2,1)S(1)}, bf16[2,256,128]{2,1,0:T(8,128)(2,1)S(1)}, u32[]{:S(2)}, u32[]{:S(2)}) collective-permute-start(bf16[2,256,128]{2,1,0:T(8,128)(2,1)S(1)} %get-tuple-element.71), channel_id=1, source_target_pairs={{0,16},{4,20},{8,24},{12,28},{16,0},{20,4},{24,8},{28,12},{32,48},... | collective-permute-start | bytes 393224 | tf_op jit(solution)/shard_map/ppermute | solution.py:34
  104.3 10.0 %collective-permute-start.35 = (bf16[2,256,128]{2,1,0:T(8,128)(2,1)S(1)}, bf16[2,256,128]{2,1,0:T(8,128)(2,1)S(1)}, u32[]{:S(2)}, u32[]{:S(2)}) collective-permute-start(bf16[2,256,128]{2,1,0:T(8,128)(2,1)S(1)} %get-tuple-element.70), channel_id=1, source_target_pairs={{0,24},{4,28},{8,0},{12,4},{16,8},{20,12},{24,16},{28,20},{32,56},... | collective-permute-start | bytes 393224 | tf_op jit(solution)/shard_map/ppermute | solution.py:34
  105.8 11.5 %collective-permute-start.45 = (bf16[2,8,32,128]{3,2,1,0:T(8,128)(2,1)S(1)}, bf16[2,8,32,128]{3,2,1,0:T(8,128)(2,1)S(1)}, u32[]{:S(2)}, u32[]{:S(2)}) collective-permute-start(bf16[2,8,32,128]{3,2,1,0:T(8,128)(2,1)S(1)} %get-tuple-element.66), channel_id=1, source_target_pairs={{0,8},{4,12},{8,16},{12,20},{16,24},{20,28},{24,0},{28,4},{32,40},... | collective-permute-start | bytes 393224 | tf_op jit(solution)/shard_map/ppermute | solution.py:34
  (30 other events, 264.0 us)

commit v3 on v0

v3 whole, which is shorter than its diff:
```python
import functools

import jax
import jax.numpy as jnp
from jax import lax
from jax.experimental import pallas as pl
from jax.experimental.pallas import tpu as pltpu
from jax.sharding import PartitionSpec as P

NY, NX, NC, NZ = 4, 4, 2, 4
BF, F32 = jnp.bfloat16, jnp.float32
LIMIT = 56 * 1024 * 1024
ROOT = 0.7978845608028654
CUBE = 0.044715
def along(dy, dx, dc):
    pairs = []
    for y in range(NY):
        for x in range(NX):
            for c in range(NC):
                to = (((y + dy) % NY) * NX + (x + dx) % NX) * NC + (c + dc) % NC
                pairs.append(((y * NX + x) * NC + c, to))
    return pairs


def shift_x(value, step):
    return lax.ppermute(value, "blk", along(0, step, 0))


def swap_core(value):
    return lax.ppermute(value, "blk", along(0, 0, 1))


def shift_z(value, step):
    return lax.ppermute(value, "tok", [(z, (z + step) % NZ) for z in range(NZ)])


def dot(a, b, ca, cb):
    return lax.dot_general(a, b, (((ca,), (cb,)), ((), ())), preferred_element_type=F32)


def window(value):
    return pl.BlockSpec(value.shape, lambda step: (0,) * len(value.shape))


def call(body, outs, args, flops, nbytes, scratch=(), kept=()):
    specs = []
    for n, arg in enumerate(args):
        if arg.dtype == jnp.int32:
            specs.append(pl.BlockSpec(memory_space=pltpu.SMEM))
        elif n in kept:
            specs.append(pl.BlockSpec(memory_space=pl.ANY))
        else:
            specs.append(window(arg))
    return pl.pallas_call(
        lambda *refs: body(*refs),
        grid=(1,),
        out_shape=outs,
        in_specs=specs,
        out_specs=[window(out) for out in outs],
        scratch_shapes=list(scratch),
        compiler_params=pltpu.CompilerParams(vmem_limit_bytes=LIMIT),
        cost_estimate=pl.CostEstimate(flops=flops, bytes_accessed=nbytes, transcendentals=0),
    )(*args)


def sds(shape, dtype):
    return jax.ShapeDtypeStruct(shape, dtype)


def first_body(tok, wf, act, slope):
    for n in range(4):
        for p in range(2):
            pre = dot(tok[n * 256 : (n + 1) * 256, p * 128 : (p + 1) * 128], wf[p], 1, 0)
            sq = pre * pre
            th = jnp.tanh(ROOT * pre * (1.0 + CUBE * sq))
            out = (0.5 * pre * (1.0 + th)).astype(BF)
            for y in range(4):
                act[y * 4 + n, p] = out
            slope[n, p] = 0.5 * (1.0 + th) + 0.5 * pre * (1.0 - th * th) * (
                ROOT * (1.0 + 3.0 * CUBE * sq)
            )


def tiles(s, p, z, w_own, parts):
    found = []
    for t in range(4):
        for kk in range(2):
            rows = slice(kk * 128, (kk + 1) * 128)
            if s == 0:
                k = 2 * t + kk
                found.append((k, w_own, (p, slice(k * 128, (k + 1) * 128))))
            else:
                found.append((((z - t) & 3) * 2 + kk, parts[t], (s - 1, p, rows)))
    return found


def back_body(pos, src, live, *refs):
    away, own = refs[9:11]
    w_own, w0, w1, w2, w3, g0, g1, g2, g3 = refs[11:20]
    acc, sems = refs[20:]
    copies = [pltpu.make_async_copy(refs[n], refs[11 + n], sems.at[n]) for n in range(9)]
    for copy in copies:
        copy.start()
    y, x, c, z = pos[0], pos[1], pos[2], pos[3]
    acc[...] = jnp.zeros_like(acc)
    for copy in copies:
        copy.wait()
    for s, g in enumerate((g0, g1, g2, g3)):
        for p in range(2):
            block = ((y * 4 + ((x - s) & 3)) * 2 + c) * 2 + p
            grad = g[:, p * 128 : (p + 1) * 128]
            for slot, ref, at in tiles(s, p, z, w_own, (w0, w1, w2, w3)):
                j = src[block, slot]
                scale = live[block, slot].astype(F32)
                r = j >> 1
                acc[((r & 1) ^ c) * 32 + (r >> 1) * 2 + (j & 1)] += dot(grad, ref[at], 1, 1) * scale
    for n in range(16):
        away[n] = acc[32 + 2 * n : 34 + 2 * n].astype(BF)
        own[n] = acc[2 * n : 2 * n + 2].astype(BF)


def load_acts(mine, other, abuf, sems):
    copies = [
        pltpu.make_async_copy(part, abuf.at[n], sems.at[n]) for n, part in enumerate((mine, other))
    ]
    for copy in copies:
        copy.start()
    for copy in copies:
        copy.wait()


def pick(cat, n, at, abuf, src, live, block, slot, c):
    j = src[block, slot]
    scale = live[block, slot].astype(F32).astype(BF)
    r = j >> 1
    cat[n, :, at * 128 : (at + 1) * 128] = abuf[(r & 1) ^ c, r >> 1, j & 1] * scale


def weight_body(pos, src, live, mine, other, g0, g1, g2, g3, z0, z1, z2, z3, abuf, cat, grads, sems):
    y, x, c, z = pos[0], pos[1], pos[2], pos[3]
    load_acts(mine, other, abuf, sems)
    for s, g in enumerate((g0, g1, g2, g3)):
        for p in range(2):
            n = s * 2 + p
            block = ((y * 4 + ((x - s) & 3)) * 2 + c) * 2 + p
            for k in range(8):
                pick(cat, p, k, abuf, src, live, block, k, c)
            grads[p] = dot(cat[p], g[:, p * 128 : (p + 1) * 128], 0, 0).reshape(8, 128, 128)
            for t, to in enumerate((z0, z1, z2, z3)):
                rows = pl.ds(pl.multiple_of(((z + t) & 3) * 32, 32), 32)
                to[n] = grads[p, :, rows, :].astype(to.dtype)


def layer_body(pos, src, live, w_own, w0, w1, w2, w3, mine, other, l0, l1, l2, l3, abuf, cat, sems):
    y, x, c, z = pos[0], pos[1], pos[2], pos[3]
    load_acts(mine, other, abuf, sems)
    for s, out in enumerate((l0, l1, l2, l3)):
        for p in range(2):
            block = ((y * 4 + ((x - s) & 3)) * 2 + c) * 2 + p
            found = tiles(s, p, z, w_own, (w0, w1, w2, w3))
            for k, (slot, _, _) in enumerate(found):
                pick(cat, p, k, abuf, src, live, block, slot, c)
            total = None
            for k in range(0, 8, 2):
                _, ref, at = found[k]
                both = ref[at[:-1] + (slice(at[-1].start, at[-1].start + 256),)]
                part = dot(cat[p, :, k * 128 : (k + 2) * 128], both, 1, 0)
                total = part if total is None else total + part
            out[:, p * 128 : (p + 1) * 128] = total.astype(BF)


def join_body(pos, p0, p1, p2, p3, out):
    x = pos[1]
    for s, part in enumerate((p0, p1, p2, p3)):
        out[pl.ds(pl.multiple_of(((x + s) & 3) * 256, 256), 256), :] = part[...]


def last_body(pos, tok, wf, slope, sums, gt, f0, f1, f2, f3, total):
    z = pos[3]
    for n in range(4):
        rows = slice(n * 256, (n + 1) * 256)
        for p in range(2):
            cols = slice(p * 128, (p + 1) * 128)
            grad_act = sums[n, p].astype(F32)
            for y in range(1, 4):
                grad_act += sums[y * 4 + n, p].astype(F32)
            grad_pre = (grad_act * slope[n, p]).astype(BF)
            gt[rows, cols] = dot(grad_pre, wf[p], 1, 1).astype(BF)
            part = dot(tok[rows, cols], grad_pre, 0, 0)
            if n == 0:
                total[p] = part
            else:
                total[p] += part
    for t, out in enumerate((f0, f1, f2, f3)):
        out[...] = total[:, pl.ds(pl.multiple_of(((z + t) & 3) * 32, 32), 32), :]


def exchange(value):
    groups = [[n * NC + c for n in range(NY * NX)] for c in range(NC)]
    return lax.all_to_all(value, "blk", 0, 0, axis_index_groups=groups, tiled=True)


def shards(tokens, w_first, w_second, tile_src, tile_live, grad_out):
    me, z = lax.axis_index("blk"), lax.axis_index("tok")
    pos = jnp.stack([me // 8, (me // 2) % 4, me % 2, z]).astype(jnp.int32)
    w_own = w_second.reshape(2, 1024, 128)

    quarter = lax.dynamic_slice_in_dim(w_own, z * 256, 256, 1)
    w0 = jnp.stack([shift_x(quarter, s) for s in (1, 2, 3)])

    whole, chunk = (16, 2, 256, 128), sds((256, 256), BF)
    x = (me // 2) % 4
    grads = [
        lax.dynamic_slice_in_dim(grad_out, ((x + s) % 4) * 256, 256, 0) for s in range(4)
    ]
    grads = [grads[0]] + [shift_x(grads[s], s) for s in (1, 2, 3)]
    act, slope = call(
        first_body,
        [sds(whole, BF), sds((4, 2, 256, 128), F32)],
        [tokens, w_first],
        67_000_000 * 2,
        3_500_000,
    )
    act, *_ = lax.optimization_barrier((act, w0, *grads[1:]))
    mine = exchange(act)
    weights = [w_own, w0] + [shift_z(w0, t) for t in (1, 2, 3)]

    inputs = [*weights, *grads]
    away, own = pl.pallas_call(
        back_body,
        out_shape=[sds(whole, BF)] * 2,
        in_specs=[pl.BlockSpec(memory_space=pltpu.SMEM)] * 3 + [pl.BlockSpec(memory_space=pl.ANY)] * 9,
        out_specs=[pl.BlockSpec(memory_space=pltpu.VMEM)] * 2,
        scratch_shapes=[pltpu.VMEM(part.shape, BF) for part in inputs]
        + [pltpu.VMEM((64, 256, 128), F32), pltpu.SemaphoreType.DMA((9,))],
        compiler_params=pltpu.CompilerParams(vmem_limit_bytes=LIMIT),
        cost_estimate=pl.CostEstimate(flops=1_080_000_000, bytes_accessed=9_000_000, transcendentals=0),
    )(pos, tile_src, tile_live, *inputs)
    away, mine = lax.optimization_barrier((away, mine))
    parts = (own.astype(F32) + swap_core(away).astype(F32)).astype(BF)
    parts, mine_later = lax.optimization_barrier((parts, mine))
    sums = exchange(parts)
    other = swap_core(mine_later)

    slab = (8, 8, 32, 128)
    cat = pltpu.VMEM((2, 256, 1024), BF)
    abuf = pltpu.VMEM((2, 16, 2, 256, 128), BF)
    parts = call(
        weight_body,
        [sds(slab, F32)] + [sds(slab, BF)] * 3,
        [pos, tile_src, tile_live, mine, other, *grads],
        540_000_000 * 2,
        12_000_000,
        [abuf, cat, pltpu.VMEM((2, 8, 128, 128), F32), pltpu.SemaphoreType.DMA((2,))],
        (3, 4),
    )
    summed, after_z = parts[0], [shift_z(parts[t], t) for t in (1, 2, 3)]
    other, _ = lax.optimization_barrier((other, parts[1]))
    layer = call(
        layer_body,
        [chunk] * 4,
        [pos, tile_src, tile_live, *weights, mine, other],
        540_000_000 * 2,
        9_000_000,
        [abuf, cat, pltpu.SemaphoreType.DMA((2,))],
        (8, 9),
    )
    sums, *_ = lax.optimization_barrier((sums, *layer))
    outs = call(
        last_body,
        [sds((1024, 256), BF)] + [sds((2, 32, 128), F32)] * 4,
        [pos, tokens, w_first, slope, sums],
        2 * 67_000_000 * 2,
        3_500_000,
        [pltpu.VMEM((2, 128, 128), F32)],
    )
    grad_tokens = outs[0]
    grad_first = outs[1]
    for part in [shift_z(outs[1 + t], t) for t in (1, 2, 3)]:
        grad_first = grad_first + part
    for part in after_z:
        summed = summed + part.astype(F32)
    grad_second = summed[0:2]
    for part in [shift_x(summed[2 * s : 2 * s + 2].astype(BF), -s) for s in (1, 2, 3)]:
        grad_second = grad_second + part.astype(F32)

    rows = [layer[0], shift_x(layer[1], -1), None, shift_x(layer[3], -3)]
    layer2, _ = lax.optimization_barrier((layer[2], rows[1]))
    rows[2] = shift_x(layer2, -2)
    (layer_out,) = call(join_body, [sds((1024, 256), BF)], [pos, *rows], 0, 1_000_000)
    return (layer_out, grad_tokens, grad_first, grad_second)


def solution(mesh):
    in_specs = (
        P("tok", "blk"),
        P("blk", None, None),
        P("blk", None, None, None),
        P(),
        P(),
        P("tok", "blk"),
    )
    out_specs = (
        P("tok", "blk"),
        P("tok", "blk"),
        P("blk", "tok", None),
        P("blk", None, "tok", None),
    )
    return jax.shard_map(shards, mesh=mesh, in_specs=in_specs, out_specs=out_specs, check_vma=False)
```

time: 400 us -> 125 us (0.31)
  waiting for transfers between devices: 257 us -> 41.4 us
  local copies, waits for them, and re-layouts: 77.1 us -> 5.44 us
  matrix products: 48.2 us -> 0 us
  starting transfers between devices: 0.34 us -> 39.6 us
  Pallas kernels: 0 us -> 30.6 us
  between operations: 14.5 us -> 0.87 us
  other arithmetic: 0.83 us -> 6.06 us
    reduce_scatter x2 -> x0, waiting for transfers between devices: 186 us -> none  [the longest x1 167 us: shards(): lax.psum_scatter(jnp.einsum('qj,tqb->jtb', one_hot, contribution, precisi...]
    all_gather x1 -> x0, waiting for transfers between devices: 70.7 us -> none  [shards(): lax.all_gather(activated.reshape(tok_rows, per_dev * tile_width), 'blk',...]
    dot_general x8 -> x0, matrix products: 48.2 us -> none  [the longest x1 21.5 us: shards(): jnp.einsum('qj,tqb->jtb', one_hot, contribution, precision=lax.Precision....]
    reshape x4 -> x0, local copies, waits for them, and re-layouts: 39.8 us -> none  [the longest x1 22.7 us: shards(): piece_blocks = piece_rows.reshape(tok_rows, block_count, tile_width)]
    dot_general x2 -> x0, local copies, waits for them, and re-layouts: 33 us -> none  [the longest x1 32.2 us: shards(): jnp.einsum('qj,tqb->jtb', one_hot, contribution, precision=lax.Precision....]
    pallas_call x0 -> x6, Pallas kernels: none -> 30.6 us  [the longest x5 23.6 us: call(): pl.pallas_call(lambda *refs: body(*refs), grid=(1,), out_shape=outs, in_s...]
    ppermute x0 -> x23, waiting for transfers between devices: none -> 27.4 us  [the longest x9 17 us: shift_z(): return lax.ppermute(value, 'tok', [(z, (z + step) % NZ) for z in range(NZ)])]
    ppermute x0 -> x23, starting transfers between devices: none -> 27.2 us  [the longest x12 15.3 us: shift_x(): return lax.ppermute(value, 'blk', along(0, step, 0))]
  transfers between devices with their start and end apart: 4 -> 25, of which waited for: 3 -> 11; matrix products, arithmetic and copies ran while one was open for 13% -> 4% of each run, Pallas kernels for 0% -> 25%
where the time goes in v3:
time: 125 us; the launch traced here: 124 us
  waiting for transfers between devices  41.4 us (33%)
  starting transfers between devices  39.6 us (32%)
  Pallas kernels  30.6 us (24%)
  other arithmetic  6.06 us (5%)
  local copies, waits for them, and re-layouts  5.44 us (4%)
    pallas_call x5, Pallas kernels, call(): pl.pallas_call(lambda *refs: body(*refs), grid=(1,), out_shape=outs, in_s...  23.6 us
    ppermute x9, waiting for transfers between devices, shift_z(): return lax.ppermute(value, 'tok', [(z, (z + step) % NZ) for z in range(NZ)])  17 us
    ppermute x12, starting transfers between devices, shift_x(): return lax.ppermute(value, 'blk', along(0, step, 0))  15.3 us
    all_to_all x2, waiting for transfers between devices, exchange(): lax.all_to_all(value, 'blk', 0, 0, axis_index_groups=groups, tiled=True)  14 us
    all_to_all x2, starting transfers between devices, exchange(): lax.all_to_all(value, 'blk', 0, 0, axis_index_groups=groups, tiled=True)  12.4 us
    ppermute x9, starting transfers between devices, shift_z(): return lax.ppermute(value, 'tok', [(z, (z + step) % NZ) for z in range(NZ)])  11.7 us
    pallas_call x1, Pallas kernels, shards(): pl.pallas_call(back_body, out_shape=[sds(whole, BF)] * 2, in_specs=[pl.Bl...  7 us
    ppermute x12, waiting for transfers between devices, shift_x(): return lax.ppermute(value, 'blk', along(0, step, 0))  6.11 us
  transfers between devices with their start and end apart: 25, of which 11 were waited for; matrix products, arithmetic and copies ran while one was open for 4% of the time, Pallas kernels for 25%

profile of v3, /device:TPU:0, one launch (start us, length us, event | category | flops | bytes accessed | tf_op | source)
XLA Modules:
  0.0 124.0 jit_solution(828085767640774604)
XLA Ops:
  1.6 2.9 %collective-permute-start.2 = (bf16[2,256,128]{2,1,0:T(8,128)(2,1)S(1)}, bf16[2,256,128]{2,1,0:T(8,128)(2,1)S(1)}, u32[]{:S(2)}, u32[]{:S(2)}) collective-permute-start(bf16[2,256,128]{2,1,0:T(8,128)(2,1)S(1)} %constant_dynamic-slice_fusion.4), channel_id=1, source_target_pairs={{0,24},{4,28},{8,0},{12,4},{16,8},{20,12},{24,16},{28,20},{32,56},... | collective-permute-start | bytes 393224 | tf_op jit(solution)/shard_map/ppermute | solution.py:26
  6.2 1.8 %constant_dynamic-slice_fusion = (bf16[256,256]{1,0:T(8,128)(2,1)S(1)}, bf16[256,256]{1,0:T(8,128)(2,1)S(1)}, bf16[256,256]{1,0:T(8,128)(2,1)}, bf16[256,256]{1,0:T(8,128)(2,1)S(1)}) fusion(bf16[1024,256]{1,0:T(8,128)(2,1)} %param.11, s32[]{:T(128)S(6)} %select_n.64, s32[]{:T(128)S(6)} %select_n.60, s32[]{:T(128)S(6)} %select_n.58, s32[]{:T(128)S(6)} %select_n.62), kind=kLoop, calls=%fused_computation.7 | loop fusion | bytes 1048592 | tf_op jit(solution)/shard_map/dynamic_slice | solution.py:214
  7.9 2.4 %collective-permute-start.8 = (bf16[256,256]{1,0:T(8,128)(2,1)S(1)}, bf16[256,256]{1,0:T(8,128)(2,1)S(1)}, u32[]{:S(2)}, u32[]{:S(2)}) collective-permute-start(bf16[256,256]{1,0:T(8,128)(2,1)S(1)} %get-tuple-element.59), channel_id=1, source_target_pairs={{0,24},{4,28},{8,0},{12,4},{16,8},{20,12},{24,16},{28,20},{32,56},... | collective-permute-start | bytes 393224 | tf_op jit(solution)/shard_map/ppermute | solution.py:26
  11.8 3.5 %shard_map.94 = (bf16[16,2,256,128]{3,2,1,0:T(8,128)(2,1)}, f32[4,2,256,128]{3,2,1,0:T(8,128)}) custom-call(bf16[1024,256]{1,0:T(8,128)(2,1)} %refs_1_.5, bf16[2,128,128]{2,1,0:T(8,128)(2,1)} %refs_2_.3), custom_call_target="tpu_custom_call" | custom-call | flops 134000000 | bytes 3500000 | tf_op jit(solution)/shard_map/pallas_call | solution.py:54
  15.4 2.6 %collective-permute-done.6.refs_6_ = bf16[256,256]{1,0:T(8,128)(2,1)S(1)} collective-permute-done((bf16[256,256]{1,0:T(8,128)(2,1)S(1)}, bf16[256,256]{1,0:T(8,128)(2,1)S(1)}, u32[]{:S(2)}, u32[]{:S(2)}) %collective-permute-start.6) | collective-permute-done | bytes 131104 | tf_op jit(solution)/shard_map/ppermute | solution.py:26
  18.0 1.4 %collective-permute-done.7.refs_7_ = bf16[256,256]{1,0:T(8,128)(2,1)S(1)} collective-permute-done((bf16[256,256]{1,0:T(8,128)(2,1)S(1)}, bf16[256,256]{1,0:T(8,128)(2,1)S(1)}, u32[]{:S(2)}, u32[]{:S(2)}) %collective-permute-start.7) | collective-permute-done | bytes 131104 | tf_op jit(solution)/shard_map/ppermute | solution.py:26
  20.0 5.4 %all-to-all-start = ((bf16[16,2,256,128]{3,2,1,0:T(8,128)(2,1)}), bf16[16,2,256,128]{3,2,1,0:T(8,128)(2,1)S(1)}, u32[]{:S(2)}, u32[]{:S(2)}) async-start(bf16[16,2,256,128]{3,2,1,0:T(8,128)(2,1)} %get-tuple-element.31), calls=%async_computation | async-start | bytes 4194304 | tf_op jit(solution)/shard_map/all_to_all | solution.py:200
  25.4 4.1 %collective-permute-start.5 = (bf16[3,2,256,128]{3,2,1,0:T(8,128)(2,1)S(1)}, bf16[3,2,256,128]{3,2,1,0:T(8,128)(2,1)S(1)}, u32[]{:S(2)}, u32[]{:S(2)}) collective-permute-start(bf16[3,2,256,128]{3,2,1,0:T(8,128)(2,1)S(1)} %pad_maximum_fusion.refs_1_.refs_4_), channel_id=1, source_target_pairs={{0,3},{1,0},{2,1},{3,2},{4,7},{5,4},{6,5},{7,6},{8,11},{9,8},{10,9... | collective-permute-start | bytes 1179656 | tf_op jit(solution)/shard_map/ppermute | solution.py:34
  32.8 11.8 %collective-permute-done.5.refs_4_.refs_7_ = bf16[3,2,256,128]{3,2,1,0:T(8,128)(2,1)S(1)} collective-permute-done((bf16[3,2,256,128]{3,2,1,0:T(8,128)(2,1)S(1)}, bf16[3,2,256,128]{3,2,1,0:T(8,128)(2,1)S(1)}, u32[]{:S(2)}, u32[]{:S(2)}) %collective-permute-start.5) | collective-permute-done | bytes 393248 | tf_op jit(solution)/shard_map/ppermute | solution.py:34
  44.6 3.5 %collective-permute-done.3.refs_2_.refs_5_ = bf16[3,2,256,128]{3,2,1,0:T(8,128)(2,1)} collective-permute-done((bf16[3,2,256,128]{3,2,1,0:T(8,128)(2,1)S(1)}, bf16[3,2,256,128]{3,2,1,0:T(8,128)(2,1)}, u32[]{:S(2)}, u32[]{:S(2)}) %collective-permute-start.3) | collective-permute-done | bytes 393248 | tf_op jit(solution)/shard_map/ppermute | solution.py:34
  48.2 7.0 %shard_map.93 = (bf16[16,2,256,128]{3,2,1,0:T(8,128)(2,1)}, bf16[16,2,256,128]{3,2,1,0:T(8,128)(2,1)}) custom-call(s32[4]{0:T(128)} %pad_add_fusion.pos.refs_0_, s32[64,8]{1,0:T(8,128)} %copy.14.src.refs_1_, s32[64,8]{1,0:T(8,128)} %copy.15.live.refs_2_, bf16[2,1024,128]{2,1,0:T(8,128)(2,1)} %bitcast.9, bf16[3,2,256,128]{3,2,1,0:T(8,128)(2,1)} %copy-done.1, ...), custom_call_target="tpu_custom_call" | custom-call | flops 1080000000 | bytes 9000000 | tf_op jit(solution)/shard_map/pallas_call | solution.py:229
  55.3 4.4 %collective-permute-done.9 = bf16[16,2,256,128]{3,2,1,0:T(8,128)(2,1)S(1)} collective-permute-done((bf16[16,2,256,128]{3,2,1,0:T(8,128)(2,1)}, bf16[16,2,256,128]{3,2,1,0:T(8,128)(2,1)S(1)}, u32[]{:S(2)}, u32[]{:S(2)}) %collective-permute-start.9) | collective-permute-done | bytes 2097184 | tf_op jit(solution)/shard_map/ppermute | solution.py:30
  59.6 3.7 %add_convert_fusion = bf16[16,2,256,128]{3,2,1,0:T(8,128)(2,1)} fusion(bf16[16,2,256,128]{3,2,1,0:T(8,128)(2,1)S(1)} %collective-permute-done.9, bf16[16,2,256,128]{3,2,1,0:T(8,128)(2,1)} %get-tuple-element.33), kind=kLoop, calls=%fused_computation | loop fusion | flops 4194304 | bytes 6291456 | tf_op jit(solution)/shard_map/convert_element_type | solution.py:240
  63.5 6.9 %all-to-all-start.1 = ((bf16[16,2,256,128]{3,2,1,0:T(8,128)(2,1)}), bf16[16,2,256,128]{3,2,1,0:T(8,128)(2,1)}, u32[]{:S(2)}, u32[]{:S(2)}) async-start(bf16[16,2,256,128]{3,2,1,0:T(8,128)(2,1)} %add_convert_fusion), calls=%async_computation.1 | async-start | bytes 4194304 | tf_op jit(solution)/shard_map/all_to_all | solution.py:200
  70.4 8.4 %shard_map.95 = (f32[8,8,32,128]{3,2,1,0:T(8,128)}, bf16[8,8,32,128]{3,2,1,0:T(8,128)(2,1)}, bf16[8,8,32,128]{3,2,1,0:T(8,128)(2,1)}, bf16[8,8,32,128]{3,2,1,0:T(8,128)(2,1)}) custom-call(s32[4]{0:T(128)} %pad_add_fusion.pos.refs_0_, s32[64,8]{1,0:T(8,128)} %copy.14.src.refs_1_, s32[64,8]{1,0:T(8,128)} %copy.15.live.refs_2_, ...), custom_call_target="tpu_custom_call" | custom-call | flops 1080000000 | bytes 12000000 | tf_op jit(solution)/shard_map/pallas_call | solution.py:54
  81.5 6.4 %shard_map.96 = (bf16[256,256]{1,0:T(8,128)(2,1)}, bf16[256,256]{1,0:T(8,128)(2,1)}, bf16[256,256]{1,0:T(8,128)(2,1)}, bf16[256,256]{1,0:T(8,128)(2,1)}) custom-call(s32[4]{0:T(128)} %pad_add_fusion.pos.refs_0_, s32[64,8]{1,0:T(8,128)} %copy.14.src.refs_1_, s32[64,8]{1,0:T(8,128)} %copy.15.live.refs_2_, bf16[2,1024,128]{2,1,0:T(8,128)(2,1)} %bitcast.10, ...), custom_call_target="tpu_custom_call" | custom-call | flops 1080000000 | bytes 9000000 | tf_op jit(solution)/shard_map/pallas_call | solution.py:54
  88.0 3.1 %collective-permute-start.11 = (bf16[256,256]{1,0:T(8,128)(2,1)}, bf16[256,256]{1,0:T(8,128)(2,1)S(1)}, u32[]{:S(2)}, u32[]{:S(2)}) collective-permute-start(bf16[256,256]{1,0:T(8,128)(2,1)} %get-tuple-element.39), channel_id=1, source_target_pairs={{0,24},{4,28},{8,0},{12,4},{16,8},{20,12},{24,16},{28,20},{32,56},... | collective-permute-start | bytes 393224 | tf_op jit(solution)/shard_map/ppermute | solution.py:26
  91.1 14.0 %all-to-all-done.1.refs_4_ = bf16[16,2,256,128]{3,2,1,0:T(8,128)(2,1)} async-done(((bf16[16,2,256,128]{3,2,1,0:T(8,128)(2,1)}), bf16[16,2,256,128]{3,2,1,0:T(8,128)(2,1)}, u32[]{:S(2)}, u32[]{:S(2)}) %all-to-all-start.1) | async-done | bytes 2097184 | tf_op jit(solution)/shard_map/all_to_all | solution.py:200
  105.1 3.4 %shard_map.98 = (bf16[1024,256]{1,0:T(8,128)(2,1)}, f32[2,32,128]{2,1,0:T(8,128)}, f32[2,32,128]{2,1,0:T(8,128)}, f32[2,32,128]{2,1,0:T(8,128)}, f32[2,32,128]{2,1,0:T(8,128)}) custom-call(s32[4]{0:T(128)} %pad_add_fusion.pos.refs_0_, bf16[1024,256]{1,0:T(8,128)(2,1)} %refs_1_.5, bf16[2,128,128]{2,1,0:T(8,128)(2,1)} %refs_2_.3, ...), custom_call_target="tpu_custom_call" | custom-call | flops 268000000 | bytes 3500000 | tf_op jit(solution)/shard_map/pallas_call | solution.py:54
  108.6 2.5 %collective-permute-start.15 = (f32[2,32,128]{2,1,0:T(8,128)}, f32[2,32,128]{2,1,0:T(8,128)S(1)}, u32[]{:S(2)}, u32[]{:S(2)}) collective-permute-start(f32[2,32,128]{2,1,0:T(8,128)} %get-tuple-element.49), channel_id=1, source_target_pairs={{0,2},{1,3},{2,0},{3,1},{4,6},{5,7},{6,4},{7,5},{8,10},{9,11},{10,... | collective-permute-start | bytes 98312 | tf_op jit(solution)/shard_map/ppermute | solution.py:34
  112.6 1.3 %collective-permute-done.14 = f32[2,32,128]{2,1,0:T(8,128)S(1)} collective-permute-done((f32[2,32,128]{2,1,0:T(8,128)}, f32[2,32,128]{2,1,0:T(8,128)S(1)}, u32[]{:S(2)}, u32[]{:S(2)}) %collective-permute-start.14) | collective-permute-done | bytes 32800 | tf_op jit(solution)/shard_map/ppermute | solution.py:34
  114.3 1.6 %collective-permute-start.22 = (bf16[2,8,32,128]{3,2,1,0:T(8,128)(2,1)S(1)}, bf16[2,8,32,128]{3,2,1,0:T(8,128)(2,1)S(1)}, u32[]{:S(2)}, u32[]{:S(2)}) collective-permute-start(bf16[2,8,32,128]{3,2,1,0:T(8,128)(2,1)S(1)} %get-tuple-element.57), channel_id=1, source_target_pairs={{0,8},{4,12},{8,16},{12,20},{16,24},{20,28},{24,0},{28,4},{32,40},... | collective-permute-start | bytes 393224 | tf_op jit(solution)/shard_map/ppermute | solution.py:26
  116.0 2.3 %collective-permute-start.21 = (bf16[2,8,32,128]{3,2,1,0:T(8,128)(2,1)S(1)}, bf16[2,8,32,128]{3,2,1,0:T(8,128)(2,1)S(1)}, u32[]{:S(2)}, u32[]{:S(2)}) collective-permute-start(bf16[2,8,32,128]{3,2,1,0:T(8,128)(2,1)S(1)} %get-tuple-element.58), channel_id=1, source_target_pairs={{0,16},{4,20},{8,24},{12,28},{16,0},{20,4},{24,8},{28,12},{32,48},... | collective-permute-start | bytes 393224 | tf_op jit(solution)/shard_map/ppermute | solution.py:26
  120.8 1.9 %shard_map.97 = bf16[1024,256]{1,0:T(8,128)(2,1)} custom-call(s32[4]{0:T(128)} %pad_add_fusion.pos.refs_0_, bf16[256,256]{1,0:T(8,128)(2,1)} %get-tuple-element.38.refs_1_, bf16[256,256]{1,0:T(8,128)(2,1)} %copy-done.8, bf16[256,256]{1,0:T(8,128)(2,1)} %copy-done.10, bf16[256,256]{1,0:T(8,128)(2,1)} %copy-done.9), custom_call_target="tpu_custom_call" | custom-call | bytes 1000000 | tf_op jit(solution)/shard_map/pallas_call | solution.py:54
  (73 shorter events, 16.8 us)
Async XLA Ops:
  1.6 9.0 %collective-permute-start.2 = (bf16[2,256,128]{2,1,0:T(8,128)(2,1)S(1)}, bf16[2,256,128]{2,1,0:T(8,128)(2,1)S(1)}, u32[]{:S(2)}, u32[]{:S(2)}) collective-permute-start(bf16[2,256,128]{2,1,0:T(8,128)(2,1)S(1)} %constant_dynamic-slice_fusion.4), channel_id=1, source_target_pairs={{0,24},{4,28},{8,0},{12,4},{16,8},{20,12},{24,16},{28,20},{32,56},... | collective-permute-start | bytes 393224 | tf_op jit(solution)/shard_map/ppermute | solution.py:26
  4.5 10.8 %collective-permute-start.1 = (bf16[2,256,128]{2,1,0:T(8,128)(2,1)S(1)}, bf16[2,256,128]{2,1,0:T(8,128)(2,1)S(1)}, u32[]{:S(2)}, u32[]{:S(2)}) collective-permute-start(bf16[2,256,128]{2,1,0:T(8,128)(2,1)S(1)} %constant_dynamic-slice_fusion.4), channel_id=1, source_target_pairs={{0,16},{4,20},{8,24},{12,28},{16,0},{20,4},{24,8},{28,12},{32,48},... | collective-permute-start | bytes 393224 | tf_op jit(solution)/shard_map/ppermute | solution.py:26
  5.3 10.0 %collective-permute-start = (bf16[2,256,128]{2,1,0:T(8,128)(2,1)S(1)}, bf16[2,256,128]{2,1,0:T(8,128)(2,1)S(1)}, u32[]{:S(2)}, u32[]{:S(2)}) collective-permute-start(bf16[2,256,128]{2,1,0:T(8,128)(2,1)S(1)} %constant_dynamic-slice_fusion.4), channel_id=1, source_target_pairs={{0,8},{4,12},{8,16},{12,20},{16,24},{20,28},{24,0},{28,4},{32,40},... | collective-permute-start | bytes 393224 | tf_op jit(solution)/shard_map/ppermute | solution.py:26
  7.9 7.4 %collective-permute-start.8 = (bf16[256,256]{1,0:T(8,128)(2,1)S(1)}, bf16[256,256]{1,0:T(8,128)(2,1)S(1)}, u32[]{:S(2)}, u32[]{:S(2)}) collective-permute-start(bf16[256,256]{1,0:T(8,128)(2,1)S(1)} %get-tuple-element.59), channel_id=1, source_target_pairs={{0,24},{4,28},{8,0},{12,4},{16,8},{20,12},{24,16},{28,20},{32,56},... | collective-permute-start | bytes 393224 | tf_op jit(solution)/shard_map/ppermute | solution.py:26
  10.3 7.7 %collective-permute-start.6 = (bf16[256,256]{1,0:T(8,128)(2,1)S(1)}, bf16[256,256]{1,0:T(8,128)(2,1)S(1)}, u32[]{:S(2)}, u32[]{:S(2)}) collective-permute-start(bf16[256,256]{1,0:T(8,128)(2,1)S(1)} %get-tuple-element.60), channel_id=1, source_target_pairs={{0,8},{4,12},{8,16},{12,20},{16,24},{20,28},{24,0},{28,4},{32,40},... | collective-permute-start | bytes 393224 | tf_op jit(solution)/shard_map/ppermute | solution.py:26
  10.6 8.8 %collective-permute-start.7 = (bf16[256,256]{1,0:T(8,128)(2,1)S(1)}, bf16[256,256]{1,0:T(8,128)(2,1)S(1)}, u32[]{:S(2)}, u32[]{:S(2)}) collective-permute-start(bf16[256,256]{1,0:T(8,128)(2,1)S(1)} %get-tuple-element.62), channel_id=1, source_target_pairs={{0,16},{4,20},{8,24},{12,28},{16,0},{20,4},{24,8},{28,12},{32,48},... | collective-permute-start | bytes 393224 | tf_op jit(solution)/shard_map/ppermute | solution.py:26
  20.0 35.2 %all-to-all-start = ((bf16[16,2,256,128]{3,2,1,0:T(8,128)(2,1)}), bf16[16,2,256,128]{3,2,1,0:T(8,128)(2,1)S(1)}, u32[]{:S(2)}, u32[]{:S(2)}) async-start(bf16[16,2,256,128]{3,2,1,0:T(8,128)(2,1)} %get-tuple-element.31), calls=%async_computation | async-start | bytes 4194304 | tf_op jit(solution)/shard_map/all_to_all | solution.py:200
  25.4 19.2 %collective-permute-start.5 = (bf16[3,2,256,128]{3,2,1,0:T(8,128)(2,1)S(1)}, bf16[3,2,256,128]{3,2,1,0:T(8,128)(2,1)S(1)}, u32[]{:S(2)}, u32[]{:S(2)}) collective-permute-start(bf16[3,2,256,128]{3,2,1,0:T(8,128)(2,1)S(1)} %pad_maximum_fusion.refs_1_.refs_4_), channel_id=1, source_target_pairs={{0,3},{1,0},{2,1},{3,2},{4,7},{5,4},{6,5},{7,6},{8,11},{9,8},{10,9... | collective-permute-start | bytes 1179656 | tf_op jit(solution)/shard_map/ppermute | solution.py:34
  29.5 15.1 %collective-permute-start.4 = (bf16[3,2,256,128]{3,2,1,0:T(8,128)(2,1)S(1)}, bf16[3,2,256,128]{3,2,1,0:T(8,128)(2,1)S(1)}, u32[]{:S(2)}, u32[]{:S(2)}) collective-permute-start(bf16[3,2,256,128]{3,2,1,0:T(8,128)(2,1)S(1)} %pad_maximum_fusion.refs_1_.refs_4_), channel_id=1, source_target_pairs={{0,2},{1,3},{2,0},{3,1},{4,6},{5,7},{6,4},{7,5},{8,10},{9,11},{10,... | collective-permute-start | bytes 1179656 | tf_op jit(solution)/shard_map/ppermute | solution.py:34
  29.5 18.6 %collective-permute-start.3 = (bf16[3,2,256,128]{3,2,1,0:T(8,128)(2,1)S(1)}, bf16[3,2,256,128]{3,2,1,0:T(8,128)(2,1)}, u32[]{:S(2)}, u32[]{:S(2)}) collective-permute-start(bf16[3,2,256,128]{3,2,1,0:T(8,128)(2,1)S(1)} %pad_maximum_fusion.refs_1_.refs_4_), channel_id=1, source_target_pairs={{0,1},{1,2},{2,3},{3,0},{4,5},{5,6},{6,7},{7,4},{8,9},{9,10},{10,1... | collective-permute-start | bytes 1179656 | tf_op jit(solution)/shard_map/ppermute | solution.py:34
  63.3 7.1 %collective-permute-start.10 = (bf16[16,2,256,128]{3,2,1,0:T(8,128)(2,1)S(1)}, bf16[16,2,256,128]{3,2,1,0:T(8,128)(2,1)}, u32[]{:S(2)}, u32[]{:S(2)}) collective-permute-start(bf16[16,2,256,128]{3,2,1,0:T(8,128)(2,1)S(1)} %all-to-all-done.refs_3_.refs_8_), channel_id=1, source_target_pairs={{0,4},{4,0},{8,12},{12,8},{16,20},{20,16},{24,28},{28,24},{32,36},... | collective-permute-start | bytes 6291464 | tf_op jit(solution)/shard_map/ppermute | solution.py:30
  63.5 41.6 %all-to-all-start.1 = ((bf16[16,2,256,128]{3,2,1,0:T(8,128)(2,1)}), bf16[16,2,256,128]{3,2,1,0:T(8,128)(2,1)}, u32[]{:S(2)}, u32[]{:S(2)}) async-start(bf16[16,2,256,128]{3,2,1,0:T(8,128)(2,1)} %add_convert_fusion), calls=%async_computation.1 | async-start | bytes 4194304 | tf_op jit(solution)/shard_map/all_to_all | solution.py:200
  78.8 29.8 %collective-permute-start.18 = (bf16[8,8,32,128]{3,2,1,0:T(8,128)(2,1)}, bf16[8,8,32,128]{3,2,1,0:T(8,128)(2,1)S(1)}, u32[]{:S(2)}, u32[]{:S(2)}) collective-permute-start(bf16[8,8,32,128]{3,2,1,0:T(8,128)(2,1)} %get-tuple-element.52), channel_id=1, source_target_pairs={{0,2},{1,3},{2,0},{3,1},{4,6},{5,7},{6,4},{7,5},{8,10},{9,11},{10,... | collective-permute-start | bytes 1572872 | tf_op jit(solution)/shard_map/ppermute | solution.py:34
  79.5 31.7 %collective-permute-start.19 = (bf16[8,8,32,128]{3,2,1,0:T(8,128)(2,1)}, bf16[8,8,32,128]{3,2,1,0:T(8,128)(2,1)S(1)}, u32[]{:S(2)}, u32[]{:S(2)}) collective-permute-start(bf16[8,8,32,128]{3,2,1,0:T(8,128)(2,1)} %get-tuple-element.53), channel_id=1, source_target_pairs={{0,3},{1,0},{2,1},{3,2},{4,7},{5,4},{6,5},{7,6},{8,11},{9,8},{10,9... | collective-permute-start | bytes 1572872 | tf_op jit(solution)/shard_map/ppermute | solution.py:34
  80.7 31.5 %collective-permute-start.17 = (bf16[8,8,32,128]{3,2,1,0:T(8,128)(2,1)}, bf16[8,8,32,128]{3,2,1,0:T(8,128)(2,1)S(1)}, u32[]{:S(2)}, u32[]{:S(2)}) collective-permute-start(bf16[8,8,32,128]{3,2,1,0:T(8,128)(2,1)} %get-tuple-element.36), channel_id=1, source_target_pairs={{0,1},{1,2},{2,3},{3,0},{4,5},{5,6},{6,7},{7,4},{8,9},{9,10},{10,1... | collective-permute-start | bytes 1572872 | tf_op jit(solution)/shard_map/ppermute | solution.py:34
  88.0 20.6 %collective-permute-start.11 = (bf16[256,256]{1,0:T(8,128)(2,1)}, bf16[256,256]{1,0:T(8,128)(2,1)S(1)}, u32[]{:S(2)}, u32[]{:S(2)}) collective-permute-start(bf16[256,256]{1,0:T(8,128)(2,1)} %get-tuple-element.39), channel_id=1, source_target_pairs={{0,24},{4,28},{8,0},{12,4},{16,8},{20,12},{24,16},{28,20},{32,56},... | collective-permute-start | bytes 393224 | tf_op jit(solution)/shard_map/ppermute | solution.py:26
  91.1 27.7 %collective-permute-start.13 = (bf16[256,256]{1,0:T(8,128)(2,1)}, bf16[256,256]{1,0:T(8,128)(2,1)S(1)}, u32[]{:S(2)}, u32[]{:S(2)}) collective-permute-start(bf16[256,256]{1,0:T(8,128)(2,1)} %get-tuple-element.42), channel_id=1, source_target_pairs={{0,8},{4,12},{8,16},{12,20},{16,24},{20,28},{24,0},{28,4},{32,40},... | collective-permute-start | bytes 393224 | tf_op jit(solution)/shard_map/ppermute | solution.py:26
  108.5 5.4 %collective-permute-start.14 = (f32[2,32,128]{2,1,0:T(8,128)}, f32[2,32,128]{2,1,0:T(8,128)S(1)}, u32[]{:S(2)}, u32[]{:S(2)}) collective-permute-start(f32[2,32,128]{2,1,0:T(8,128)} %get-tuple-element.48), channel_id=1, source_target_pairs={{0,1},{1,2},{2,3},{3,0},{4,5},{5,6},{6,7},{7,4},{8,9},{9,10},{10,1... | collective-permute-start | bytes 98312 | tf_op jit(solution)/shard_map/ppermute | solution.py:34
  108.6 5.7 %collective-permute-start.15 = (f32[2,32,128]{2,1,0:T(8,128)}, f32[2,32,128]{2,1,0:T(8,128)S(1)}, u32[]{:S(2)}, u32[]{:S(2)}) collective-permute-start(f32[2,32,128]{2,1,0:T(8,128)} %get-tuple-element.49), channel_id=1, source_target_pairs={{0,2},{1,3},{2,0},{3,1},{4,6},{5,7},{6,4},{7,5},{8,10},{9,11},{10,... | collective-permute-start | bytes 98312 | tf_op jit(solution)/shard_map/ppermute | solution.py:34
  111.1 4.8 %collective-permute-start.16 = (f32[2,32,128]{2,1,0:T(8,128)}, f32[2,32,128]{2,1,0:T(8,128)S(1)}, u32[]{:S(2)}, u32[]{:S(2)}) collective-permute-start(f32[2,32,128]{2,1,0:T(8,128)} %get-tuple-element.50), channel_id=1, source_target_pairs={{0,3},{1,0},{2,1},{3,2},{4,7},{5,4},{6,5},{7,6},{8,11},{9,8},{10,9... | collective-permute-start | bytes 98312 | tf_op jit(solution)/shard_map/ppermute | solution.py:34
  112.2 8.0 %collective-permute-start.12 = (bf16[256,256]{1,0:T(8,128)(2,1)S(1)}, bf16[256,256]{1,0:T(8,128)(2,1)S(1)}, u32[]{:S(2)}, u32[]{:S(2)}) collective-permute-start(bf16[256,256]{1,0:T(8,128)(2,1)S(1)} %copy-done.14), channel_id=1, source_target_pairs={{0,16},{4,20},{8,24},{12,28},{16,0},{20,4},{24,8},{28,12},{32,48},... | collective-permute-start | bytes 393224 | tf_op jit(solution)/shard_map/ppermute | solution.py:26
  113.9 8.8 %collective-permute-start.20 = (bf16[2,8,32,128]{3,2,1,0:T(8,128)(2,1)S(1)}, bf16[2,8,32,128]{3,2,1,0:T(8,128)(2,1)S(1)}, u32[]{:S(2)}, u32[]{:S(2)}) collective-permute-start(bf16[2,8,32,128]{3,2,1,0:T(8,128)(2,1)S(1)} %get-tuple-element.56), channel_id=1, source_target_pairs={{0,24},{4,28},{8,0},{12,4},{16,8},{20,12},{24,16},{28,20},{32,56},... | collective-permute-start | bytes 393224 | tf_op jit(solution)/shard_map/ppermute | solution.py:26
  114.3 8.4 %collective-permute-start.22 = (bf16[2,8,32,128]{3,2,1,0:T(8,128)(2,1)S(1)}, bf16[2,8,32,128]{3,2,1,0:T(8,128)(2,1)S(1)}, u32[]{:S(2)}, u32[]{:S(2)}) collective-permute-start(bf16[2,8,32,128]{3,2,1,0:T(8,128)(2,1)S(1)} %get-tuple-element.57), channel_id=1, source_target_pairs={{0,8},{4,12},{8,16},{12,20},{16,24},{20,28},{24,0},{28,4},{32,40},... | collective-permute-start | bytes 393224 | tf_op jit(solution)/shard_map/ppermute | solution.py:26
  116.0 7.3 %collective-permute-start.21 = (bf16[2,8,32,128]{3,2,1,0:T(8,128)(2,1)S(1)}, bf16[2,8,32,128]{3,2,1,0:T(8,128)(2,1)S(1)}, u32[]{:S(2)}, u32[]{:S(2)}) collective-permute-start(bf16[2,8,32,128]{3,2,1,0:T(8,128)(2,1)S(1)} %get-tuple-element.58), channel_id=1, source_target_pairs={{0,16},{4,20},{8,24},{12,28},{16,0},{20,4},{24,8},{28,12},{32,48},... | collective-permute-start | bytes 393224 | tf_op jit(solution)/shard_map/ppermute | solution.py:26
  (16 other events, 124.0 us)

commit v4 on v3

--- a/solution.py
+++ b/solution.py
@@ -99,13 +99,13 @@
     w_own, w0, w1, w2, w3, g0, g1, g2, g3 = refs[11:20]
     acc, sems = refs[20:]
     copies = [pltpu.make_async_copy(refs[n], refs[11 + n], sems.at[n]) for n in range(9)]
-    for copy in copies:
-        copy.start()
+    for n in (0, 5, 1, 2, 3, 4, 6, 7, 8):
+        copies[n].start()
     y, x, c, z = pos[0], pos[1], pos[2], pos[3]
     acc[...] = jnp.zeros_like(acc)
-    for copy in copies:
-        copy.wait()
     for s, g in enumerate((g0, g1, g2, g3)):
+        for n in ((0, 5), (1, 2, 3, 4, 6), (7,), (8,))[s]:
+            copies[n].wait()
         for p in range(2):
             block = ((y * 4 + ((x - s) & 3)) * 2 + c) * 2 + p
             grad = g[:, p * 128 : (p + 1) * 128]
@@ -265,7 +265,10 @@
         [abuf, cat, pltpu.SemaphoreType.DMA((2,))],
         (8, 9),
     )
-    sums, *_ = lax.optimization_barrier((sums, *layer))
+    rows = [layer[0], shift_x(layer[1], -1), None, shift_x(layer[3], -3)]
+    layer2, _ = lax.optimization_barrier((layer[2], rows[1]))
+    rows[2] = shift_x(layer2, -2)
+    sums, *_ = lax.optimization_barrier((sums, layer[2], rows[1], rows[3], layer2))
     outs = call(
         last_body,
         [sds((1024, 256), BF)] + [sds((2, 32, 128), F32)] * 4,
@@ -284,9 +287,6 @@
     for part in [shift_x(summed[2 * s : 2 * s + 2].astype(BF), -s) for s in (1, 2, 3)]:
         grad_second = grad_second + part.astype(F32)
 
-    rows = [layer[0], shift_x(layer[1], -1), None, shift_x(layer[3], -3)]
-    layer2, _ = lax.optimization_barrier((layer[2], rows[1]))
-    rows[2] = shift_x(layer2, -2)
     (layer_out,) = call(join_body, [sds((1024, 256), BF)], [pos, *rows], 0, 1_000_000)
     return (layer_out, grad_tokens, grad_first, grad_second)
 

time: 125 us -> 123 us (0.984)
  waiting for transfers between devices: 41.4 us -> 39 us
    all_to_all x2, waiting for transfers between devices: 14 us -> 0.72 us  [exchange(): lax.all_to_all(value, 'blk', 0, 0, axis_index_groups=groups, tiled=True)]
    ppermute x12, waiting for transfers between devices: 6.11 us -> 18.7 us  [shift_x(): return lax.ppermute(value, 'blk', along(0, step, 0))]
    ppermute x9, waiting for transfers between devices: 17 us -> 15.3 us  [shift_z(): return lax.ppermute(value, 'tok', [(z, (z + step) % NZ) for z in range(NZ)])]
    unnamed x32 -> x30, local copies, waits for them, and re-layouts: 2.71 us -> 2.74 us
  transfers between devices with their start and end apart: 25 -> 25, of which waited for: 11 -> 9; matrix products, arithmetic and copies ran while one was open for 4% -> 4% of each run, Pallas kernels for 25% -> 25%
where the time goes in v4:
time: 123 us
  starting transfers between devices  40.5 us (33%)
  waiting for transfers between devices  39 us (32%)
  Pallas kernels  30.7 us (25%)
  other arithmetic  6.1 us (5%)
  local copies, waits for them, and re-layouts  5.47 us (4%)
    pallas_call x5, Pallas kernels, call(): pl.pallas_call(lambda *refs: body(*refs), grid=(1,), out_shape=outs, in_s...  23.7 us
    ppermute x12, waiting for transfers between devices, shift_x(): return lax.ppermute(value, 'blk', along(0, step, 0))  18.7 us
    ppermute x12, starting transfers between devices, shift_x(): return lax.ppermute(value, 'blk', along(0, step, 0))  16.3 us
    ppermute x9, waiting for transfers between devices, shift_z(): return lax.ppermute(value, 'tok', [(z, (z + step) % NZ) for z in range(NZ)])  15.3 us
    all_to_all x2, starting transfers between devices, exchange(): lax.all_to_all(value, 'blk', 0, 0, axis_index_groups=groups, tiled=True)  12.4 us
    ppermute x9, starting transfers between devices, shift_z(): return lax.ppermute(value, 'tok', [(z, (z + step) % NZ) for z in range(NZ)])  11.7 us
    pallas_call x1, Pallas kernels, shards(): pl.pallas_call(back_body, out_shape=[sds(whole, BF)] * 2, in_specs=[pl.Bl...  6.98 us
    ppermute x2, waiting for transfers between devices, swap_core(): return lax.ppermute(value, 'blk', along(0, 0, 1))  4.36 us
  transfers between devices with their start and end apart: 25, of which 9 were waited for; matrix products, arithmetic and copies ran while one was open for 4% of the time, Pallas kernels for 25%

profile of v4, /device:TPU:0, one launch (start us, length us, event | category | flops | bytes accessed | tf_op | source)
XLA Modules:
  0.0 122.7 jit_solution(12537048063763261916)
XLA Ops:
  1.6 2.9 %collective-permute-start.2 = (bf16[2,256,128]{2,1,0:T(8,128)(2,1)S(1)}, bf16[2,256,128]{2,1,0:T(8,128)(2,1)S(1)}, u32[]{:S(2)}, u32[]{:S(2)}) collective-permute-start(bf16[2,256,128]{2,1,0:T(8,128)(2,1)S(1)} %constant_dynamic-slice_fusion.4), channel_id=1, source_target_pairs={{0,24},{4,28},{8,0},{12,4},{16,8},{20,12},{24,16},{28,20},{32,56},... | collective-permute-start | bytes 393224 | tf_op jit(solution)/shard_map/ppermute | solution.py:26
  6.2 1.8 %constant_dynamic-slice_fusion = (bf16[256,256]{1,0:T(8,128)(2,1)S(1)}, bf16[256,256]{1,0:T(8,128)(2,1)S(1)}, bf16[256,256]{1,0:T(8,128)(2,1)}, bf16[256,256]{1,0:T(8,128)(2,1)S(1)}) fusion(bf16[1024,256]{1,0:T(8,128)(2,1)} %param.11, s32[]{:T(128)S(6)} %select_n.64, s32[]{:T(128)S(6)} %select_n.60, s32[]{:T(128)S(6)} %select_n.58, s32[]{:T(128)S(6)} %select_n.62), kind=kLoop, calls=%fused_computation.7 | loop fusion | bytes 1048592 | tf_op jit(solution)/shard_map/dynamic_slice | solution.py:214
  7.9 2.4 %collective-permute-start.8 = (bf16[256,256]{1,0:T(8,128)(2,1)S(1)}, bf16[256,256]{1,0:T(8,128)(2,1)S(1)}, u32[]{:S(2)}, u32[]{:S(2)}) collective-permute-start(bf16[256,256]{1,0:T(8,128)(2,1)S(1)} %get-tuple-element.59), channel_id=1, source_target_pairs={{0,24},{4,28},{8,0},{12,4},{16,8},{20,12},{24,16},{28,20},{32,56},... | collective-permute-start | bytes 393224 | tf_op jit(solution)/shard_map/ppermute | solution.py:26
  11.8 3.5 %shard_map.94 = (bf16[16,2,256,128]{3,2,1,0:T(8,128)(2,1)}, f32[4,2,256,128]{3,2,1,0:T(8,128)}) custom-call(bf16[1024,256]{1,0:T(8,128)(2,1)} %refs_1_.5, bf16[2,128,128]{2,1,0:T(8,128)(2,1)} %refs_2_.3), custom_call_target="tpu_custom_call" | custom-call | flops 134000000 | bytes 3500000 | tf_op jit(solution)/shard_map/pallas_call | solution.py:54
  15.4 2.6 %collective-permute-done.6.refs_6_ = bf16[256,256]{1,0:T(8,128)(2,1)S(1)} collective-permute-done((bf16[256,256]{1,0:T(8,128)(2,1)S(1)}, bf16[256,256]{1,0:T(8,128)(2,1)S(1)}, u32[]{:S(2)}, u32[]{:S(2)}) %collective-permute-start.6) | collective-permute-done | bytes 131104 | tf_op jit(solution)/shard_map/ppermute | solution.py:26
  18.0 1.4 %collective-permute-done.7.refs_7_ = bf16[256,256]{1,0:T(8,128)(2,1)S(1)} collective-permute-done((bf16[256,256]{1,0:T(8,128)(2,1)S(1)}, bf16[256,256]{1,0:T(8,128)(2,1)S(1)}, u32[]{:S(2)}, u32[]{:S(2)}) %collective-permute-start.7) | collective-permute-done | bytes 131104 | tf_op jit(solution)/shard_map/ppermute | solution.py:26
  20.0 5.4 %all-to-all-start = ((bf16[16,2,256,128]{3,2,1,0:T(8,128)(2,1)}), bf16[16,2,256,128]{3,2,1,0:T(8,128)(2,1)S(1)}, u32[]{:S(2)}, u32[]{:S(2)}) async-start(bf16[16,2,256,128]{3,2,1,0:T(8,128)(2,1)} %get-tuple-element.31), calls=%async_computation | async-start | bytes 4194304 | tf_op jit(solution)/shard_map/all_to_all | solution.py:200
  25.4 4.1 %collective-permute-start.5 = (bf16[3,2,256,128]{3,2,1,0:T(8,128)(2,1)S(1)}, bf16[3,2,256,128]{3,2,1,0:T(8,128)(2,1)S(1)}, u32[]{:S(2)}, u32[]{:S(2)}) collective-permute-start(bf16[3,2,256,128]{3,2,1,0:T(8,128)(2,1)S(1)} %pad_maximum_fusion.refs_1_.refs_4_), channel_id=1, source_target_pairs={{0,3},{1,0},{2,1},{3,2},{4,7},{5,4},{6,5},{7,6},{8,11},{9,8},{10,9... | collective-permute-start | bytes 1179656 | tf_op jit(solution)/shard_map/ppermute | solution.py:34
  29.6 1.3 %collective-permute-start.3 = (bf16[3,2,256,128]{3,2,1,0:T(8,128)(2,1)S(1)}, bf16[3,2,256,128]{3,2,1,0:T(8,128)(2,1)}, u32[]{:S(2)}, u32[]{:S(2)}) collective-permute-start(bf16[3,2,256,128]{3,2,1,0:T(8,128)(2,1)S(1)} %pad_maximum_fusion.refs_1_.refs_4_), channel_id=1, source_target_pairs={{0,1},{1,2},{2,3},{3,0},{4,5},{5,6},{6,7},{7,4},{8,9},{9,10},{10,1... | collective-permute-start | bytes 1179656 | tf_op jit(solution)/shard_map/ppermute | solution.py:34
  32.9 11.8 %collective-permute-done.5.refs_4_.refs_7_ = bf16[3,2,256,128]{3,2,1,0:T(8,128)(2,1)S(1)} collective-permute-done((bf16[3,2,256,128]{3,2,1,0:T(8,128)(2,1)S(1)}, bf16[3,2,256,128]{3,2,1,0:T(8,128)(2,1)S(1)}, u32[]{:S(2)}, u32[]{:S(2)}) %collective-permute-start.5) | collective-permute-done | bytes 393248 | tf_op jit(solution)/shard_map/ppermute | solution.py:34
  44.7 3.5 %collective-permute-done.3.refs_2_.refs_5_ = bf16[3,2,256,128]{3,2,1,0:T(8,128)(2,1)} collective-permute-done((bf16[3,2,256,128]{3,2,1,0:T(8,128)(2,1)S(1)}, bf16[3,2,256,128]{3,2,1,0:T(8,128)(2,1)}, u32[]{:S(2)}, u32[]{:S(2)}) %collective-permute-start.3) | collective-permute-done | bytes 393248 | tf_op jit(solution)/shard_map/ppermute | solution.py:34
  48.2 7.0 %shard_map.93 = (bf16[16,2,256,128]{3,2,1,0:T(8,128)(2,1)}, bf16[16,2,256,128]{3,2,1,0:T(8,128)(2,1)}) custom-call(s32[4]{0:T(128)} %pad_add_fusion.pos.refs_0_, s32[64,8]{1,0:T(8,128)} %copy.14.src.refs_1_, s32[64,8]{1,0:T(8,128)} %copy.15.live.refs_2_, bf16[2,1024,128]{2,1,0:T(8,128)(2,1)} %bitcast.9, bf16[3,2,256,128]{3,2,1,0:T(8,128)(2,1)} %copy-done.1, ...), custom_call_target="tpu_custom_call" | custom-call | flops 1080000000 | bytes 9000000 | tf_op jit(solution)/shard_map/pallas_call | solution.py:229
  55.3 4.4 %collective-permute-done.9 = bf16[16,2,256,128]{3,2,1,0:T(8,128)(2,1)S(1)} collective-permute-done((bf16[16,2,256,128]{3,2,1,0:T(8,128)(2,1)}, bf16[16,2,256,128]{3,2,1,0:T(8,128)(2,1)S(1)}, u32[]{:S(2)}, u32[]{:S(2)}) %collective-permute-start.9) | collective-permute-done | bytes 2097184 | tf_op jit(solution)/shard_map/ppermute | solution.py:30
  59.6 3.7 %add_convert_fusion = bf16[16,2,256,128]{3,2,1,0:T(8,128)(2,1)} fusion(bf16[16,2,256,128]{3,2,1,0:T(8,128)(2,1)S(1)} %collective-permute-done.9, bf16[16,2,256,128]{3,2,1,0:T(8,128)(2,1)} %get-tuple-element.33), kind=kLoop, calls=%fused_computation | loop fusion | flops 4194304 | bytes 6291456 | tf_op jit(solution)/shard_map/convert_element_type | solution.py:240
  63.5 6.9 %all-to-all-start.1 = ((bf16[16,2,256,128]{3,2,1,0:T(8,128)(2,1)}), bf16[16,2,256,128]{3,2,1,0:T(8,128)(2,1)}, u32[]{:S(2)}, u32[]{:S(2)}) async-start(bf16[16,2,256,128]{3,2,1,0:T(8,128)(2,1)} %add_convert_fusion), calls=%async_computation.1 | async-start | bytes 4194304 | tf_op jit(solution)/shard_map/all_to_all | solution.py:200
  70.4 8.4 %shard_map.95 = (f32[8,8,32,128]{3,2,1,0:T(8,128)}, bf16[8,8,32,128]{3,2,1,0:T(8,128)(2,1)}, bf16[8,8,32,128]{3,2,1,0:T(8,128)(2,1)}, bf16[8,8,32,128]{3,2,1,0:T(8,128)(2,1)}) custom-call(s32[4]{0:T(128)} %pad_add_fusion.pos.refs_0_, s32[64,8]{1,0:T(8,128)} %copy.14.src.refs_1_, s32[64,8]{1,0:T(8,128)} %copy.15.live.refs_2_, ...), custom_call_target="tpu_custom_call" | custom-call | flops 1080000000 | bytes 12000000 | tf_op jit(solution)/shard_map/pallas_call | solution.py:54
  81.5 6.4 %shard_map.96 = (bf16[256,256]{1,0:T(8,128)(2,1)}, bf16[256,256]{1,0:T(8,128)(2,1)}, bf16[256,256]{1,0:T(8,128)(2,1)}, bf16[256,256]{1,0:T(8,128)(2,1)}) custom-call(s32[4]{0:T(128)} %pad_add_fusion.pos.refs_0_, s32[64,8]{1,0:T(8,128)} %copy.14.src.refs_1_, s32[64,8]{1,0:T(8,128)} %copy.15.live.refs_2_, bf16[2,1024,128]{2,1,0:T(8,128)(2,1)} %bitcast.10, ...), custom_call_target="tpu_custom_call" | custom-call | flops 1080000000 | bytes 9000000 | tf_op jit(solution)/shard_map/pallas_call | solution.py:54
  88.0 3.1 %collective-permute-start.11 = (bf16[256,256]{1,0:T(8,128)(2,1)}, bf16[256,256]{1,0:T(8,128)(2,1)S(1)}, u32[]{:S(2)}, u32[]{:S(2)}) collective-permute-start(bf16[256,256]{1,0:T(8,128)(2,1)} %get-tuple-element.39), channel_id=1, source_target_pairs={{0,24},{4,28},{8,0},{12,4},{16,8},{20,12},{24,16},{28,20},{32,56},... | collective-permute-start | bytes 393224 | tf_op jit(solution)/shard_map/ppermute | solution.py:26
  91.1 13.3 %collective-permute-done.11.refs_2_ = bf16[256,256]{1,0:T(8,128)(2,1)S(1)} collective-permute-done((bf16[256,256]{1,0:T(8,128)(2,1)}, bf16[256,256]{1,0:T(8,128)(2,1)S(1)}, u32[]{:S(2)}, u32[]{:S(2)}) %collective-permute-start.11) | collective-permute-done | bytes 131104 | tf_op jit(solution)/shard_map/ppermute | solution.py:26
  105.1 3.5 %shard_map.98 = (bf16[1024,256]{1,0:T(8,128)(2,1)}, f32[2,32,128]{2,1,0:T(8,128)}, f32[2,32,128]{2,1,0:T(8,128)}, f32[2,32,128]{2,1,0:T(8,128)}, f32[2,32,128]{2,1,0:T(8,128)}) custom-call(s32[4]{0:T(128)} %pad_add_fusion.pos.refs_0_, bf16[1024,256]{1,0:T(8,128)(2,1)} %refs_1_.5, bf16[2,128,128]{2,1,0:T(8,128)(2,1)} %refs_2_.3, ...), custom_call_target="tpu_custom_call" | custom-call | flops 268000000 | bytes 3500000 | tf_op jit(solution)/shard_map/pallas_call | solution.py:54
  108.6 2.5 %collective-permute-start.15 = (f32[2,32,128]{2,1,0:T(8,128)}, f32[2,32,128]{2,1,0:T(8,128)S(1)}, u32[]{:S(2)}, u32[]{:S(2)}) collective-permute-start(f32[2,32,128]{2,1,0:T(8,128)} %get-tuple-element.49), channel_id=1, source_target_pairs={{0,2},{1,3},{2,0},{3,1},{4,6},{5,7},{6,4},{7,5},{8,10},{9,11},{10,... | collective-permute-start | bytes 98312 | tf_op jit(solution)/shard_map/ppermute | solution.py:34
  112.6 1.8 %collective-permute-start.20 = (bf16[2,8,32,128]{3,2,1,0:T(8,128)(2,1)S(1)}, bf16[2,8,32,128]{3,2,1,0:T(8,128)(2,1)S(1)}, u32[]{:S(2)}, u32[]{:S(2)}) collective-permute-start(bf16[2,8,32,128]{3,2,1,0:T(8,128)(2,1)S(1)} %get-tuple-element.56), channel_id=1, source_target_pairs={{0,24},{4,28},{8,0},{12,4},{16,8},{20,12},{24,16},{28,20},{32,56},... | collective-permute-start | bytes 393224 | tf_op jit(solution)/shard_map/ppermute | solution.py:26
  114.7 2.9 %collective-permute-start.21 = (bf16[2,8,32,128]{3,2,1,0:T(8,128)(2,1)S(1)}, bf16[2,8,32,128]{3,2,1,0:T(8,128)(2,1)S(1)}, u32[]{:S(2)}, u32[]{:S(2)}) collective-permute-start(bf16[2,8,32,128]{3,2,1,0:T(8,128)(2,1)S(1)} %get-tuple-element.58), channel_id=1, source_target_pairs={{0,16},{4,20},{8,24},{12,28},{16,0},{20,4},{24,8},{28,12},{32,48},... | collective-permute-start | bytes 393224 | tf_op jit(solution)/shard_map/ppermute | solution.py:26
  118.9 1.9 %shard_map.97 = bf16[1024,256]{1,0:T(8,128)(2,1)} custom-call(s32[4]{0:T(128)} %pad_add_fusion.pos.refs_0_, bf16[256,256]{1,0:T(8,128)(2,1)} %get-tuple-element.38.refs_1_, bf16[256,256]{1,0:T(8,128)(2,1)} %copy-done.8, bf16[256,256]{1,0:T(8,128)(2,1)} %copy-done.10, bf16[256,256]{1,0:T(8,128)(2,1)} %copy-done.9), custom_call_target="tpu_custom_call" | custom-call | bytes 1000000 | tf_op jit(solution)/shard_map/pallas_call | solution.py:54
  (71 shorter events, 15.5 us)
Async XLA Ops:
  1.6 9.0 %collective-permute-start.2 = (bf16[2,256,128]{2,1,0:T(8,128)(2,1)S(1)}, bf16[2,256,128]{2,1,0:T(8,128)(2,1)S(1)}, u32[]{:S(2)}, u32[]{:S(2)}) collective-permute-start(bf16[2,256,128]{2,1,0:T(8,128)(2,1)S(1)} %constant_dynamic-slice_fusion.4), channel_id=1, source_target_pairs={{0,24},{4,28},{8,0},{12,4},{16,8},{20,12},{24,16},{28,20},{32,56},... | collective-permute-start | bytes 393224 | tf_op jit(solution)/shard_map/ppermute | solution.py:26
  4.5 10.8 %collective-permute-start.1 = (bf16[2,256,128]{2,1,0:T(8,128)(2,1)S(1)}, bf16[2,256,128]{2,1,0:T(8,128)(2,1)S(1)}, u32[]{:S(2)}, u32[]{:S(2)}) collective-permute-start(bf16[2,256,128]{2,1,0:T(8,128)(2,1)S(1)} %constant_dynamic-slice_fusion.4), channel_id=1, source_target_pairs={{0,16},{4,20},{8,24},{12,28},{16,0},{20,4},{24,8},{28,12},{32,48},... | collective-permute-start | bytes 393224 | tf_op jit(solution)/shard_map/ppermute | solution.py:26
  5.3 10.0 %collective-permute-start = (bf16[2,256,128]{2,1,0:T(8,128)(2,1)S(1)}, bf16[2,256,128]{2,1,0:T(8,128)(2,1)S(1)}, u32[]{:S(2)}, u32[]{:S(2)}) collective-permute-start(bf16[2,256,128]{2,1,0:T(8,128)(2,1)S(1)} %constant_dynamic-slice_fusion.4), channel_id=1, source_target_pairs={{0,8},{4,12},{8,16},{12,20},{16,24},{20,28},{24,0},{28,4},{32,40},... | collective-permute-start | bytes 393224 | tf_op jit(solution)/shard_map/ppermute | solution.py:26
  7.9 7.4 %collective-permute-start.8 = (bf16[256,256]{1,0:T(8,128)(2,1)S(1)}, bf16[256,256]{1,0:T(8,128)(2,1)S(1)}, u32[]{:S(2)}, u32[]{:S(2)}) collective-permute-start(bf16[256,256]{1,0:T(8,128)(2,1)S(1)} %get-tuple-element.59), channel_id=1, source_target_pairs={{0,24},{4,28},{8,0},{12,4},{16,8},{20,12},{24,16},{28,20},{32,56},... | collective-permute-start | bytes 393224 | tf_op jit(solution)/shard_map/ppermute | solution.py:26
  10.3 7.7 %collective-permute-start.6 = (bf16[256,256]{1,0:T(8,128)(2,1)S(1)}, bf16[256,256]{1,0:T(8,128)(2,1)S(1)}, u32[]{:S(2)}, u32[]{:S(2)}) collective-permute-start(bf16[256,256]{1,0:T(8,128)(2,1)S(1)} %get-tuple-element.60), channel_id=1, source_target_pairs={{0,8},{4,12},{8,16},{12,20},{16,24},{20,28},{24,0},{28,4},{32,40},... | collective-permute-start | bytes 393224 | tf_op jit(solution)/shard_map/ppermute | solution.py:26
  10.6 8.8 %collective-permute-start.7 = (bf16[256,256]{1,0:T(8,128)(2,1)S(1)}, bf16[256,256]{1,0:T(8,128)(2,1)S(1)}, u32[]{:S(2)}, u32[]{:S(2)}) collective-permute-start(bf16[256,256]{1,0:T(8,128)(2,1)S(1)} %get-tuple-element.62), channel_id=1, source_target_pairs={{0,16},{4,20},{8,24},{12,28},{16,0},{20,4},{24,8},{28,12},{32,48},... | collective-permute-start | bytes 393224 | tf_op jit(solution)/shard_map/ppermute | solution.py:26
  20.0 35.2 %all-to-all-start = ((bf16[16,2,256,128]{3,2,1,0:T(8,128)(2,1)}), bf16[16,2,256,128]{3,2,1,0:T(8,128)(2,1)S(1)}, u32[]{:S(2)}, u32[]{:S(2)}) async-start(bf16[16,2,256,128]{3,2,1,0:T(8,128)(2,1)} %get-tuple-element.31), calls=%async_computation | async-start | bytes 4194304 | tf_op jit(solution)/shard_map/all_to_all | solution.py:200
  25.4 19.2 %collective-permute-start.5 = (bf16[3,2,256,128]{3,2,1,0:T(8,128)(2,1)S(1)}, bf16[3,2,256,128]{3,2,1,0:T(8,128)(2,1)S(1)}, u32[]{:S(2)}, u32[]{:S(2)}) collective-permute-start(bf16[3,2,256,128]{3,2,1,0:T(8,128)(2,1)S(1)} %pad_maximum_fusion.refs_1_.refs_4_), channel_id=1, source_target_pairs={{0,3},{1,0},{2,1},{3,2},{4,7},{5,4},{6,5},{7,6},{8,11},{9,8},{10,9... | collective-permute-start | bytes 1179656 | tf_op jit(solution)/shard_map/ppermute | solution.py:34
  29.5 15.1 %collective-permute-start.4 = (bf16[3,2,256,128]{3,2,1,0:T(8,128)(2,1)S(1)}, bf16[3,2,256,128]{3,2,1,0:T(8,128)(2,1)S(1)}, u32[]{:S(2)}, u32[]{:S(2)}) collective-permute-start(bf16[3,2,256,128]{3,2,1,0:T(8,128)(2,1)S(1)} %pad_maximum_fusion.refs_1_.refs_4_), channel_id=1, source_target_pairs={{0,2},{1,3},{2,0},{3,1},{4,6},{5,7},{6,4},{7,5},{8,10},{9,11},{10,... | collective-permute-start | bytes 1179656 | tf_op jit(solution)/shard_map/ppermute | solution.py:34
  29.6 18.6 %collective-permute-start.3 = (bf16[3,2,256,128]{3,2,1,0:T(8,128)(2,1)S(1)}, bf16[3,2,256,128]{3,2,1,0:T(8,128)(2,1)}, u32[]{:S(2)}, u32[]{:S(2)}) collective-permute-start(bf16[3,2,256,128]{3,2,1,0:T(8,128)(2,1)S(1)} %pad_maximum_fusion.refs_1_.refs_4_), channel_id=1, source_target_pairs={{0,1},{1,2},{2,3},{3,0},{4,5},{5,6},{6,7},{7,4},{8,9},{9,10},{10,1... | collective-permute-start | bytes 1179656 | tf_op jit(solution)/shard_map/ppermute | solution.py:34
  63.3 7.1 %collective-permute-start.10 = (bf16[16,2,256,128]{3,2,1,0:T(8,128)(2,1)S(1)}, bf16[16,2,256,128]{3,2,1,0:T(8,128)(2,1)}, u32[]{:S(2)}, u32[]{:S(2)}) collective-permute-start(bf16[16,2,256,128]{3,2,1,0:T(8,128)(2,1)S(1)} %all-to-all-done.refs_3_.refs_8_), channel_id=1, source_target_pairs={{0,4},{4,0},{8,12},{12,8},{16,20},{20,16},{24,28},{28,24},{32,36},... | collective-permute-start | bytes 6291464 | tf_op jit(solution)/shard_map/ppermute | solution.py:30
  63.5 41.6 %all-to-all-start.1 = ((bf16[16,2,256,128]{3,2,1,0:T(8,128)(2,1)}), bf16[16,2,256,128]{3,2,1,0:T(8,128)(2,1)}, u32[]{:S(2)}, u32[]{:S(2)}) async-start(bf16[16,2,256,128]{3,2,1,0:T(8,128)(2,1)} %add_convert_fusion), calls=%async_computation.1 | async-start | bytes 4194304 | tf_op jit(solution)/shard_map/all_to_all | solution.py:200
  78.8 29.8 %collective-permute-start.18 = (bf16[8,8,32,128]{3,2,1,0:T(8,128)(2,1)}, bf16[8,8,32,128]{3,2,1,0:T(8,128)(2,1)S(1)}, u32[]{:S(2)}, u32[]{:S(2)}) collective-permute-start(bf16[8,8,32,128]{3,2,1,0:T(8,128)(2,1)} %get-tuple-element.52), channel_id=1, source_target_pairs={{0,2},{1,3},{2,0},{3,1},{4,6},{5,7},{6,4},{7,5},{8,10},{9,11},{10,... | collective-permute-start | bytes 1572872 | tf_op jit(solution)/shard_map/ppermute | solution.py:34
  79.5 31.6 %collective-permute-start.19 = (bf16[8,8,32,128]{3,2,1,0:T(8,128)(2,1)}, bf16[8,8,32,128]{3,2,1,0:T(8,128)(2,1)S(1)}, u32[]{:S(2)}, u32[]{:S(2)}) collective-permute-start(bf16[8,8,32,128]{3,2,1,0:T(8,128)(2,1)} %get-tuple-element.53), channel_id=1, source_target_pairs={{0,3},{1,0},{2,1},{3,2},{4,7},{5,4},{6,5},{7,6},{8,11},{9,8},{10,9... | collective-permute-start | bytes 1572872 | tf_op jit(solution)/shard_map/ppermute | solution.py:34
  80.7 31.5 %collective-permute-start.17 = (bf16[8,8,32,128]{3,2,1,0:T(8,128)(2,1)}, bf16[8,8,32,128]{3,2,1,0:T(8,128)(2,1)S(1)}, u32[]{:S(2)}, u32[]{:S(2)}) collective-permute-start(bf16[8,8,32,128]{3,2,1,0:T(8,128)(2,1)} %get-tuple-element.36), channel_id=1, source_target_pairs={{0,1},{1,2},{2,3},{3,0},{4,5},{5,6},{6,7},{7,4},{8,9},{9,10},{10,1... | collective-permute-start | bytes 1572872 | tf_op jit(solution)/shard_map/ppermute | solution.py:34
  88.0 16.4 %collective-permute-start.11 = (bf16[256,256]{1,0:T(8,128)(2,1)}, bf16[256,256]{1,0:T(8,128)(2,1)S(1)}, u32[]{:S(2)}, u32[]{:S(2)}) collective-permute-start(bf16[256,256]{1,0:T(8,128)(2,1)} %get-tuple-element.39), channel_id=1, source_target_pairs={{0,24},{4,28},{8,0},{12,4},{16,8},{20,12},{24,16},{28,20},{32,56},... | collective-permute-start | bytes 393224 | tf_op jit(solution)/shard_map/ppermute | solution.py:26
  91.1 14.0 %collective-permute-start.13 = (bf16[256,256]{1,0:T(8,128)(2,1)}, bf16[256,256]{1,0:T(8,128)(2,1)S(1)}, u32[]{:S(2)}, u32[]{:S(2)}) collective-permute-start(bf16[256,256]{1,0:T(8,128)(2,1)} %get-tuple-element.42), channel_id=1, source_target_pairs={{0,8},{4,12},{8,16},{12,20},{16,24},{20,28},{24,0},{28,4},{32,40},... | collective-permute-start | bytes 393224 | tf_op jit(solution)/shard_map/ppermute | solution.py:26
  104.4 13.8 %collective-permute-start.12 = (bf16[256,256]{1,0:T(8,128)(2,1)}, bf16[256,256]{1,0:T(8,128)(2,1)S(1)}, u32[]{:S(2)}, u32[]{:S(2)}) collective-permute-start(bf16[256,256]{1,0:T(8,128)(2,1)} %get-tuple-element.41), channel_id=1, source_target_pairs={{0,16},{4,20},{8,24},{12,28},{16,0},{20,4},{24,8},{28,12},{32,48},... | collective-permute-start | bytes 393224 | tf_op jit(solution)/shard_map/ppermute | solution.py:26
  108.6 5.8 %collective-permute-start.14 = (f32[2,32,128]{2,1,0:T(8,128)}, f32[2,32,128]{2,1,0:T(8,128)S(1)}, u32[]{:S(2)}, u32[]{:S(2)}) collective-permute-start(f32[2,32,128]{2,1,0:T(8,128)} %get-tuple-element.48), channel_id=1, source_target_pairs={{0,1},{1,2},{2,3},{3,0},{4,5},{5,6},{6,7},{7,4},{8,9},{9,10},{10,1... | collective-permute-start | bytes 98312 | tf_op jit(solution)/shard_map/ppermute | solution.py:34
  108.6 6.1 %collective-permute-start.15 = (f32[2,32,128]{2,1,0:T(8,128)}, f32[2,32,128]{2,1,0:T(8,128)S(1)}, u32[]{:S(2)}, u32[]{:S(2)}) collective-permute-start(f32[2,32,128]{2,1,0:T(8,128)} %get-tuple-element.49), channel_id=1, source_target_pairs={{0,2},{1,3},{2,0},{3,1},{4,6},{5,7},{6,4},{7,5},{8,10},{9,11},{10,... | collective-permute-start | bytes 98312 | tf_op jit(solution)/shard_map/ppermute | solution.py:34
  111.1 6.5 %collective-permute-start.16 = (f32[2,32,128]{2,1,0:T(8,128)}, f32[2,32,128]{2,1,0:T(8,128)S(1)}, u32[]{:S(2)}, u32[]{:S(2)}) collective-permute-start(f32[2,32,128]{2,1,0:T(8,128)} %get-tuple-element.50), channel_id=1, source_target_pairs={{0,3},{1,0},{2,1},{3,2},{4,7},{5,4},{6,5},{7,6},{8,11},{9,8},{10,9... | collective-permute-start | bytes 98312 | tf_op jit(solution)/shard_map/ppermute | solution.py:34
  112.6 8.2 %collective-permute-start.20 = (bf16[2,8,32,128]{3,2,1,0:T(8,128)(2,1)S(1)}, bf16[2,8,32,128]{3,2,1,0:T(8,128)(2,1)S(1)}, u32[]{:S(2)}, u32[]{:S(2)}) collective-permute-start(bf16[2,8,32,128]{3,2,1,0:T(8,128)(2,1)S(1)} %get-tuple-element.56), channel_id=1, source_target_pairs={{0,24},{4,28},{8,0},{12,4},{16,8},{20,12},{24,16},{28,20},{32,56},... | collective-permute-start | bytes 393224 | tf_op jit(solution)/shard_map/ppermute | solution.py:26
  114.3 6.5 %collective-permute-start.22 = (bf16[2,8,32,128]{3,2,1,0:T(8,128)(2,1)S(1)}, bf16[2,8,32,128]{3,2,1,0:T(8,128)(2,1)S(1)}, u32[]{:S(2)}, u32[]{:S(2)}) collective-permute-start(bf16[2,8,32,128]{3,2,1,0:T(8,128)(2,1)S(1)} %get-tuple-element.57), channel_id=1, source_target_pairs={{0,8},{4,12},{8,16},{12,20},{16,24},{20,28},{24,0},{28,4},{32,40},... | collective-permute-start | bytes 393224 | tf_op jit(solution)/shard_map/ppermute | solution.py:26
  114.7 7.2 %collective-permute-start.21 = (bf16[2,8,32,128]{3,2,1,0:T(8,128)(2,1)S(1)}, bf16[2,8,32,128]{3,2,1,0:T(8,128)(2,1)S(1)}, u32[]{:S(2)}, u32[]{:S(2)}) collective-permute-start(bf16[2,8,32,128]{3,2,1,0:T(8,128)(2,1)S(1)} %get-tuple-element.58), channel_id=1, source_target_pairs={{0,16},{4,20},{8,24},{12,28},{16,0},{20,4},{24,8},{28,12},{32,48},... | collective-permute-start | bytes 393224 | tf_op jit(solution)/shard_map/ppermute | solution.py:26
  (15 other events, 109.4 us)

commit v5 on v4

--- a/solution.py
+++ b/solution.py
@@ -95,10 +95,10 @@
 
 
 def back_body(pos, src, live, *refs):
-    away, own = refs[9:11]
-    w_own, w0, w1, w2, w3, g0, g1, g2, g3 = refs[11:20]
-    acc, sems = refs[20:]
-    copies = [pltpu.make_async_copy(refs[n], refs[11 + n], sems.at[n]) for n in range(9)]
+    away, own = refs[9:11], refs[11:13]
+    w_own, w0, w1, w2, w3, g0, g1, g2, g3 = refs[13:22]
+    acc, sems = refs[22:]
+    copies = [pltpu.make_async_copy(refs[n], refs[13 + n], sems.at[n]) for n in range(9)]
     for n in (0, 5, 1, 2, 3, 4, 6, 7, 8):
         copies[n].start()
     y, x, c, z = pos[0], pos[1], pos[2], pos[3]
@@ -115,8 +115,8 @@
                 r = j >> 1
                 acc[((r & 1) ^ c) * 32 + (r >> 1) * 2 + (j & 1)] += dot(grad, ref[at], 1, 1) * scale
     for n in range(16):
-        away[n] = acc[32 + 2 * n : 34 + 2 * n].astype(BF)
-        own[n] = acc[2 * n : 2 * n + 2].astype(BF)
+        away[n // 8][n % 8] = acc[32 + 2 * n : 34 + 2 * n].astype(BF)
+        own[n // 8][n % 8] = acc[2 * n : 2 * n + 2].astype(BF)
 
 
 def load_acts(mine, other, abuf, sems):
@@ -226,18 +226,24 @@
     weights = [w_own, w0] + [shift_z(w0, t) for t in (1, 2, 3)]
 
     inputs = [*weights, *grads]
-    away, own = pl.pallas_call(
+    half = sds((8, 2, 256, 128), BF)
+    *away, own_low, own_high = pl.pallas_call(
         back_body,
-        out_shape=[sds(whole, BF)] * 2,
+        out_shape=[half] * 4,
         in_specs=[pl.BlockSpec(memory_space=pltpu.SMEM)] * 3 + [pl.BlockSpec(memory_space=pl.ANY)] * 9,
-        out_specs=[pl.BlockSpec(memory_space=pltpu.VMEM)] * 2,
+        out_specs=[pl.BlockSpec(memory_space=pltpu.VMEM)] * 4,
         scratch_shapes=[pltpu.VMEM(part.shape, BF) for part in inputs]
         + [pltpu.VMEM((64, 256, 128), F32), pltpu.SemaphoreType.DMA((9,))],
         compiler_params=pltpu.CompilerParams(vmem_limit_bytes=LIMIT),
         cost_estimate=pl.CostEstimate(flops=1_080_000_000, bytes_accessed=9_000_000, transcendentals=0),
     )(pos, tile_src, tile_live, *inputs)
-    away, mine = lax.optimization_barrier((away, mine))
-    parts = (own.astype(F32) + swap_core(away).astype(F32)).astype(BF)
+    *away, mine = lax.optimization_barrier((*away, mine))
+    parts = jnp.concatenate(
+        [
+            (own.astype(F32) + swap_core(part).astype(F32)).astype(BF)
+            for own, part in zip((own_low, own_high), away)
+        ]
+    )
     parts, mine_later = lax.optimization_barrier((parts, mine))
     sums = exchange(parts)
     other = swap_core(mine_later)

time: 123 us -> 122 us (level)
  waiting for transfers between devices: 39 us -> 37.1 us
    ppermute x2 -> x3, waiting for transfers between devices: 4.36 us -> 2.37 us  [swap_core(): return lax.ppermute(value, 'blk', along(0, 0, 1))]
    convert_element_type x1 -> x2, other arithmetic: 3.67 us -> 1.79 us  [shards(): (own.astype(F32) + swap_core(part).astype(F32)).astype(BF)]
    concatenate x0 -> x1, other arithmetic: none -> 1.53 us  [shards(): jnp.concatenate([(own.astype(F32) + swap_core(part).astype(F32)).astype(B...]
    unnamed x30 -> x32, local copies, waits for them, and re-layouts: 2.74 us -> 2.72 us
  transfers between devices with their start and end apart: 25 -> 26, of which waited for: 9 -> 9; matrix products, arithmetic and copies ran while one was open for 4% -> 5% of each run, Pallas kernels for 25% -> 25%
where the time goes in v5:
time: 122 us; the launch traced here: 121 us
  starting transfers between devices  41.2 us (34%)
  waiting for transfers between devices  37.1 us (30%)
  Pallas kernels  30.6 us (25%)
  other arithmetic  5.74 us (5%)
  local copies, waits for them, and re-layouts  5.46 us (4%)
    pallas_call x5, Pallas kernels, call(): pl.pallas_call(lambda *refs: body(*refs), grid=(1,), out_shape=outs, in_s...  23.7 us
    ppermute x12, waiting for transfers between devices, shift_x(): return lax.ppermute(value, 'blk', along(0, step, 0))  18.7 us
    ppermute x12, starting transfers between devices, shift_x(): return lax.ppermute(value, 'blk', along(0, step, 0))  15.9 us
    ppermute x9, waiting for transfers between devices, shift_z(): return lax.ppermute(value, 'tok', [(z, (z + step) % NZ) for z in range(NZ)])  15.3 us
    all_to_all x2, starting transfers between devices, exchange(): lax.all_to_all(value, 'blk', 0, 0, axis_index_groups=groups, tiled=True)  12.4 us
    ppermute x9, starting transfers between devices, shift_z(): return lax.ppermute(value, 'tok', [(z, (z + step) % NZ) for z in range(NZ)])  12.1 us
    pallas_call x1, Pallas kernels, shards(): pl.pallas_call(back_body, out_shape=[half] * 4, in_specs=[pl.BlockSpec(me...  6.87 us
    unnamed x32, local copies, waits for them, and re-layouts  2.72 us
  transfers between devices with their start and end apart: 26, of which 9 were waited for; matrix products, arithmetic and copies ran while one was open for 5% of the time, Pallas kernels for 25%

profile of v5, /device:TPU:0, one launch (start us, length us, event | category | flops | bytes accessed | tf_op | source)
XLA Modules:
  0.0 120.9 jit_solution(4151252654547864878)
XLA Ops:
  1.6 2.9 %collective-permute-start.2 = (bf16[2,256,128]{2,1,0:T(8,128)(2,1)S(1)}, bf16[2,256,128]{2,1,0:T(8,128)(2,1)S(1)}, u32[]{:S(2)}, u32[]{:S(2)}) collective-permute-start(bf16[2,256,128]{2,1,0:T(8,128)(2,1)S(1)} %constant_dynamic-slice_fusion.4), channel_id=1, source_target_pairs={{0,24},{4,28},{8,0},{12,4},{16,8},{20,12},{24,16},{28,20},{32,56},... | collective-permute-start | bytes 393224 | tf_op jit(solution)/shard_map/ppermute | solution.py:26
  6.2 1.8 %constant_dynamic-slice_fusion = (bf16[256,256]{1,0:T(8,128)(2,1)S(1)}, bf16[256,256]{1,0:T(8,128)(2,1)S(1)}, bf16[256,256]{1,0:T(8,128)(2,1)}, bf16[256,256]{1,0:T(8,128)(2,1)S(1)}) fusion(bf16[1024,256]{1,0:T(8,128)(2,1)} %param.11, s32[]{:T(128)S(6)} %select_n.64, s32[]{:T(128)S(6)} %select_n.60, s32[]{:T(128)S(6)} %select_n.58, s32[]{:T(128)S(6)} %select_n.62), kind=kLoop, calls=%fused_computation.9 | loop fusion | bytes 1048592 | tf_op jit(solution)/shard_map/dynamic_slice | solution.py:214
  7.9 2.4 %collective-permute-start.8 = (bf16[256,256]{1,0:T(8,128)(2,1)S(1)}, bf16[256,256]{1,0:T(8,128)(2,1)S(1)}, u32[]{:S(2)}, u32[]{:S(2)}) collective-permute-start(bf16[256,256]{1,0:T(8,128)(2,1)S(1)} %get-tuple-element.65), channel_id=1, source_target_pairs={{0,24},{4,28},{8,0},{12,4},{16,8},{20,12},{24,16},{28,20},{32,56},... | collective-permute-start | bytes 393224 | tf_op jit(solution)/shard_map/ppermute | solution.py:26
  11.8 3.5 %shard_map.94 = (bf16[16,2,256,128]{3,2,1,0:T(8,128)(2,1)}, f32[4,2,256,128]{3,2,1,0:T(8,128)}) custom-call(bf16[1024,256]{1,0:T(8,128)(2,1)} %refs_1_.5, bf16[2,128,128]{2,1,0:T(8,128)(2,1)} %refs_2_.3), custom_call_target="tpu_custom_call" | custom-call | flops 134000000 | bytes 3500000 | tf_op jit(solution)/shard_map/pallas_call | solution.py:54
  15.4 2.6 %collective-permute-done.6.refs_6_ = bf16[256,256]{1,0:T(8,128)(2,1)S(1)} collective-permute-done((bf16[256,256]{1,0:T(8,128)(2,1)S(1)}, bf16[256,256]{1,0:T(8,128)(2,1)S(1)}, u32[]{:S(2)}, u32[]{:S(2)}) %collective-permute-start.6) | collective-permute-done | bytes 131104 | tf_op jit(solution)/shard_map/ppermute | solution.py:26
  20.0 5.4 %all-to-all-start = ((bf16[16,2,256,128]{3,2,1,0:T(8,128)(2,1)}), bf16[16,2,256,128]{3,2,1,0:T(8,128)(2,1)S(1)}, u32[]{:S(2)}, u32[]{:S(2)}) async-start(bf16[16,2,256,128]{3,2,1,0:T(8,128)(2,1)} %get-tuple-element.35), calls=%async_computation | async-start | bytes 4194304 | tf_op jit(solution)/shard_map/all_to_all | solution.py:200
  25.4 4.1 %collective-permute-start.5 = (bf16[3,2,256,128]{3,2,1,0:T(8,128)(2,1)S(1)}, bf16[3,2,256,128]{3,2,1,0:T(8,128)(2,1)S(1)}, u32[]{:S(2)}, u32[]{:S(2)}) collective-permute-start(bf16[3,2,256,128]{3,2,1,0:T(8,128)(2,1)S(1)} %pad_maximum_fusion.1.refs_1_.refs_4_), channel_id=1, source_target_pairs={{0,3},{1,0},{2,1},{3,2},{4,7},{5,4},{6,5},{7,6},{8,11},{9,8},{10,9... | collective-permute-start | bytes 1179656 | tf_op jit(solution)/shard_map/ppermute | solution.py:34
  32.9 11.8 %collective-permute-done.5.refs_4_.refs_7_ = bf16[3,2,256,128]{3,2,1,0:T(8,128)(2,1)S(1)} collective-permute-done((bf16[3,2,256,128]{3,2,1,0:T(8,128)(2,1)S(1)}, bf16[3,2,256,128]{3,2,1,0:T(8,128)(2,1)S(1)}, u32[]{:S(2)}, u32[]{:S(2)}) %collective-permute-start.5) | collective-permute-done | bytes 393248 | tf_op jit(solution)/shard_map/ppermute | solution.py:34
  44.7 3.5 %collective-permute-done.3.refs_2_.refs_5_ = bf16[3,2,256,128]{3,2,1,0:T(8,128)(2,1)} collective-permute-done((bf16[3,2,256,128]{3,2,1,0:T(8,128)(2,1)S(1)}, bf16[3,2,256,128]{3,2,1,0:T(8,128)(2,1)}, u32[]{:S(2)}, u32[]{:S(2)}) %collective-permute-start.3) | collective-permute-done | bytes 393248 | tf_op jit(solution)/shard_map/ppermute | solution.py:34
  48.2 6.9 %shard_map.93 = (bf16[8,2,256,128]{3,2,1,0:T(8,128)(2,1)}, bf16[8,2,256,128]{3,2,1,0:T(8,128)(2,1)}, bf16[8,2,256,128]{3,2,1,0:T(8,128)(2,1)}, bf16[8,2,256,128]{3,2,1,0:T(8,128)(2,1)}) custom-call(s32[4]{0:T(128)} %pad_add_fusion.pos.refs_0_, s32[64,8]{1,0:T(8,128)} %copy.14.src.refs_1_, s32[64,8]{1,0:T(8,128)} %copy.15.live.refs_2_, ...), custom_call_target="tpu_custom_call" | custom-call | flops 1080000000 | bytes 9000000 | tf_op jit(solution)/shard_map/pallas_call | solution.py:230
  55.7 2.4 %collective-permute-done.9 = bf16[8,2,256,128]{3,2,1,0:T(8,128)(2,1)S(1)} collective-permute-done((bf16[8,2,256,128]{3,2,1,0:T(8,128)(2,1)}, bf16[8,2,256,128]{3,2,1,0:T(8,128)(2,1)S(1)}, u32[]{:S(2)}, u32[]{:S(2)}) %collective-permute-start.9) | collective-permute-done | bytes 1048608 | tf_op jit(solution)/shard_map/ppermute | solution.py:30
  58.0 1.5 %add_convert_fusion.1 = bf16[8,2,256,128]{3,2,1,0:T(8,128)(2,1)S(1)} fusion(bf16[8,2,256,128]{3,2,1,0:T(8,128)(2,1)S(1)} %collective-permute-done.9, bf16[8,2,256,128]{3,2,1,0:T(8,128)(2,1)} %get-tuple-element.37), kind=kLoop, calls=%fused_computation.2 | loop fusion | flops 2097152 | bytes 3145728 | tf_op jit(solution)/shard_map/convert_element_type | solution.py:243
  59.9 1.5 %pad_maximum_fusion = bf16[16,2,256,128]{3,2,1,0:T(8,128)(2,1)} fusion(bf16[8,2,256,128]{3,2,1,0:T(8,128)(2,1)S(1)} %add_convert_fusion, bf16[8,2,256,128]{3,2,1,0:T(8,128)(2,1)S(1)} %add_convert_fusion.1), kind=kLoop, calls=%fused_computation | loop fusion | flops 1048576 | bytes 4194304 | tf_op jit(solution)/shard_map/concatenate | solution.py:241
  61.5 6.9 %all-to-all-start.1 = ((bf16[16,2,256,128]{3,2,1,0:T(8,128)(2,1)}), bf16[16,2,256,128]{3,2,1,0:T(8,128)(2,1)}, u32[]{:S(2)}, u32[]{:S(2)}) async-start(bf16[16,2,256,128]{3,2,1,0:T(8,128)(2,1)} %pad_maximum_fusion), calls=%async_computation.1 | async-start | bytes 4194304 | tf_op jit(solution)/shard_map/all_to_all | solution.py:200
  68.5 8.4 %shard_map.95 = (f32[8,8,32,128]{3,2,1,0:T(8,128)}, bf16[8,8,32,128]{3,2,1,0:T(8,128)(2,1)}, bf16[8,8,32,128]{3,2,1,0:T(8,128)(2,1)}, bf16[8,8,32,128]{3,2,1,0:T(8,128)(2,1)}) custom-call(s32[4]{0:T(128)} %pad_add_fusion.pos.refs_0_, s32[64,8]{1,0:T(8,128)} %copy.14.src.refs_1_, s32[64,8]{1,0:T(8,128)} %copy.15.live.refs_2_, ...), custom_call_target="tpu_custom_call" | custom-call | flops 1080000000 | bytes 12000000 | tf_op jit(solution)/shard_map/pallas_call | solution.py:54
  79.7 6.4 %shard_map.96 = (bf16[256,256]{1,0:T(8,128)(2,1)}, bf16[256,256]{1,0:T(8,128)(2,1)}, bf16[256,256]{1,0:T(8,128)(2,1)}, bf16[256,256]{1,0:T(8,128)(2,1)}) custom-call(s32[4]{0:T(128)} %pad_add_fusion.pos.refs_0_, s32[64,8]{1,0:T(8,128)} %copy.14.src.refs_1_, s32[64,8]{1,0:T(8,128)} %copy.15.live.refs_2_, bf16[2,1024,128]{2,1,0:T(8,128)(2,1)} %bitcast.10, ...), custom_call_target="tpu_custom_call" | custom-call | flops 1080000000 | bytes 9000000 | tf_op jit(solution)/shard_map/pallas_call | solution.py:54
  86.1 3.1 %collective-permute-start.12 = (bf16[256,256]{1,0:T(8,128)(2,1)}, bf16[256,256]{1,0:T(8,128)(2,1)S(1)}, u32[]{:S(2)}, u32[]{:S(2)}) collective-permute-start(bf16[256,256]{1,0:T(8,128)(2,1)} %get-tuple-element.45), channel_id=1, source_target_pairs={{0,24},{4,28},{8,0},{12,4},{16,8},{20,12},{24,16},{28,20},{32,56},... | collective-permute-start | bytes 393224 | tf_op jit(solution)/shard_map/ppermute | solution.py:26
  89.2 13.3 %collective-permute-done.12.refs_2_ = bf16[256,256]{1,0:T(8,128)(2,1)S(1)} collective-permute-done((bf16[256,256]{1,0:T(8,128)(2,1)}, bf16[256,256]{1,0:T(8,128)(2,1)S(1)}, u32[]{:S(2)}, u32[]{:S(2)}) %collective-permute-start.12) | collective-permute-done | bytes 131104 | tf_op jit(solution)/shard_map/ppermute | solution.py:26
  103.2 3.5 %shard_map.98 = (bf16[1024,256]{1,0:T(8,128)(2,1)}, f32[2,32,128]{2,1,0:T(8,128)}, f32[2,32,128]{2,1,0:T(8,128)}, f32[2,32,128]{2,1,0:T(8,128)}, f32[2,32,128]{2,1,0:T(8,128)}) custom-call(s32[4]{0:T(128)} %pad_add_fusion.pos.refs_0_, bf16[1024,256]{1,0:T(8,128)(2,1)} %refs_1_.5, bf16[2,128,128]{2,1,0:T(8,128)(2,1)} %refs_2_.3, ...), custom_call_target="tpu_custom_call" | custom-call | flops 268000000 | bytes 3500000 | tf_op jit(solution)/shard_map/pallas_call | solution.py:54
  106.6 2.5 %collective-permute-start.16 = (f32[2,32,128]{2,1,0:T(8,128)}, f32[2,32,128]{2,1,0:T(8,128)S(1)}, u32[]{:S(2)}, u32[]{:S(2)}) collective-permute-start(f32[2,32,128]{2,1,0:T(8,128)} %get-tuple-element.55), channel_id=1, source_target_pairs={{0,2},{1,3},{2,0},{3,1},{4,6},{5,7},{6,4},{7,5},{8,10},{9,11},{10,... | collective-permute-start | bytes 98312 | tf_op jit(solution)/shard_map/ppermute | solution.py:34
  109.2 1.5 %collective-permute-start.17 = (f32[2,32,128]{2,1,0:T(8,128)}, f32[2,32,128]{2,1,0:T(8,128)S(1)}, u32[]{:S(2)}, u32[]{:S(2)}) collective-permute-start(f32[2,32,128]{2,1,0:T(8,128)} %get-tuple-element.56), channel_id=1, source_target_pairs={{0,3},{1,0},{2,1},{3,2},{4,7},{5,4},{6,5},{7,6},{8,11},{9,8},{10,9... | collective-permute-start | bytes 98312 | tf_op jit(solution)/shard_map/ppermute | solution.py:34
  111.0 1.5 %collective-permute-start.21 = (bf16[2,8,32,128]{3,2,1,0:T(8,128)(2,1)S(1)}, bf16[2,8,32,128]{3,2,1,0:T(8,128)(2,1)S(1)}, u32[]{:S(2)}, u32[]{:S(2)}) collective-permute-start(bf16[2,8,32,128]{3,2,1,0:T(8,128)(2,1)S(1)} %get-tuple-element.62), channel_id=1, source_target_pairs={{0,24},{4,28},{8,0},{12,4},{16,8},{20,12},{24,16},{28,20},{32,56},... | collective-permute-start | bytes 393224 | tf_op jit(solution)/shard_map/ppermute | solution.py:26
  113.2 2.6 %collective-permute-start.22 = (bf16[2,8,32,128]{3,2,1,0:T(8,128)(2,1)S(1)}, bf16[2,8,32,128]{3,2,1,0:T(8,128)(2,1)S(1)}, u32[]{:S(2)}, u32[]{:S(2)}) collective-permute-start(bf16[2,8,32,128]{3,2,1,0:T(8,128)(2,1)S(1)} %get-tuple-element.64), channel_id=1, source_target_pairs={{0,16},{4,20},{8,24},{12,28},{16,0},{20,4},{24,8},{28,12},{32,48},... | collective-permute-start | bytes 393224 | tf_op jit(solution)/shard_map/ppermute | solution.py:26
  117.1 1.9 %shard_map.97 = bf16[1024,256]{1,0:T(8,128)(2,1)} custom-call(s32[4]{0:T(128)} %pad_add_fusion.pos.refs_0_, bf16[256,256]{1,0:T(8,128)(2,1)} %get-tuple-element.44.refs_1_, bf16[256,256]{1,0:T(8,128)(2,1)} %copy-done.9, bf16[256,256]{1,0:T(8,128)(2,1)} %copy-done.11, bf16[256,256]{1,0:T(8,128)(2,1)} %copy-done.10), custom_call_target="tpu_custom_call" | custom-call | bytes 1000000 | tf_op jit(solution)/shard_map/pallas_call | solution.py:54
  (77 shorter events, 18.3 us)
Async XLA Ops:
  1.6 9.0 %collective-permute-start.2 = (bf16[2,256,128]{2,1,0:T(8,128)(2,1)S(1)}, bf16[2,256,128]{2,1,0:T(8,128)(2,1)S(1)}, u32[]{:S(2)}, u32[]{:S(2)}) collective-permute-start(bf16[2,256,128]{2,1,0:T(8,128)(2,1)S(1)} %constant_dynamic-slice_fusion.4), channel_id=1, source_target_pairs={{0,24},{4,28},{8,0},{12,4},{16,8},{20,12},{24,16},{28,20},{32,56},... | collective-permute-start | bytes 393224 | tf_op jit(solution)/shard_map/ppermute | solution.py:26
  4.5 10.8 %collective-permute-start.1 = (bf16[2,256,128]{2,1,0:T(8,128)(2,1)S(1)}, bf16[2,256,128]{2,1,0:T(8,128)(2,1)S(1)}, u32[]{:S(2)}, u32[]{:S(2)}) collective-permute-start(bf16[2,256,128]{2,1,0:T(8,128)(2,1)S(1)} %constant_dynamic-slice_fusion.4), channel_id=1, source_target_pairs={{0,16},{4,20},{8,24},{12,28},{16,0},{20,4},{24,8},{28,12},{32,48},... | collective-permute-start | bytes 393224 | tf_op jit(solution)/shard_map/ppermute | solution.py:26
  5.3 10.0 %collective-permute-start = (bf16[2,256,128]{2,1,0:T(8,128)(2,1)S(1)}, bf16[2,256,128]{2,1,0:T(8,128)(2,1)S(1)}, u32[]{:S(2)}, u32[]{:S(2)}) collective-permute-start(bf16[2,256,128]{2,1,0:T(8,128)(2,1)S(1)} %constant_dynamic-slice_fusion.4), channel_id=1, source_target_pairs={{0,8},{4,12},{8,16},{12,20},{16,24},{20,28},{24,0},{28,4},{32,40},... | collective-permute-start | bytes 393224 | tf_op jit(solution)/shard_map/ppermute | solution.py:26
  7.9 7.4 %collective-permute-start.8 = (bf16[256,256]{1,0:T(8,128)(2,1)S(1)}, bf16[256,256]{1,0:T(8,128)(2,1)S(1)}, u32[]{:S(2)}, u32[]{:S(2)}) collective-permute-start(bf16[256,256]{1,0:T(8,128)(2,1)S(1)} %get-tuple-element.65), channel_id=1, source_target_pairs={{0,24},{4,28},{8,0},{12,4},{16,8},{20,12},{24,16},{28,20},{32,56},... | collective-permute-start | bytes 393224 | tf_op jit(solution)/shard_map/ppermute | solution.py:26
  10.3 7.7 %collective-permute-start.6 = (bf16[256,256]{1,0:T(8,128)(2,1)S(1)}, bf16[256,256]{1,0:T(8,128)(2,1)S(1)}, u32[]{:S(2)}, u32[]{:S(2)}) collective-permute-start(bf16[256,256]{1,0:T(8,128)(2,1)S(1)} %get-tuple-element.66), channel_id=1, source_target_pairs={{0,8},{4,12},{8,16},{12,20},{16,24},{20,28},{24,0},{28,4},{32,40},... | collective-permute-start | bytes 393224 | tf_op jit(solution)/shard_map/ppermute | solution.py:26
  10.6 8.8 %collective-permute-start.7 = (bf16[256,256]{1,0:T(8,128)(2,1)S(1)}, bf16[256,256]{1,0:T(8,128)(2,1)S(1)}, u32[]{:S(2)}, u32[]{:S(2)}) collective-permute-start(bf16[256,256]{1,0:T(8,128)(2,1)S(1)} %get-tuple-element.68), channel_id=1, source_target_pairs={{0,16},{4,20},{8,24},{12,28},{16,0},{20,4},{24,8},{28,12},{32,48},... | collective-permute-start | bytes 393224 | tf_op jit(solution)/shard_map/ppermute | solution.py:26
  20.0 35.1 %all-to-all-start = ((bf16[16,2,256,128]{3,2,1,0:T(8,128)(2,1)}), bf16[16,2,256,128]{3,2,1,0:T(8,128)(2,1)S(1)}, u32[]{:S(2)}, u32[]{:S(2)}) async-start(bf16[16,2,256,128]{3,2,1,0:T(8,128)(2,1)} %get-tuple-element.35), calls=%async_computation | async-start | bytes 4194304 | tf_op jit(solution)/shard_map/all_to_all | solution.py:200
  25.4 19.2 %collective-permute-start.5 = (bf16[3,2,256,128]{3,2,1,0:T(8,128)(2,1)S(1)}, bf16[3,2,256,128]{3,2,1,0:T(8,128)(2,1)S(1)}, u32[]{:S(2)}, u32[]{:S(2)}) collective-permute-start(bf16[3,2,256,128]{3,2,1,0:T(8,128)(2,1)S(1)} %pad_maximum_fusion.1.refs_1_.refs_4_), channel_id=1, source_target_pairs={{0,3},{1,0},{2,1},{3,2},{4,7},{5,4},{6,5},{7,6},{8,11},{9,8},{10,9... | collective-permute-start | bytes 1179656 | tf_op jit(solution)/shard_map/ppermute | solution.py:34
  29.5 15.1 %collective-permute-start.4 = (bf16[3,2,256,128]{3,2,1,0:T(8,128)(2,1)S(1)}, bf16[3,2,256,128]{3,2,1,0:T(8,128)(2,1)S(1)}, u32[]{:S(2)}, u32[]{:S(2)}) collective-permute-start(bf16[3,2,256,128]{3,2,1,0:T(8,128)(2,1)S(1)} %pad_maximum_fusion.1.refs_1_.refs_4_), channel_id=1, source_target_pairs={{0,2},{1,3},{2,0},{3,1},{4,6},{5,7},{6,4},{7,5},{8,10},{9,11},{10,... | collective-permute-start | bytes 1179656 | tf_op jit(solution)/shard_map/ppermute | solution.py:34
  29.6 18.6 %collective-permute-start.3 = (bf16[3,2,256,128]{3,2,1,0:T(8,128)(2,1)S(1)}, bf16[3,2,256,128]{3,2,1,0:T(8,128)(2,1)}, u32[]{:S(2)}, u32[]{:S(2)}) collective-permute-start(bf16[3,2,256,128]{3,2,1,0:T(8,128)(2,1)S(1)} %pad_maximum_fusion.1.refs_1_.refs_4_), channel_id=1, source_target_pairs={{0,1},{1,2},{2,3},{3,0},{4,5},{5,6},{6,7},{7,4},{8,9},{9,10},{10,1... | collective-permute-start | bytes 1179656 | tf_op jit(solution)/shard_map/ppermute | solution.py:34
  61.4 7.1 %collective-permute-start.11 = (bf16[16,2,256,128]{3,2,1,0:T(8,128)(2,1)S(1)}, bf16[16,2,256,128]{3,2,1,0:T(8,128)(2,1)}, u32[]{:S(2)}, u32[]{:S(2)}) collective-permute-start(bf16[16,2,256,128]{3,2,1,0:T(8,128)(2,1)S(1)} %all-to-all-done.refs_3_.refs_8_), channel_id=1, source_target_pairs={{0,4},{4,0},{8,12},{12,8},{16,20},{20,16},{24,28},{28,24},{32,36},... | collective-permute-start | bytes 6291464 | tf_op jit(solution)/shard_map/ppermute | solution.py:30
  61.5 41.6 %all-to-all-start.1 = ((bf16[16,2,256,128]{3,2,1,0:T(8,128)(2,1)}), bf16[16,2,256,128]{3,2,1,0:T(8,128)(2,1)}, u32[]{:S(2)}, u32[]{:S(2)}) async-start(bf16[16,2,256,128]{3,2,1,0:T(8,128)(2,1)} %pad_maximum_fusion), calls=%async_computation.1 | async-start | bytes 4194304 | tf_op jit(solution)/shard_map/all_to_all | solution.py:200
  76.9 29.8 %collective-permute-start.19 = (bf16[8,8,32,128]{3,2,1,0:T(8,128)(2,1)}, bf16[8,8,32,128]{3,2,1,0:T(8,128)(2,1)S(1)}, u32[]{:S(2)}, u32[]{:S(2)}) collective-permute-start(bf16[8,8,32,128]{3,2,1,0:T(8,128)(2,1)} %get-tuple-element.58), channel_id=1, source_target_pairs={{0,2},{1,3},{2,0},{3,1},{4,6},{5,7},{6,4},{7,5},{8,10},{9,11},{10,... | collective-permute-start | bytes 1572872 | tf_op jit(solution)/shard_map/ppermute | solution.py:34
  77.6 31.5 %collective-permute-start.20 = (bf16[8,8,32,128]{3,2,1,0:T(8,128)(2,1)}, bf16[8,8,32,128]{3,2,1,0:T(8,128)(2,1)S(1)}, u32[]{:S(2)}, u32[]{:S(2)}) collective-permute-start(bf16[8,8,32,128]{3,2,1,0:T(8,128)(2,1)} %get-tuple-element.59), channel_id=1, source_target_pairs={{0,3},{1,0},{2,1},{3,2},{4,7},{5,4},{6,5},{7,6},{8,11},{9,8},{10,9... | collective-permute-start | bytes 1572872 | tf_op jit(solution)/shard_map/ppermute | solution.py:34
  78.8 31.9 %collective-permute-start.18 = (bf16[8,8,32,128]{3,2,1,0:T(8,128)(2,1)}, bf16[8,8,32,128]{3,2,1,0:T(8,128)(2,1)S(1)}, u32[]{:S(2)}, u32[]{:S(2)}) collective-permute-start(bf16[8,8,32,128]{3,2,1,0:T(8,128)(2,1)} %get-tuple-element.42), channel_id=1, source_target_pairs={{0,1},{1,2},{2,3},{3,0},{4,5},{5,6},{6,7},{7,4},{8,9},{9,10},{10,1... | collective-permute-start | bytes 1572872 | tf_op jit(solution)/shard_map/ppermute | solution.py:34
  86.1 16.3 %collective-permute-start.12 = (bf16[256,256]{1,0:T(8,128)(2,1)}, bf16[256,256]{1,0:T(8,128)(2,1)S(1)}, u32[]{:S(2)}, u32[]{:S(2)}) collective-permute-start(bf16[256,256]{1,0:T(8,128)(2,1)} %get-tuple-element.45), channel_id=1, source_target_pairs={{0,24},{4,28},{8,0},{12,4},{16,8},{20,12},{24,16},{28,20},{32,56},... | collective-permute-start | bytes 393224 | tf_op jit(solution)/shard_map/ppermute | solution.py:26
  89.2 14.0 %collective-permute-start.14 = (bf16[256,256]{1,0:T(8,128)(2,1)}, bf16[256,256]{1,0:T(8,128)(2,1)S(1)}, u32[]{:S(2)}, u32[]{:S(2)}) collective-permute-start(bf16[256,256]{1,0:T(8,128)(2,1)} %get-tuple-element.48), channel_id=1, source_target_pairs={{0,8},{4,12},{8,16},{12,20},{16,24},{20,28},{24,0},{28,4},{32,40},... | collective-permute-start | bytes 393224 | tf_op jit(solution)/shard_map/ppermute | solution.py:26
  102.4 14.0 %collective-permute-start.13 = (bf16[256,256]{1,0:T(8,128)(2,1)}, bf16[256,256]{1,0:T(8,128)(2,1)S(1)}, u32[]{:S(2)}, u32[]{:S(2)}) collective-permute-start(bf16[256,256]{1,0:T(8,128)(2,1)} %get-tuple-element.47), channel_id=1, source_target_pairs={{0,16},{4,20},{8,24},{12,28},{16,0},{20,4},{24,8},{28,12},{32,48},... | collective-permute-start | bytes 393224 | tf_op jit(solution)/shard_map/ppermute | solution.py:26
  106.6 5.9 %collective-permute-start.15 = (f32[2,32,128]{2,1,0:T(8,128)}, f32[2,32,128]{2,1,0:T(8,128)S(1)}, u32[]{:S(2)}, u32[]{:S(2)}) collective-permute-start(f32[2,32,128]{2,1,0:T(8,128)} %get-tuple-element.54), channel_id=1, source_target_pairs={{0,1},{1,2},{2,3},{3,0},{4,5},{5,6},{6,7},{7,4},{8,9},{9,10},{10,1... | collective-permute-start | bytes 98312 | tf_op jit(solution)/shard_map/ppermute | solution.py:34
  106.6 6.5 %collective-permute-start.16 = (f32[2,32,128]{2,1,0:T(8,128)}, f32[2,32,128]{2,1,0:T(8,128)S(1)}, u32[]{:S(2)}, u32[]{:S(2)}) collective-permute-start(f32[2,32,128]{2,1,0:T(8,128)} %get-tuple-element.55), channel_id=1, source_target_pairs={{0,2},{1,3},{2,0},{3,1},{4,6},{5,7},{6,4},{7,5},{8,10},{9,11},{10,... | collective-permute-start | bytes 98312 | tf_op jit(solution)/shard_map/ppermute | solution.py:34
  109.2 6.6 %collective-permute-start.17 = (f32[2,32,128]{2,1,0:T(8,128)}, f32[2,32,128]{2,1,0:T(8,128)S(1)}, u32[]{:S(2)}, u32[]{:S(2)}) collective-permute-start(f32[2,32,128]{2,1,0:T(8,128)} %get-tuple-element.56), channel_id=1, source_target_pairs={{0,3},{1,0},{2,1},{3,2},{4,7},{5,4},{6,5},{7,6},{8,11},{9,8},{10,9... | collective-permute-start | bytes 98312 | tf_op jit(solution)/shard_map/ppermute | solution.py:34
  111.0 7.9 %collective-permute-start.21 = (bf16[2,8,32,128]{3,2,1,0:T(8,128)(2,1)S(1)}, bf16[2,8,32,128]{3,2,1,0:T(8,128)(2,1)S(1)}, u32[]{:S(2)}, u32[]{:S(2)}) collective-permute-start(bf16[2,8,32,128]{3,2,1,0:T(8,128)(2,1)S(1)} %get-tuple-element.62), channel_id=1, source_target_pairs={{0,24},{4,28},{8,0},{12,4},{16,8},{20,12},{24,16},{28,20},{32,56},... | collective-permute-start | bytes 393224 | tf_op jit(solution)/shard_map/ppermute | solution.py:26
  112.5 6.5 %collective-permute-start.23 = (bf16[2,8,32,128]{3,2,1,0:T(8,128)(2,1)S(1)}, bf16[2,8,32,128]{3,2,1,0:T(8,128)(2,1)S(1)}, u32[]{:S(2)}, u32[]{:S(2)}) collective-permute-start(bf16[2,8,32,128]{3,2,1,0:T(8,128)(2,1)S(1)} %get-tuple-element.63), channel_id=1, source_target_pairs={{0,8},{4,12},{8,16},{12,20},{16,24},{20,28},{24,0},{28,4},{32,40},... | collective-permute-start | bytes 393224 | tf_op jit(solution)/shard_map/ppermute | solution.py:26
  113.2 7.0 %collective-permute-start.22 = (bf16[2,8,32,128]{3,2,1,0:T(8,128)(2,1)S(1)}, bf16[2,8,32,128]{3,2,1,0:T(8,128)(2,1)S(1)}, u32[]{:S(2)}, u32[]{:S(2)}) collective-permute-start(bf16[2,8,32,128]{3,2,1,0:T(8,128)(2,1)S(1)} %get-tuple-element.64), channel_id=1, source_target_pairs={{0,16},{4,20},{8,24},{12,28},{16,0},{20,4},{24,8},{28,12},{32,48},... | collective-permute-start | bytes 393224 | tf_op jit(solution)/shard_map/ppermute | solution.py:26
  (17 other events, 115.8 us)

commit v6 on v5

--- a/solution.py
+++ b/solution.py
@@ -222,8 +222,11 @@
         3_500_000,
     )
     act, *_ = lax.optimization_barrier((act, w0, *grads[1:]))
+    mine_ready = act
     mine = exchange(act)
     weights = [w_own, w0] + [shift_z(w0, t) for t in (1, 2, 3)]
+    grad_later, _ = lax.optimization_barrier((grad_out, mine_ready))
+    grads[0] = lax.dynamic_slice_in_dim(grad_later, x * 256, 256, 0)
 
     inputs = [*weights, *grads]
     half = sds((8, 2, 256, 128), BF)

time: 122 us -> 123 us (level)
    dynamic_slice x0 -> x1, local copies, waits for them, and re-layouts: none -> 1.57 us  [shards(): grads[0] = lax.dynamic_slice_in_dim(grad_later, x * 256, 256, 0)]
    ppermute x9, starting transfers between devices: 12.1 us -> 13.5 us  [shift_z(): return lax.ppermute(value, 'tok', [(z, (z + step) % NZ) for z in range(NZ)])]
  transfers between devices with their start and end apart: 26 -> 26, of which waited for: 9 -> 10; matrix products, arithmetic and copies ran while one was open for 5% -> 6% of each run, Pallas kernels for 25% -> 25%
where the time goes in v6:
time: 123 us; the launch traced here: 122 us
  starting transfers between devices  42.2 us (34%)
  waiting for transfers between devices  36.4 us (30%)
  Pallas kernels  30.6 us (25%)
  local copies, waits for them, and re-layouts  6.3 us (5%)
  other arithmetic  5.74 us (5%)
    pallas_call x5, Pallas kernels, call(): pl.pallas_call(lambda *refs: body(*refs), grid=(1,), out_shape=outs, in_s...  23.7 us
    ppermute x12, waiting for transfers between devices, shift_x(): return lax.ppermute(value, 'blk', along(0, step, 0))  18.5 us
    ppermute x12, starting transfers between devices, shift_x(): return lax.ppermute(value, 'blk', along(0, step, 0))  16.2 us
    ppermute x9, waiting for transfers between devices, shift_z(): return lax.ppermute(value, 'tok', [(z, (z + step) % NZ) for z in range(NZ)])  14.8 us
    ppermute x9, starting transfers between devices, shift_z(): return lax.ppermute(value, 'tok', [(z, (z + step) % NZ) for z in range(NZ)])  13.5 us
    all_to_all x2, starting transfers between devices, exchange(): lax.all_to_all(value, 'blk', 0, 0, axis_index_groups=groups, tiled=True)  11.7 us
    pallas_call x1, Pallas kernels, shards(): pl.pallas_call(back_body, out_shape=[half] * 4, in_specs=[pl.BlockSpec(me...  6.88 us
    unnamed x32, local copies, waits for them, and re-layouts  2.72 us
  transfers between devices with their start and end apart: 26, of which 10 were waited for; matrix products, arithmetic and copies ran while one was open for 6% of the time, Pallas kernels for 25%

profile of v6, /device:TPU:0, one launch (start us, length us, event | category | flops | bytes accessed | tf_op | source)
XLA Modules:
  0.0 122.1 jit_solution(12312726924432886520)
XLA Ops:
  1.6 2.9 %collective-permute-start.2 = (bf16[2,256,128]{2,1,0:T(8,128)(2,1)S(1)}, bf16[2,256,128]{2,1,0:T(8,128)(2,1)S(1)}, u32[]{:S(2)}, u32[]{:S(2)}) collective-permute-start(bf16[2,256,128]{2,1,0:T(8,128)(2,1)S(1)} %constant_dynamic-slice_fusion.4), channel_id=1, source_target_pairs={{0,24},{4,28},{8,0},{12,4},{16,8},{20,12},{24,16},{28,20},{32,56},... | collective-permute-start | bytes 393224 | tf_op jit(solution)/shard_map/ppermute | solution.py:26
  7.2 2.4 %collective-permute-start.8 = (bf16[256,256]{1,0:T(8,128)(2,1)S(1)}, bf16[256,256]{1,0:T(8,128)(2,1)S(1)}, u32[]{:S(2)}, u32[]{:S(2)}) collective-permute-start(bf16[256,256]{1,0:T(8,128)(2,1)S(1)} %get-tuple-element.67), channel_id=1, source_target_pairs={{0,24},{4,28},{8,0},{12,4},{16,8},{20,12},{24,16},{28,20},{32,56},... | collective-permute-start | bytes 393224 | tf_op jit(solution)/shard_map/ppermute | solution.py:26
  9.6 1.5 %collective-permute-start.7 = (bf16[256,256]{1,0:T(8,128)(2,1)S(1)}, bf16[256,256]{1,0:T(8,128)(2,1)S(1)}, u32[]{:S(2)}, u32[]{:S(2)}) collective-permute-start(bf16[256,256]{1,0:T(8,128)(2,1)S(1)} %get-tuple-element.68), channel_id=1, source_target_pairs={{0,16},{4,20},{8,24},{12,28},{16,0},{20,4},{24,8},{28,12},{32,48},... | collective-permute-start | bytes 393224 | tf_op jit(solution)/shard_map/ppermute | solution.py:26
  11.6 3.5 %shard_map.93 = (bf16[16,2,256,128]{3,2,1,0:T(8,128)(2,1)}, f32[4,2,256,128]{3,2,1,0:T(8,128)}) custom-call(bf16[1024,256]{1,0:T(8,128)(2,1)} %refs_1_.5, bf16[2,128,128]{2,1,0:T(8,128)(2,1)} %refs_2_.3), custom_call_target="tpu_custom_call" | custom-call | flops 134000000 | bytes 3500000 | tf_op jit(solution)/shard_map/pallas_call | solution.py:54
  16.0 1.8 %collective-permute-done.7.refs_7_ = bf16[256,256]{1,0:T(8,128)(2,1)S(1)} collective-permute-done((bf16[256,256]{1,0:T(8,128)(2,1)S(1)}, bf16[256,256]{1,0:T(8,128)(2,1)S(1)}, u32[]{:S(2)}, u32[]{:S(2)}) %collective-permute-start.7) | collective-permute-done | bytes 131104 | tf_op jit(solution)/shard_map/ppermute | solution.py:26
  17.8 1.6 %collective-permute-done.6.refs_6_ = bf16[256,256]{1,0:T(8,128)(2,1)S(1)} collective-permute-done((bf16[256,256]{1,0:T(8,128)(2,1)S(1)}, bf16[256,256]{1,0:T(8,128)(2,1)S(1)}, u32[]{:S(2)}, u32[]{:S(2)}) %collective-permute-start.6) | collective-permute-done | bytes 131104 | tf_op jit(solution)/shard_map/ppermute | solution.py:26
  20.0 4.8 %all-to-all-start = ((bf16[16,2,256,128]{3,2,1,0:T(8,128)(2,1)}), bf16[16,2,256,128]{3,2,1,0:T(8,128)(2,1)S(1)}, u32[]{:S(2)}, u32[]{:S(2)}) async-start(bf16[16,2,256,128]{3,2,1,0:T(8,128)(2,1)} %get-tuple-element.34), calls=%async_computation | async-start | bytes 4194304 | tf_op jit(solution)/shard_map/all_to_all | solution.py:200
  24.8 4.1 %collective-permute-start.5 = (bf16[3,2,256,128]{3,2,1,0:T(8,128)(2,1)S(1)}, bf16[3,2,256,128]{3,2,1,0:T(8,128)(2,1)S(1)}, u32[]{:S(2)}, u32[]{:S(2)}) collective-permute-start(bf16[3,2,256,128]{3,2,1,0:T(8,128)(2,1)S(1)} %pad_maximum_fusion.1.refs_1_.refs_4_), channel_id=1, source_target_pairs={{0,3},{1,0},{2,1},{3,2},{4,7},{5,4},{6,5},{7,6},{8,11},{9,8},{10,9... | collective-permute-start | bytes 1179656 | tf_op jit(solution)/shard_map/ppermute | solution.py:34
  32.3 1.6 %constant_dynamic-slice_fusion.refs_5_ = bf16[256,256]{1,0:T(8,128)(2,1)} fusion(bf16[1024,256]{1,0:T(8,128)(2,1)} %param.11, s32[]{:T(128)S(6)} %select_n.59), kind=kLoop, calls=%fused_computation.9 | loop fusion | bytes 262148 | tf_op jit(solution)/shard_map/dynamic_slice | solution.py:229
  33.8 11.3 %collective-permute-done.5.refs_4_.refs_7_ = bf16[3,2,256,128]{3,2,1,0:T(8,128)(2,1)S(1)} collective-permute-done((bf16[3,2,256,128]{3,2,1,0:T(8,128)(2,1)S(1)}, bf16[3,2,256,128]{3,2,1,0:T(8,128)(2,1)S(1)}, u32[]{:S(2)}, u32[]{:S(2)}) %collective-permute-start.5) | collective-permute-done | bytes 393248 | tf_op jit(solution)/shard_map/ppermute | solution.py:34
  45.1 3.5 %collective-permute-done.3.refs_2_.refs_5_ = bf16[3,2,256,128]{3,2,1,0:T(8,128)(2,1)} collective-permute-done((bf16[3,2,256,128]{3,2,1,0:T(8,128)(2,1)S(1)}, bf16[3,2,256,128]{3,2,1,0:T(8,128)(2,1)}, u32[]{:S(2)}, u32[]{:S(2)}) %collective-permute-start.3) | collective-permute-done | bytes 393248 | tf_op jit(solution)/shard_map/ppermute | solution.py:34
  48.6 6.9 %shard_map.94 = (bf16[8,2,256,128]{3,2,1,0:T(8,128)(2,1)}, bf16[8,2,256,128]{3,2,1,0:T(8,128)(2,1)}, bf16[8,2,256,128]{3,2,1,0:T(8,128)(2,1)}, bf16[8,2,256,128]{3,2,1,0:T(8,128)(2,1)}) custom-call(s32[4]{0:T(128)} %pad_add_fusion.pos.refs_0_, s32[64,8]{1,0:T(8,128)} %copy.14.src.refs_1_, s32[64,8]{1,0:T(8,128)} %copy.15.live.refs_2_, ...), custom_call_target="tpu_custom_call" | custom-call | flops 1080000000 | bytes 9000000 | tf_op jit(solution)/shard_map/pallas_call | solution.py:233
  56.1 2.4 %collective-permute-done.9 = bf16[8,2,256,128]{3,2,1,0:T(8,128)(2,1)S(1)} collective-permute-done((bf16[8,2,256,128]{3,2,1,0:T(8,128)(2,1)}, bf16[8,2,256,128]{3,2,1,0:T(8,128)(2,1)S(1)}, u32[]{:S(2)}, u32[]{:S(2)}) %collective-permute-start.9) | collective-permute-done | bytes 1048608 | tf_op jit(solution)/shard_map/ppermute | solution.py:30
  58.5 1.5 %add_convert_fusion.1 = bf16[8,2,256,128]{3,2,1,0:T(8,128)(2,1)S(1)} fusion(bf16[8,2,256,128]{3,2,1,0:T(8,128)(2,1)S(1)} %collective-permute-done.9, bf16[8,2,256,128]{3,2,1,0:T(8,128)(2,1)} %get-tuple-element.39), kind=kLoop, calls=%fused_computation.2 | loop fusion | flops 2097152 | bytes 3145728 | tf_op jit(solution)/shard_map/convert_element_type | solution.py:246
  60.3 1.5 %pad_maximum_fusion = bf16[16,2,256,128]{3,2,1,0:T(8,128)(2,1)} fusion(bf16[8,2,256,128]{3,2,1,0:T(8,128)(2,1)S(1)} %add_convert_fusion, bf16[8,2,256,128]{3,2,1,0:T(8,128)(2,1)S(1)} %add_convert_fusion.1), kind=kLoop, calls=%fused_computation | loop fusion | flops 1048576 | bytes 4194304 | tf_op jit(solution)/shard_map/concatenate | solution.py:244
  62.0 6.9 %all-to-all-start.1 = ((bf16[16,2,256,128]{3,2,1,0:T(8,128)(2,1)}), bf16[16,2,256,128]{3,2,1,0:T(8,128)(2,1)}, u32[]{:S(2)}, u32[]{:S(2)}) async-start(bf16[16,2,256,128]{3,2,1,0:T(8,128)(2,1)} %pad_maximum_fusion), calls=%async_computation.1 | async-start | bytes 4194304 | tf_op jit(solution)/shard_map/all_to_all | solution.py:200
  68.9 8.4 %shard_map.95 = (f32[8,8,32,128]{3,2,1,0:T(8,128)}, bf16[8,8,32,128]{3,2,1,0:T(8,128)(2,1)}, bf16[8,8,32,128]{3,2,1,0:T(8,128)(2,1)}, bf16[8,8,32,128]{3,2,1,0:T(8,128)(2,1)}) custom-call(s32[4]{0:T(128)} %pad_add_fusion.pos.refs_0_, s32[64,8]{1,0:T(8,128)} %copy.14.src.refs_1_, s32[64,8]{1,0:T(8,128)} %copy.15.live.refs_2_, ...), custom_call_target="tpu_custom_call" | custom-call | flops 1080000000 | bytes 12000000 | tf_op jit(solution)/shard_map/pallas_call | solution.py:54
  80.7 6.4 %shard_map.96 = (bf16[256,256]{1,0:T(8,128)(2,1)}, bf16[256,256]{1,0:T(8,128)(2,1)}, bf16[256,256]{1,0:T(8,128)(2,1)}, bf16[256,256]{1,0:T(8,128)(2,1)}) custom-call(s32[4]{0:T(128)} %pad_add_fusion.pos.refs_0_, s32[64,8]{1,0:T(8,128)} %copy.14.src.refs_1_, s32[64,8]{1,0:T(8,128)} %copy.15.live.refs_2_, bf16[2,1024,128]{2,1,0:T(8,128)(2,1)} %bitcast.10, ...), custom_call_target="tpu_custom_call" | custom-call | flops 1080000000 | bytes 9000000 | tf_op jit(solution)/shard_map/pallas_call | solution.py:54
  87.2 3.0 %collective-permute-start.12 = (bf16[256,256]{1,0:T(8,128)(2,1)}, bf16[256,256]{1,0:T(8,128)(2,1)S(1)}, u32[]{:S(2)}, u32[]{:S(2)}) collective-permute-start(bf16[256,256]{1,0:T(8,128)(2,1)} %get-tuple-element.47), channel_id=1, source_target_pairs={{0,24},{4,28},{8,0},{12,4},{16,8},{20,12},{24,16},{28,20},{32,56},... | collective-permute-start | bytes 393224 | tf_op jit(solution)/shard_map/ppermute | solution.py:26
  90.2 12.7 %collective-permute-done.12.refs_2_ = bf16[256,256]{1,0:T(8,128)(2,1)S(1)} collective-permute-done((bf16[256,256]{1,0:T(8,128)(2,1)}, bf16[256,256]{1,0:T(8,128)(2,1)S(1)}, u32[]{:S(2)}, u32[]{:S(2)}) %collective-permute-start.12) | collective-permute-done | bytes 131104 | tf_op jit(solution)/shard_map/ppermute | solution.py:26
  103.6 3.5 %shard_map.98 = (bf16[1024,256]{1,0:T(8,128)(2,1)}, f32[2,32,128]{2,1,0:T(8,128)}, f32[2,32,128]{2,1,0:T(8,128)}, f32[2,32,128]{2,1,0:T(8,128)}, f32[2,32,128]{2,1,0:T(8,128)}) custom-call(s32[4]{0:T(128)} %pad_add_fusion.pos.refs_0_, bf16[1024,256]{1,0:T(8,128)(2,1)} %refs_1_.5, bf16[2,128,128]{2,1,0:T(8,128)(2,1)} %refs_2_.3, ...), custom_call_target="tpu_custom_call" | custom-call | flops 268000000 | bytes 3500000 | tf_op jit(solution)/shard_map/pallas_call | solution.py:54
  107.3 3.6 %collective-permute-start.16 = (f32[2,32,128]{2,1,0:T(8,128)}, f32[2,32,128]{2,1,0:T(8,128)S(1)}, u32[]{:S(2)}, u32[]{:S(2)}) collective-permute-start(f32[2,32,128]{2,1,0:T(8,128)} %get-tuple-element.57), channel_id=1, source_target_pairs={{0,2},{1,3},{2,0},{3,1},{4,6},{5,7},{6,4},{7,5},{8,10},{9,11},{10,... | collective-permute-start | bytes 98312 | tf_op jit(solution)/shard_map/ppermute | solution.py:34
  114.4 2.6 %collective-permute-start.22 = (bf16[2,8,32,128]{3,2,1,0:T(8,128)(2,1)S(1)}, bf16[2,8,32,128]{3,2,1,0:T(8,128)(2,1)S(1)}, u32[]{:S(2)}, u32[]{:S(2)}) collective-permute-start(bf16[2,8,32,128]{3,2,1,0:T(8,128)(2,1)S(1)} %get-tuple-element.66), channel_id=1, source_target_pairs={{0,16},{4,20},{8,24},{12,28},{16,0},{20,4},{24,8},{28,12},{32,48},... | collective-permute-start | bytes 393224 | tf_op jit(solution)/shard_map/ppermute | solution.py:26
  118.2 1.9 %shard_map.97 = bf16[1024,256]{1,0:T(8,128)(2,1)} custom-call(s32[4]{0:T(128)} %pad_add_fusion.pos.refs_0_, bf16[256,256]{1,0:T(8,128)(2,1)} %get-tuple-element.46.refs_1_, bf16[256,256]{1,0:T(8,128)(2,1)} %copy-done.9, bf16[256,256]{1,0:T(8,128)(2,1)} %copy-done.11, bf16[256,256]{1,0:T(8,128)(2,1)} %copy-done.10), custom_call_target="tpu_custom_call" | custom-call | bytes 1000000 | tf_op jit(solution)/shard_map/pallas_call | solution.py:54
  (78 shorter events, 21.0 us)
Async XLA Ops:
  1.6 10.0 %collective-permute-start.2 = (bf16[2,256,128]{2,1,0:T(8,128)(2,1)S(1)}, bf16[2,256,128]{2,1,0:T(8,128)(2,1)S(1)}, u32[]{:S(2)}, u32[]{:S(2)}) collective-permute-start(bf16[2,256,128]{2,1,0:T(8,128)(2,1)S(1)} %constant_dynamic-slice_fusion.4), channel_id=1, source_target_pairs={{0,24},{4,28},{8,0},{12,4},{16,8},{20,12},{24,16},{28,20},{32,56},... | collective-permute-start | bytes 393224 | tf_op jit(solution)/shard_map/ppermute | solution.py:26
  4.5 10.6 %collective-permute-start.1 = (bf16[2,256,128]{2,1,0:T(8,128)(2,1)S(1)}, bf16[2,256,128]{2,1,0:T(8,128)(2,1)S(1)}, u32[]{:S(2)}, u32[]{:S(2)}) collective-permute-start(bf16[2,256,128]{2,1,0:T(8,128)(2,1)S(1)} %constant_dynamic-slice_fusion.4), channel_id=1, source_target_pairs={{0,16},{4,20},{8,24},{12,28},{16,0},{20,4},{24,8},{28,12},{32,48},... | collective-permute-start | bytes 393224 | tf_op jit(solution)/shard_map/ppermute | solution.py:26
  5.3 10.6 %collective-permute-start = (bf16[2,256,128]{2,1,0:T(8,128)(2,1)S(1)}, bf16[2,256,128]{2,1,0:T(8,128)(2,1)S(1)}, u32[]{:S(2)}, u32[]{:S(2)}) collective-permute-start(bf16[2,256,128]{2,1,0:T(8,128)(2,1)S(1)} %constant_dynamic-slice_fusion.4), channel_id=1, source_target_pairs={{0,8},{4,12},{8,16},{12,20},{16,24},{20,28},{24,0},{28,4},{32,40},... | collective-permute-start | bytes 393224 | tf_op jit(solution)/shard_map/ppermute | solution.py:26
  7.2 8.7 %collective-permute-start.8 = (bf16[256,256]{1,0:T(8,128)(2,1)S(1)}, bf16[256,256]{1,0:T(8,128)(2,1)S(1)}, u32[]{:S(2)}, u32[]{:S(2)}) collective-permute-start(bf16[256,256]{1,0:T(8,128)(2,1)S(1)} %get-tuple-element.67), channel_id=1, source_target_pairs={{0,24},{4,28},{8,0},{12,4},{16,8},{20,12},{24,16},{28,20},{32,56},... | collective-permute-start | bytes 393224 | tf_op jit(solution)/shard_map/ppermute | solution.py:26
  9.6 8.1 %collective-permute-start.7 = (bf16[256,256]{1,0:T(8,128)(2,1)S(1)}, bf16[256,256]{1,0:T(8,128)(2,1)S(1)}, u32[]{:S(2)}, u32[]{:S(2)}) collective-permute-start(bf16[256,256]{1,0:T(8,128)(2,1)S(1)} %get-tuple-element.68), channel_id=1, source_target_pairs={{0,16},{4,20},{8,24},{12,28},{16,0},{20,4},{24,8},{28,12},{32,48},... | collective-permute-start | bytes 393224 | tf_op jit(solution)/shard_map/ppermute | solution.py:26
  11.6 7.8 %collective-permute-start.6 = (bf16[256,256]{1,0:T(8,128)(2,1)S(1)}, bf16[256,256]{1,0:T(8,128)(2,1)S(1)}, u32[]{:S(2)}, u32[]{:S(2)}) collective-permute-start(bf16[256,256]{1,0:T(8,128)(2,1)S(1)} %get-tuple-element.69), channel_id=1, source_target_pairs={{0,8},{4,12},{8,16},{12,20},{16,24},{20,28},{24,0},{28,4},{32,40},... | collective-permute-start | bytes 393224 | tf_op jit(solution)/shard_map/ppermute | solution.py:26
  20.0 35.5 %all-to-all-start = ((bf16[16,2,256,128]{3,2,1,0:T(8,128)(2,1)}), bf16[16,2,256,128]{3,2,1,0:T(8,128)(2,1)S(1)}, u32[]{:S(2)}, u32[]{:S(2)}) async-start(bf16[16,2,256,128]{3,2,1,0:T(8,128)(2,1)} %get-tuple-element.34), calls=%async_computation | async-start | bytes 4194304 | tf_op jit(solution)/shard_map/all_to_all | solution.py:200
  24.8 20.3 %collective-permute-start.5 = (bf16[3,2,256,128]{3,2,1,0:T(8,128)(2,1)S(1)}, bf16[3,2,256,128]{3,2,1,0:T(8,128)(2,1)S(1)}, u32[]{:S(2)}, u32[]{:S(2)}) collective-permute-start(bf16[3,2,256,128]{3,2,1,0:T(8,128)(2,1)S(1)} %pad_maximum_fusion.1.refs_1_.refs_4_), channel_id=1, source_target_pairs={{0,3},{1,0},{2,1},{3,2},{4,7},{5,4},{6,5},{7,6},{8,11},{9,8},{10,9... | collective-permute-start | bytes 1179656 | tf_op jit(solution)/shard_map/ppermute | solution.py:34
  28.9 16.2 %collective-permute-start.4 = (bf16[3,2,256,128]{3,2,1,0:T(8,128)(2,1)S(1)}, bf16[3,2,256,128]{3,2,1,0:T(8,128)(2,1)S(1)}, u32[]{:S(2)}, u32[]{:S(2)}) collective-permute-start(bf16[3,2,256,128]{3,2,1,0:T(8,128)(2,1)S(1)} %pad_maximum_fusion.1.refs_1_.refs_4_), channel_id=1, source_target_pairs={{0,2},{1,3},{2,0},{3,1},{4,6},{5,7},{6,4},{7,5},{8,10},{9,11},{10,... | collective-permute-start | bytes 1179656 | tf_op jit(solution)/shard_map/ppermute | solution.py:34
  28.9 19.7 %collective-permute-start.3 = (bf16[3,2,256,128]{3,2,1,0:T(8,128)(2,1)S(1)}, bf16[3,2,256,128]{3,2,1,0:T(8,128)(2,1)}, u32[]{:S(2)}, u32[]{:S(2)}) collective-permute-start(bf16[3,2,256,128]{3,2,1,0:T(8,128)(2,1)S(1)} %pad_maximum_fusion.1.refs_1_.refs_4_), channel_id=1, source_target_pairs={{0,1},{1,2},{2,3},{3,0},{4,5},{5,6},{6,7},{7,4},{8,9},{9,10},{10,1... | collective-permute-start | bytes 1179656 | tf_op jit(solution)/shard_map/ppermute | solution.py:34
  61.9 7.1 %collective-permute-start.11 = (bf16[16,2,256,128]{3,2,1,0:T(8,128)(2,1)S(1)}, bf16[16,2,256,128]{3,2,1,0:T(8,128)(2,1)}, u32[]{:S(2)}, u32[]{:S(2)}) collective-permute-start(bf16[16,2,256,128]{3,2,1,0:T(8,128)(2,1)S(1)} %all-to-all-done.refs_3_.refs_8_), channel_id=1, source_target_pairs={{0,4},{4,0},{8,12},{12,8},{16,20},{20,16},{24,28},{28,24},{32,36},... | collective-permute-start | bytes 6291464 | tf_op jit(solution)/shard_map/ppermute | solution.py:30
  62.0 41.6 %all-to-all-start.1 = ((bf16[16,2,256,128]{3,2,1,0:T(8,128)(2,1)}), bf16[16,2,256,128]{3,2,1,0:T(8,128)(2,1)}, u32[]{:S(2)}, u32[]{:S(2)}) async-start(bf16[16,2,256,128]{3,2,1,0:T(8,128)(2,1)} %pad_maximum_fusion), calls=%async_computation.1 | async-start | bytes 4194304 | tf_op jit(solution)/shard_map/all_to_all | solution.py:200
  77.3 29.9 %collective-permute-start.19 = (bf16[8,8,32,128]{3,2,1,0:T(8,128)(2,1)}, bf16[8,8,32,128]{3,2,1,0:T(8,128)(2,1)S(1)}, u32[]{:S(2)}, u32[]{:S(2)}) collective-permute-start(bf16[8,8,32,128]{3,2,1,0:T(8,128)(2,1)} %get-tuple-element.60), channel_id=1, source_target_pairs={{0,2},{1,3},{2,0},{3,1},{4,6},{5,7},{6,4},{7,5},{8,10},{9,11},{10,... | collective-permute-start | bytes 1572872 | tf_op jit(solution)/shard_map/ppermute | solution.py:34
  78.7 32.1 %collective-permute-start.20 = (bf16[8,8,32,128]{3,2,1,0:T(8,128)(2,1)}, bf16[8,8,32,128]{3,2,1,0:T(8,128)(2,1)S(1)}, u32[]{:S(2)}, u32[]{:S(2)}) collective-permute-start(bf16[8,8,32,128]{3,2,1,0:T(8,128)(2,1)} %get-tuple-element.61), channel_id=1, source_target_pairs={{0,3},{1,0},{2,1},{3,2},{4,7},{5,4},{6,5},{7,6},{8,11},{9,8},{10,9... | collective-permute-start | bytes 1572872 | tf_op jit(solution)/shard_map/ppermute | solution.py:34
  79.4 32.4 %collective-permute-start.18 = (bf16[8,8,32,128]{3,2,1,0:T(8,128)(2,1)}, bf16[8,8,32,128]{3,2,1,0:T(8,128)(2,1)S(1)}, u32[]{:S(2)}, u32[]{:S(2)}) collective-permute-start(bf16[8,8,32,128]{3,2,1,0:T(8,128)(2,1)} %get-tuple-element.44), channel_id=1, source_target_pairs={{0,1},{1,2},{2,3},{3,0},{4,5},{5,6},{6,7},{7,4},{8,9},{9,10},{10,1... | collective-permute-start | bytes 1572872 | tf_op jit(solution)/shard_map/ppermute | solution.py:34
  87.2 15.7 %collective-permute-start.12 = (bf16[256,256]{1,0:T(8,128)(2,1)}, bf16[256,256]{1,0:T(8,128)(2,1)S(1)}, u32[]{:S(2)}, u32[]{:S(2)}) collective-permute-start(bf16[256,256]{1,0:T(8,128)(2,1)} %get-tuple-element.47), channel_id=1, source_target_pairs={{0,24},{4,28},{8,0},{12,4},{16,8},{20,12},{24,16},{28,20},{32,56},... | collective-permute-start | bytes 393224 | tf_op jit(solution)/shard_map/ppermute | solution.py:26
  90.2 13.4 %collective-permute-start.14 = (bf16[256,256]{1,0:T(8,128)(2,1)}, bf16[256,256]{1,0:T(8,128)(2,1)S(1)}, u32[]{:S(2)}, u32[]{:S(2)}) collective-permute-start(bf16[256,256]{1,0:T(8,128)(2,1)} %get-tuple-element.50), channel_id=1, source_target_pairs={{0,8},{4,12},{8,16},{12,20},{16,24},{20,28},{24,0},{28,4},{32,40},... | collective-permute-start | bytes 393224 | tf_op jit(solution)/shard_map/ppermute | solution.py:26
  102.9 14.7 %collective-permute-start.13 = (bf16[256,256]{1,0:T(8,128)(2,1)}, bf16[256,256]{1,0:T(8,128)(2,1)S(1)}, u32[]{:S(2)}, u32[]{:S(2)}) collective-permute-start(bf16[256,256]{1,0:T(8,128)(2,1)} %get-tuple-element.49), channel_id=1, source_target_pairs={{0,16},{4,20},{8,24},{12,28},{16,0},{20,4},{24,8},{28,12},{32,48},... | collective-permute-start | bytes 393224 | tf_op jit(solution)/shard_map/ppermute | solution.py:26
  107.1 6.6 %collective-permute-start.15 = (f32[2,32,128]{2,1,0:T(8,128)}, f32[2,32,128]{2,1,0:T(8,128)S(1)}, u32[]{:S(2)}, u32[]{:S(2)}) collective-permute-start(f32[2,32,128]{2,1,0:T(8,128)} %get-tuple-element.56), channel_id=1, source_target_pairs={{0,1},{1,2},{2,3},{3,0},{4,5},{5,6},{6,7},{7,4},{8,9},{9,10},{10,1... | collective-permute-start | bytes 98312 | tf_op jit(solution)/shard_map/ppermute | solution.py:34
  107.3 7.1 %collective-permute-start.16 = (f32[2,32,128]{2,1,0:T(8,128)}, f32[2,32,128]{2,1,0:T(8,128)S(1)}, u32[]{:S(2)}, u32[]{:S(2)}) collective-permute-start(f32[2,32,128]{2,1,0:T(8,128)} %get-tuple-element.57), channel_id=1, source_target_pairs={{0,2},{1,3},{2,0},{3,1},{4,6},{5,7},{6,4},{7,5},{8,10},{9,11},{10,... | collective-permute-start | bytes 98312 | tf_op jit(solution)/shard_map/ppermute | solution.py:34
  110.9 6.1 %collective-permute-start.17 = (f32[2,32,128]{2,1,0:T(8,128)}, f32[2,32,128]{2,1,0:T(8,128)S(1)}, u32[]{:S(2)}, u32[]{:S(2)}) collective-permute-start(f32[2,32,128]{2,1,0:T(8,128)} %get-tuple-element.58), channel_id=1, source_target_pairs={{0,3},{1,0},{2,1},{3,2},{4,7},{5,4},{6,5},{7,6},{8,11},{9,8},{10,9... | collective-permute-start | bytes 98312 | tf_op jit(solution)/shard_map/ppermute | solution.py:34
  112.3 7.9 %collective-permute-start.21 = (bf16[2,8,32,128]{3,2,1,0:T(8,128)(2,1)S(1)}, bf16[2,8,32,128]{3,2,1,0:T(8,128)(2,1)S(1)}, u32[]{:S(2)}, u32[]{:S(2)}) collective-permute-start(bf16[2,8,32,128]{3,2,1,0:T(8,128)(2,1)S(1)} %get-tuple-element.64), channel_id=1, source_target_pairs={{0,24},{4,28},{8,0},{12,4},{16,8},{20,12},{24,16},{28,20},{32,56},... | collective-permute-start | bytes 393224 | tf_op jit(solution)/shard_map/ppermute | solution.py:26
  113.7 6.5 %collective-permute-start.23 = (bf16[2,8,32,128]{3,2,1,0:T(8,128)(2,1)S(1)}, bf16[2,8,32,128]{3,2,1,0:T(8,128)(2,1)S(1)}, u32[]{:S(2)}, u32[]{:S(2)}) collective-permute-start(bf16[2,8,32,128]{3,2,1,0:T(8,128)(2,1)S(1)} %get-tuple-element.65), channel_id=1, source_target_pairs={{0,8},{4,12},{8,16},{12,20},{16,24},{20,28},{24,0},{28,4},{32,40},... | collective-permute-start | bytes 393224 | tf_op jit(solution)/shard_map/ppermute | solution.py:26
  114.4 7.0 %collective-permute-start.22 = (bf16[2,8,32,128]{3,2,1,0:T(8,128)(2,1)S(1)}, bf16[2,8,32,128]{3,2,1,0:T(8,128)(2,1)S(1)}, u32[]{:S(2)}, u32[]{:S(2)}) collective-permute-start(bf16[2,8,32,128]{3,2,1,0:T(8,128)(2,1)S(1)} %get-tuple-element.66), channel_id=1, source_target_pairs={{0,16},{4,20},{8,24},{12,28},{16,0},{20,4},{24,8},{28,12},{32,48},... | collective-permute-start | bytes 393224 | tf_op jit(solution)/shard_map/ppermute | solution.py:26
  (17 other events, 114.6 us)
